TPU v7x, 32 devices: a whole 2x2x4 slice. The times are simulated.
32 devices in a mesh: seq: 8 (over z, y), wsh: 4 (over x, core).
Axes of the slice: x: 2, y: 2, z: 4, core: 2. Of those that a mesh axis runs over, the one named last changes fastest.
Arguments:
- tokens: bfloat16 [2, 4, 8192, 768], P(None, 'wsh', 'seq'), may hold values from -6 to 6
- cotangent: bfloat16 [2, 4, 8192, 768], P(None, 'wsh', 'seq'), may hold values from -6 to 6
- lengths: int32 [2, 4], P(None, 'wsh'), may hold values from 2048 to 8192, as said below
- ema_alpha: bfloat16 [768, 16], P('wsh'), may hold values from -7 to -1
- ema_delta: bfloat16 [768, 16], P('wsh'), may hold values from -7 to -2
- ema_beta: bfloat16 [768, 16], P('wsh'), may hold values from -1.5 to 1.5
- ema_eta: bfloat16 [768, 16], P('wsh'), may hold values from -1.5 to 1.5
- ema_omega: bfloat16 [768], P('wsh'), may hold values from -4 to 4
- mix_weight: bfloat16 [768, 3200], P('wsh'), may hold values from -0.4375 to 0.4375
- mix_bias: bfloat16 [3200], P('wsh'), may hold values from -1.796875 to 1.796875
- value_weight: bfloat16 [768, 1536], P('wsh'), may hold values from -0.21875 to 0.21875
- value_bias: bfloat16 [1536], P('wsh'), may hold values from -1.796875 to 1.796875
- qk_gain: bfloat16 [128, 2], P('wsh'), may hold values from 0.5 to 1.5
- qk_bias: bfloat16 [128], P('wsh'), may hold values from -1.796875 to 1.796875
- rel_bias: bfloat16 [256], P('wsh'), may hold values from -5 to 5
- out_weight: bfloat16 [1536, 768], P('wsh'), may hold values from -0.625 to 0.625
- norm_gain: bfloat16 [768, 2], P('wsh'), may hold values from 0.5 to 1.5
- norm_bias: bfloat16 [768, 2], P('wsh'), may hold values from -1.796875 to 1.796875
- ffn_in: bfloat16 [768, 1536], P('wsh'), may hold values from -0.21875 to 0.21875
- ffn_in_bias: bfloat16 [1536], P('wsh'), may hold values from -1.796875 to 1.796875
- ffn_out: bfloat16 [1536, 768], P('wsh'), may hold values from -0.15625 to 0.15625
- ffn_out_bias: bfloat16 [768], P('wsh'), may hold values from -1.796875 to 1.796875
Outputs:
- output: bfloat16 [2, 4, 8192, 768], P(None, 'wsh', 'seq')
- input_grad: bfloat16 [2, 4, 8192, 768], P(None, 'wsh', 'seq')
- alpha_grad: float32 [768, 16], P('wsh')
- delta_grad: float32 [768, 16], P('wsh')
- beta_grad: float32 [768, 16], P('wsh')
- eta_grad: float32 [768, 16], P('wsh')
- omega_grad: float32 [768], P('wsh')
- mix_weight_grad: float32 [768, 3200], P('wsh')
- mix_bias_grad: float32 [3200], P('wsh')
- value_weight_grad: float32 [768, 1536], P('wsh')
- value_bias_grad: float32 [1536], P('wsh')
- qk_gain_grad: float32 [128, 2], P('wsh')
- qk_bias_grad: float32 [128], P('wsh')
- rel_bias_grad: float32 [256], P('wsh')
- out_weight_grad: float32 [1536, 768], P('wsh')
- norm_gain_grad: float32 [768, 2], P('wsh')
- norm_bias_grad: float32 [768, 2], P('wsh')
- ffn_in_grad: float32 [768, 1536], P('wsh')
- ffn_in_bias_grad: float32 [1536], P('wsh')
- ffn_out_grad: float32 [1536, 768], P('wsh')
- ffn_out_bias_grad: float32 [768], P('wsh')
Inputs may be any that keep to these rules, and one draw needn't show every extreme that they name: `lengths`: in every micro-batch some sequence uses all 8192 positions.
All inputs are finite; a program needn't handle non-finite values.
Results may differ from a plain program's by a relative error of at most 0.015.
Values may be sent and summed in bfloat16 or wider, within the bound.
A program may use at most 1.125 GiB of HBM per device.

v0:
```python
import functools

import jax
import jax.numpy as jnp
from jax import lax
from jax.experimental import pallas as pl
from jax.experimental.pallas import tpu as pltpu
from jax.sharding import PartitionSpec as P

BLOCK = 128
LANES = 128
CH = 8
PAD = 8
CHUNK = 768
STRIP = 32
EPSILON = 1e-05
VMEM_LIMIT = 62 * 1024 * 1024
F32 = jnp.float32
BF16 = jnp.bfloat16


def dot_rows(left_op, right_op):
    return jnp.einsum("ri,rj->ij", left_op, right_op, preferred_element_type=jnp.float32)


def skew_matrix(wrapped):
    lead = wrapped.shape[:-1]
    flat = jnp.tile(wrapped, (1,) * len(lead) + (BLOCK,))[..., : BLOCK * (2 * BLOCK - 1)]
    return flat.reshape(lead + (BLOCK, 2 * BLOCK - 1))[..., :BLOCK]


def power(v, n):
    k = 1
    while k < n:
        v = v * v
        k *= 2
    return v

def rows_of(scr, s, T):
    return scr[pl.ds(s, CH, stride=T+PAD), :]

def spread(scr, v, T):
    for k in range(CH):
        scr[k*(T+PAD):k*(T+PAD)+T, :] = v[k*T:(k+1)*T, :]

def collect(scr, T):
    return jnp.concatenate([scr[k*(T+PAD):k*(T+PAD)+T, :] for k in range(CH)], axis=0)

def ends_kernel(H, T, x_ref, q_ref, e_ref, s_ref, scr):
    spread(scr, x_ref[0].astype(F32), T)
    q = [jnp.broadcast_to(q_ref[h:h+1, :], (CH, LANES)) for h in range(H)]
    def step(s, st):
        xs = rows_of(scr, s, T)
        return tuple(q[h]*st[h] + xs for h in range(H))
    st = lax.fori_loop(0, T, step, tuple(jnp.zeros((CH,LANES),F32) for _ in range(H)), unroll=8)
    for h in range(H):
        e_ref[0, h*CH:(h+1)*CH, :] = st[h]
    qT = power(q_ref[...], T)
    c = jnp.zeros((H,LANES),F32)
    for k in range(CH):
        c = qT*c + e_ref[0, pl.ds(k,H,stride=CH), :]
    s_ref[0] = c

def fwd_kernel(H, T, x_ref, q_ref, w_ref, om_ref, e_ref, c_ref, *refs):
    xp_ref, p_ref, f_ref, scr, cs, ps = refs[-6:]
    spread(scr, x_ref[0].astype(F32), T)
    qT = power(q_ref[...], T)
    c = c_ref[0]
    for k in range(CH):
        cs[pl.ds(k,H,stride=CH), :] = c
        c = qT*c + e_ref[0, pl.ds(k,H,stride=CH), :]
    q = [jnp.broadcast_to(q_ref[h:h+1, :], (CH, LANES)) for h in range(H)]
    w = [jnp.broadcast_to(w_ref[h:h+1, :], (CH, LANES)) for h in range(H)]
    om = jnp.broadcast_to(om_ref[...], (CH,LANES))
    def step(s, st):
        xs = rows_of(scr, s, T)
        st = tuple(q[h]*st[h] + xs for h in range(H))
        terms = [w[h]*st[h] for h in range(H)]
        while len(terms) > 1:
            terms = [terms[i]+terms[i+1] for i in range(0,len(terms)-1,2)] + ([terms[-1]] if len(terms)%2 else [])
        ps[pl.ds(s, CH, stride=T+PAD), :] = terms[0] + om*xs
        return st
    st = lax.fori_loop(0, T, step, tuple(cs[h*CH:(h+1)*CH, :] for h in range(H)), unroll=8)
    for h in range(H):
        f_ref[0, h*CH:(h+1)*CH, :] = st[h]
    p = collect(ps, T)
    p_ref[0] = p
    xp_ref[0] = (p*jax.nn.sigmoid(p)).astype(xp_ref.dtype)

def bends_kernel(H, T, dxp_ref, p_ref, q_ref, d_ref, e_ref, s_ref, ds):
    p = p_ref[0]
    sg = jax.nn.sigmoid(p)
    d = dxp_ref[0].astype(F32) * (sg*(1.0+p*(1.0-sg)))
    d_ref[0] = d
    spread(ds, d, T)
    q = [jnp.broadcast_to(q_ref[h:h+1, :], (CH, LANES)) for h in range(H)]
    def step(s, st):
        xs = rows_of(ds, T-1-s, T)
        return tuple(q[h]*st[h] + xs for h in range(H))
    st = lax.fori_loop(0, T, step, tuple(jnp.zeros((CH,LANES),F32) for _ in range(H)), unroll=8)
    for h in range(H):
        e_ref[0, h*CH:(h+1)*CH, :] = st[h]
    qT = power(q_ref[...], T)
    c = jnp.zeros((H,LANES),F32)
    for k in reversed(range(CH)):
        c = qT*c + e_ref[0, pl.ds(k,H,stride=CH), :]
    s_ref[0] = c

def bwd_kernel(H, T, d_ref, x_ref, q_ref, qi_ref, w_ref, om_ref, f_ref, e_ref, c_ref, t_ref, k_ref, *refs):
    dx_ref, out_ref, s1_ref, s3_ref, go_ref, scr, cs, dx, ds = refs[-9:]
    g = pl.program_id(1)
    x = x_ref[0].astype(F32)
    spread(scr, x, T)
    dv = d_ref[0]
    spread(ds, dv, T)
    qT = power(q_ref[...], T)
    c = c_ref[0]
    for k in reversed(range(CH)):
        cs[pl.ds(k,H,stride=CH), :] = c
        c = qT*c + e_ref[0, pl.ds(k,H,stride=CH), :]
    om = jnp.broadcast_to(om_ref[...], (CH,LANES))
    HH = H//2
    zero = jnp.zeros((CH,LANES),F32)
    @pl.when(g==0)
    def _():
        go_ref[...] = jnp.zeros_like(go_ref)
        s1_ref[...] = jnp.zeros_like(s1_ref)
        s3_ref[...] = jnp.zeros_like(s3_ref)
    go_ref[...] += jnp.sum(dv*x, axis=0, keepdims=True)
    for half in range(2):
        hs = range(half*HH, half*HH+HH)
        q = [jnp.broadcast_to(q_ref[h:h+1, :], (CH, LANES)) for h in hs]
        qi = [jnp.broadcast_to(qi_ref[h:h+1, :], (CH, LANES)) for h in hs]
        w = [jnp.broadcast_to(w_ref[h:h+1, :], (CH, LANES)) for h in hs]
        def step(s, carry):
            l, st, a1, a3 = carry
            at = pl.ds(T-1-s, CH, stride=T+PAD)
            d = ds[at, :]
            xs = scr[at, :]
            a1 = tuple(a1[i] + d*st[i] for i in range(HH))
            l = tuple(q[i]*l[i] + d for i in range(HH))
            st = tuple((st[i]-xs)*qi[i] for i in range(HH))
            a3 = tuple(a3[i] + l[i]*st[i] for i in range(HH))
            terms = [w[i]*l[i] for i in range(HH)]
            while len(terms) > 1:
                terms = [terms[i]+terms[i+1] for i in range(0,len(terms)-1,2)]
            if half == 0:
                dx[at, :] = terms[0] + om*d
            else:
                dx[at, :] = dx[at, :] + terms[0]
            return l, st, a1, a3
        init = (tuple(cs[h*CH:(h+1)*CH,:] for h in hs), tuple(f_ref[0,h*CH:(h+1)*CH,:] for h in hs), (zero,)*HH, (zero,)*HH)
        l, st, a1, a3 = lax.fori_loop(0, T, step, init, unroll=4)
        for i,h in enumerate(hs):
            s1_ref[h:h+1,:] += jnp.sum(a1[i],axis=0,keepdims=True)
            s3_ref[h:h+1,:] += jnp.sum(a3[i],axis=0,keepdims=True)
    dx_ref[0] = (t_ref[0] + collect(dx, T).astype(dx_ref.dtype).astype(F32)).astype(dx_ref.dtype)

    @pl.when(g == pl.num_programs(1) - 1)
    def _():
        s1, s3 = s1_ref[...], s3_ref[...]
        out_ref[0:H, :] = k_ref[0:H, :] * s1 + k_ref[H : 2 * H, :] * s3
        out_ref[H : 2 * H, :] = k_ref[2 * H : 3 * H, :] * s3
        out_ref[2 * H : 3 * H, :] = k_ref[3 * H : 4 * H, :] * s1
        out_ref[3 * H : 4 * H, :] = k_ref[4 * H : 5 * H, :] * s1
        out_ref[4 * H : 4 * H + 8, :] = jnp.broadcast_to(go_ref[...], (8, LANES))


def specs(L, H, first=0):
    blk = pl.BlockSpec((1, L, LANES), lambda c, g: (g, 0, c + first))
    par = pl.BlockSpec((H, LANES), lambda c, g: (0, c + first))
    one = pl.BlockSpec((1, LANES), lambda c, g: (0, c + first))
    st = pl.BlockSpec((1, H * CH, LANES), lambda c, g: (g, 0, c + first))
    car = pl.BlockSpec((1, H, LANES), lambda c, g: (g, 0, c + first))
    return blk, par, one, st, car


def ema_ends(x, q):
    G, L, C = x.shape
    H = q.shape[0]
    blk, par, one, st, car = specs(L, H)
    return pl.pallas_call(
        functools.partial(ends_kernel, H, L // CH),
        grid=(C // LANES, G),
        in_specs=[blk, par],
        out_specs=[st, car],
        out_shape=[jax.ShapeDtypeStruct((G, H * CH, C), F32), jax.ShapeDtypeStruct((G, H, C), F32)],
        scratch_shapes=[pltpu.VMEM((L + CH * PAD, LANES), F32)],
        cost_estimate=cost_of(0, 11),
        name="ema_ends",
    )(x, q)


def ema_forward(span, so_far, x, q, w, om, e, c):
    G, L, C = x.shape
    H = q.shape[0]
    first, count = span
    blk, par, one, st, car = specs(L, H, first)
    return pl.pallas_call(
        functools.partial(fwd_kernel, H, L // CH),
        grid=(count, G),
        in_specs=[blk, par, par, one, st, car] + [pl.BlockSpec(memory_space=pl.ANY)] * len(so_far),
        out_specs=[blk, blk, st],
        out_shape=[
            jax.ShapeDtypeStruct((G, L, C), BF16), jax.ShapeDtypeStruct((G, L, C), F32),
            jax.ShapeDtypeStruct((G, H * CH, C), F32),
        ],
        scratch_shapes=[
            pltpu.VMEM((L + CH * PAD, LANES), F32), pltpu.VMEM((H * CH, LANES), F32),
            pltpu.VMEM((L + CH * PAD, LANES), F32),
        ],
        input_output_aliases={6 + k: k for k in range(len(so_far))},
        cost_estimate=cost_of(0, 3 * count),
        name="ema_forward",
    )(x, q, w, om, e, c, *so_far)


def ema_back_ends(dxp, p, q):
    G, L, C = p.shape
    H = q.shape[0]
    blk, par, one, st, car = specs(L, H)
    return pl.pallas_call(
        functools.partial(bends_kernel, H, L // CH),
        grid=(C // LANES, G),
        in_specs=[blk, blk, par],
        out_specs=[blk, st, car],
        out_shape=[
            jax.ShapeDtypeStruct((G, L, C), F32), jax.ShapeDtypeStruct((G, H * CH, C), F32),
            jax.ShapeDtypeStruct((G, H, C), F32),
        ],
        scratch_shapes=[pltpu.VMEM((L + CH * PAD, LANES), F32)],
        cost_estimate=cost_of(0, 15),
        name="ema_back_ends",
    )(dxp, p, q)


def ema_backward(span, so_far, d, x, q, qi, w, om, f, e, c, t, k):
    G, L, C = x.shape
    H = q.shape[0]
    first, count = span
    blk, par, one, st, car = specs(L, H, first)
    factors = pl.BlockSpec((5 * H, LANES), lambda c, g: (0, c + first))
    sums = pl.BlockSpec((4 * H + 8, LANES), lambda c, g: (0, c + first))
    return pl.pallas_call(
        functools.partial(bwd_kernel, H, L // CH),
        grid=(count, G),
        in_specs=[blk, blk, par, par, par, one, st, st, car, blk, factors]
        + [pl.BlockSpec(memory_space=pl.ANY)] * len(so_far),
        out_specs=[blk, sums],
        out_shape=[
            jax.ShapeDtypeStruct((G, L, C), BF16), jax.ShapeDtypeStruct((4 * H + 8, C), F32),
        ],
        scratch_shapes=[
            pltpu.VMEM((H, LANES), F32), pltpu.VMEM((H, LANES), F32), pltpu.VMEM((1, LANES), F32),
            pltpu.VMEM((L + CH * PAD, LANES), F32), pltpu.VMEM((H * CH, LANES), F32),
            pltpu.VMEM((L + CH * PAD, LANES), F32), pltpu.VMEM((L + CH * PAD, LANES), F32),
        ],
        input_output_aliases={11 + n: n for n in range(len(so_far))},
        cost_estimate=cost_of(0, 8 * count),
        name="ema_backward",
    )(d, x, q, qi, w, om, f, e, c, t, k, *so_far)


def sig(v):
    return 0.5 * jnp.tanh(0.5 * v) + 0.5


def dot_nn(left_op, right_op):
    return jnp.dot(left_op, right_op, preferred_element_type=F32)


def dot_nt(left_op, right_op):
    return lax.dot_general(left_op, right_op, (((1,), (1,)), ((), ())), preferred_element_type=F32)


def dot_tn(left_op, right_op):
    return lax.dot_general(left_op, right_op, (((0,), (0,)), ((), ())), preferred_element_type=F32)


def piece_copies(pieces, target):
    j = lax.axis_index("wsh")
    bit = lax.rem(lax.axis_index("seq"), 2)
    rows = target.shape[0] // 4
    half = rows // 2
    if len(pieces) == 4:
        starts = [(j ^ k) * rows for k in range(4)]
    else:
        low, high = bit * half, (1 - bit) * half
        starts = [j * rows, (j ^ 1) * rows]
        starts += [(j ^ 2) * rows + low, (j ^ 2) * rows + high, (j ^ 3) * rows + low, (j ^ 3) * rows + high]
    return [
        (piece, target.at[pl.ds(pl.multiple_of(start, 32), piece.shape[0]), :])
        for piece, start in zip(pieces, starts)
    ]


def bring(groups, sem):
    @pl.when(pl.program_id(0) == 0)
    def _():
        copies = []
        for pieces, target in groups:
            for source, spot in piece_copies(pieces, target):
                copies.append(pltpu.make_async_copy(source, spot, sem.at[len(copies)]))
        for copy in copies:
            copy.start()
        for copy in copies:
            copy.wait()


def fold(rows):
    total = rows[:8]
    for k in range(8, STRIP, 8):
        total = total + rows[k : k + 8]
    return total


def add_sums(ref, at, rows):
    ref[:, at] += jnp.sum(rows, axis=0, keepdims=True)


def mix_fwd_kernel(R, dims, x_ref, xp_ref, bm_ref, bv_ref, qk_ref, rel_ref, *refs):
    D, Z, V = dims
    pieces, refs = refs[:18], refs[18:]
    u_ref, h_ref, r_ref, v_ref, z_ref, p_ref, m_ref, wm, wv, wo, sem = refs
    bring(((pieces[:6], wm), (pieces[6:12], wv), (pieces[12:], wo)), sem)
    xp = xp_ref[...]
    x = x_ref[...]
    z = dot_nn(xp, wm[:, D : D + Z]) + bm_ref[:, D : D + Z]
    z_ref[...] = z
    shared = z * sig(z)
    query = (shared * qk_ref[0:1, :] + qk_ref[2:3, :]).astype(BF16)
    key = (shared * qk_ref[1:2, :]).astype(BF16)
    probs = []
    row = lax.broadcasted_iota(jnp.int32, (BLOCK, BLOCK), 0)
    col = lax.broadcasted_iota(jnp.int32, (BLOCK, BLOCK), 1)
    for b in range(R // BLOCK):
        at = slice(b * BLOCK, (b + 1) * BLOCK)
        score = dot_nt(query[at], key[at]) * Z ** (-0.5) + rel_ref[...]
        score = jnp.where(row >= col, score, -1e30)
        grown = jnp.exp(score - jnp.max(score, axis=-1, keepdims=True))
        prob = grown / jnp.sum(grown, axis=-1, keepdims=True)
        p_ref[at, :] = prob
        probs.append(prob.astype(BF16))
    for c in range(0, V, CHUNK):
        at = slice(c, c + CHUNK)
        rat = slice(D + Z + c, D + Z + c + CHUNK)
        v = dot_nn(x, wv[:, at]) + bv_ref[:, at]
        v_ref[:, at] = v
        value = (v * sig(v)).astype(BF16)
        r = dot_nn(xp, wm[:, rat]) + bm_ref[:, rat]
        r_ref[:, at] = r
        reset = r * sig(r)
        for b in range(0, R // BLOCK, 2):
            rows = slice(b * BLOCK, (b + 2) * BLOCK)
            m_ref[rows, at] = (reset[rows] * dot_nn(pair_of(probs[b], probs[b + 1]), value[rows])).astype(BF16)
    u_ref[...] = dot_nn(xp, wm[:, :D]) + bm_ref[:, :D]
    h_ref[...] = dot_nn(xp, wm[:, D + Z + V :]) + bm_ref[:, D + Z + V :] + dot_nn(m_ref[...], wo[...])


def slope_of(pre, logistic):
    return logistic * (1.0 + pre * (1.0 - logistic))


def mean_of(rows):
    return jnp.mean(rows, axis=-1, keepdims=True)


def ffn_kernel(R, dims, x_ref, u_ref, h_ref, cot_ref, live_ref, gn_ref, bf_ref, bo_ref, *refs):
    D, FF = dims
    pieces, refs = refs[:8], refs[8:]
    (
        o_ref, h1_ref, act_ref, dg_ref, df_ref, dum_ref, dt_ref, sd_ref, sf_ref,
        wi, wo, f_scr, n1_scr, a_scr, i1_scr, sem,
    ) = refs
    bring(((pieces[:4], wi), (pieces[4:], wo)), sem)

    @pl.when(pl.program_id(0) == 0)
    def _():
        sd_ref[...] = jnp.zeros_like(sd_ref)
        sf_ref[...] = jnp.zeros_like(sf_ref)

    g1, g2, b1, b2 = (gn_ref[k : k + 1, :] for k in range(4))
    part = min(256, R)

    def strips(s):
        return [slice(k, k + STRIP) for k in range(s * part, (s + 1) * part, STRIP)]

    def first(s):
        for at in strips(s):
            x = x_ref[at, :].astype(F32)
            h = h_ref[at, :]
            y = x + sig(u_ref[at, :]) * (h * sig(h) - x)
            center = y - mean_of(y)
            inverse = lax.rsqrt(mean_of(center * center) + EPSILON)
            n1 = center * inverse
            n1_scr[at, :] = n1
            i1_scr[at, :] = jnp.broadcast_to(inverse, (STRIP, LANES))
            h1_ref[at, :] = (n1 * g1 + b1).astype(BF16)

    def spread(s):
        rows = slice(s * part, (s + 1) * part)
        for c in range(0, FF, CHUNK):
            at = slice(c, c + CHUNK)
            f = dot_nn(h1_ref[rows, :], wi[:, at]) + bf_ref[:, at]
            f_scr[rows, at] = f
            act_ref[rows, at] = (f * sig(f)).astype(BF16)

    def narrow(s):
        rows = slice(s * part, (s + 1) * part)
        a_scr[rows, :] = dot_nn(act_ref[rows, :], wo[...])

    def second(s):
        zero = jnp.zeros((8, D), F32)
        s_gain, s_shift, s_bias = zero, zero, zero
        for at in strips(s):
            y2 = n1_scr[at, :] * g1 + b1 + a_scr[at, :] + bo_ref[...]
            center = y2 - mean_of(y2)
            inverse = lax.rsqrt(mean_of(center * center) + EPSILON)
            n2 = center * inverse
            live = live_ref[at, :]
            o_ref[at, :] = ((n2 * g2 + b2) * live).astype(BF16)
            dn = cot_ref[at, :].astype(F32) * live
            w = dn * g2
            dy2 = inverse * (w - mean_of(w) - n2 * mean_of(w * n2))
            a_scr[at, :] = dy2
            dg_ref[at, :] = dy2.astype(BF16)
            s_gain, s_shift, s_bias = s_gain + fold(dn * n2), s_shift + fold(dn), s_bias + fold(dy2)
        sd_ref[1:2, :] += jnp.sum(s_gain, axis=0, keepdims=True)
        sd_ref[3:4, :] += jnp.sum(s_shift, axis=0, keepdims=True)
        sd_ref[4:5, :] += jnp.sum(s_bias, axis=0, keepdims=True)

    def spread_back(s):
        rows = slice(s * part, (s + 1) * part)
        for c in range(0, FF, CHUNK):
            at = slice(c, c + CHUNK)
            f = f_scr[rows, at]
            df = (dot_nt(dg_ref[rows, :], wo[at, :]) * slope_of(f, sig(f))).astype(BF16)
            df_ref[rows, at] = df
            add_sums(sf_ref, at, df.astype(F32))

    def narrow_back(s):
        rows = slice(s * part, (s + 1) * part)
        a_scr[rows, :] += dot_nt(df_ref[rows, :], wi[...])

    def third(s):
        zero = jnp.zeros((8, D), F32)
        s_gain, s_shift = zero, zero
        for at in strips(s):
            dh1 = a_scr[at, :]
            n1 = n1_scr[at, :]
            w = dh1 * g1
            dy = i1_scr[at, 0:1] * (w - mean_of(w) - n1 * mean_of(w * n1))
            x = x_ref[at, :].astype(F32)
            h = h_ref[at, :]
            sh = sig(h)
            gate = sig(u_ref[at, :])
            rest = 1.0 - gate
            dyg = dy * gate
            dum_ref[at, :D] = (dyg * (h * sh - x) * rest).astype(BF16)
            dum_ref[at, D:] = (dyg * slope_of(h, sh)).astype(BF16)
            dt_ref[at, :] = dy * rest
            s_gain, s_shift = s_gain + fold(dh1 * n1), s_shift + fold(dh1)
        sd_ref[0:1, :] += jnp.sum(s_gain, axis=0, keepdims=True)
        sd_ref[2:3, :] += jnp.sum(s_shift, axis=0, keepdims=True)

    stages = (first, spread, narrow, second, spread_back, narrow_back, third)
    count = R // part
    for tick in range(len(stages) + count - 1):
        for s in range(count):
            if 0 <= tick - s < len(stages):
                stages[tick - s](s)


def pair_of(top, bottom):
    none = jnp.zeros_like(top)
    return jnp.concatenate([jnp.concatenate([top, none], axis=1), jnp.concatenate([none, bottom], axis=1)], axis=0)


def sum_spots(D, Z, V, FF):
    spans = [("mix", D, Z), ("rel", 0, 2 * BLOCK), ("qk", 0, 3 * Z), ("mix", 0, D), ("mix", D + Z + V, D)]
    spans += [("mix", D + Z + k, D) for k in range(0, V, D)] + [("value", k, D) for k in range(0, V, D)]
    spans += [("ffn", k, D) for k in range(0, FF, D)] + [("rows", k * D, D) for k in range(5)]
    spots, place = [], 0
    for name, start, size in spans:
        spots.append((name, start, place // D, place % D, size))
        place += size
    return spots


def mix_bwd_kernel(R, dims, dum_ref, dt_ref, r_ref, v_ref, z_ref, p_ref, qk_ref, sd_ref, sf_ref, *refs):
    D, Z, V = dims
    pieces, refs = refs[:18], refs[18:]
    db_ref, dv_ref, dxp_ref, do_ref, all_ref, sm_ref, sv_ref, sq_ref, ss_ref, wm, wv, wo, acc, sem = refs
    bring(((pieces[:6], wm), (pieces[6:12], wv), (pieces[12:], wo)), sem)

    @pl.when(pl.program_id(0) == 0)
    def _():
        for ref in (sm_ref, sv_ref, sq_ref, ss_ref):
            ref[...] = jnp.zeros_like(ref)

    last = D + Z + V
    blocks = [slice(b * BLOCK, (b + 1) * BLOCK) for b in range(R // BLOCK)]
    full = [p_ref[rows, :] for rows in blocks]
    probs = [prob.astype(BF16) for prob in full]
    pairs = [slice(k, k + 2 * BLOCK) for k in range(0, R, 2 * BLOCK)]
    double = [pair_of(probs[2 * k], probs[2 * k + 1]) for k in range(len(pairs))]
    wide = [jnp.zeros((2 * BLOCK, 2 * BLOCK), F32) for _ in pairs]
    size = 512

    def head(c):
        return dot_nt(dum_ref[:, D:], wo[c : c + size, :])

    def chunk(c, dmix):
        at = slice(c, c + size)
        rat = slice(D + Z + c, D + Z + c + size)
        zat = slice(Z + c, Z + c + size)
        sum_r = jnp.zeros((1, size), F32)
        sum_v = jnp.zeros((1, size), F32)
        for b, rows in enumerate(pairs):
            r = r_ref[rows, at]
            v = v_ref[rows, at]
            sr = sig(r)
            sv = sig(v)
            value = (v * sv).astype(BF16)
            datt = (dmix[rows] * (r * sr)).astype(BF16)
            dr = (dmix[rows] * slope_of(r, sr) * dot_nn(double[b], value)).astype(BF16)
            db_ref[rows, zat] = dr
            sum_r += jnp.sum(dr.astype(F32), axis=0, keepdims=True)
            wide[b] += dot_nt(datt, value)
            dv = (dot_tn(double[b], datt) * slope_of(v, sv)).astype(BF16)
            dv_ref[rows, at] = dv
            sum_v += jnp.sum(dv.astype(F32), axis=0, keepdims=True)
        sm_ref[:, rat] += sum_r
        sv_ref[:, at] += sum_v

    def give(c):
        at = slice(c, c + size)
        rat = slice(D + Z + c, D + Z + c + size)
        zat = slice(Z + c, Z + c + size)
        acc[...] += dot_nt(db_ref[:, zat], wm[:, rat])
        do_ref[...] += dot_nt(dv_ref[:, at], wv[:, at])

    starts = list(range(0, V, size))
    dmix = head(starts[0])
    acc[...] = dot_nt(dum_ref[:, :D], wm[:, :D]) + dot_nt(dum_ref[:, D:], wm[:, last:])
    do_ref[...] = dt_ref[...]
    chunk(starts[0], dmix)
    for n, c in enumerate(starts[1:]):
        dmix = head(c)
        give(starts[n])
        chunk(c, dmix)
    add_sums(sm_ref, slice(0, D), dum_ref[:, :D].astype(F32))
    add_sums(sm_ref, slice(last, D + last), dum_ref[:, D:].astype(F32))
    for b, rows in enumerate(blocks):
        z = z_ref[rows, :]
        sz = sig(z)
        shared = z * sz
        query = (shared * qk_ref[0:1, :] + qk_ref[2:3, :]).astype(BF16)
        key = (shared * qk_ref[1:2, :]).astype(BF16)
        side = slice(b % 2 * BLOCK, b % 2 * BLOCK + BLOCK)
        dprob = wide[b // 2][side, side]
        inner = jnp.sum(full[b] * dprob, axis=-1, keepdims=True)
        ds = (full[b] * (dprob - inner)).astype(BF16)
        ss_ref[...] += ds.astype(F32)
        dq = dot_nn(ds, key) * Z ** (-0.5)
        dk = dot_tn(ds, query) * Z ** (-0.5)
        sq_ref[0:1, :] += jnp.sum(dq * shared, axis=0, keepdims=True)
        sq_ref[1:2, :] += jnp.sum(dk * shared, axis=0, keepdims=True)
        sq_ref[2:3, :] += jnp.sum(dq, axis=0, keepdims=True)
        dz = (dq * qk_ref[0:1, :] + dk * qk_ref[1:2, :]) * slope_of(z, sz)
        dz = dz.astype(BF16)
        db_ref[rows, :Z] = dz
        add_sums(sm_ref, slice(D, D + Z), dz.astype(F32))
    give(starts[-1])
    dxp_ref[...] = (acc[...] + dot_nt(db_ref[:, :Z], wm[:, D : D + Z])).astype(BF16)

    @pl.when(pl.program_id(0) == pl.num_programs(0) - 1)
    def _():
        moved = jnp.concatenate([ss_ref[...].T, jnp.zeros((BLOCK, BLOCK), F32)], axis=1)
        row = lax.broadcasted_iota(jnp.int32, moved.shape, 0)
        step = 1
        while step < BLOCK:
            moved = jnp.where(jnp.bitwise_and(row, step) == 0, pltpu.roll(moved, step, 1), moved)
            step *= 2
        spots = sum_spots(D, Z, V, sf_ref.shape[1])
        sums = {
            "mix": sm_ref[...], "value": sv_ref[...], "ffn": sf_ref[...], "rel": jnp.sum(moved, axis=0, keepdims=True),
            "qk": jnp.concatenate([sq_ref[k : k + 1, :] for k in range(3)], axis=1),
            "rows": jnp.concatenate([sd_ref[k : k + 1, :] for k in range(5)], axis=1),
        }
        all_ref[...] = jnp.zeros_like(all_ref)
        for name, start, row, col, size in spots:
            all_ref[row : row + 1, col : col + size] = sums[name][:, start : start + size]


def cost_of(flops, microseconds):
    return pl.CostEstimate(flops=flops, bytes_accessed=microseconds * 3_600_000, transcendentals=0)


def any_specs(n):
    return [pl.BlockSpec(memory_space=pl.ANY)] * n


def tile(R, n):
    return pl.BlockSpec((R, n), lambda t: (t, 0))


def fixed(r, n):
    return pl.BlockSpec((r, n), lambda t: (0, 0))


def shape(r, n, dtype=F32):
    return jax.ShapeDtypeStruct((r, n), dtype)


def mix_forward(R, x, xp, bm, bv, qk, rel, pieces):
    T, D = x.shape
    V = bv.shape[1]
    Z = qk.shape[1]
    E = bm.shape[1]
    return pl.pallas_call(
        functools.partial(mix_fwd_kernel, R, (D, Z, V)),
        grid=(T // R,),
        in_specs=[tile(R, D), tile(R, D), fixed(1, E), fixed(1, V), fixed(8, Z), fixed(BLOCK, BLOCK)]
        + any_specs(18),
        out_specs=[tile(R, D), tile(R, D), tile(R, V), tile(R, V), tile(R, Z), tile(R, BLOCK), tile(R, V)],
        out_shape=[
            shape(T, D), shape(T, D), shape(T, V), shape(T, V), shape(T, Z), shape(T, BLOCK), shape(T, V, BF16),
        ],
        scratch_shapes=[
            pltpu.VMEM((D, E), BF16), pltpu.VMEM((D, V), BF16), pltpu.VMEM((V, D), BF16),
            pltpu.SemaphoreType.DMA((18,)),
        ],
        compiler_params=pltpu.CompilerParams(vmem_limit_bytes=VMEM_LIMIT),
        cost_estimate=cost_of(2 * T * D * (E + 2 * V), 33),
        name="mix_forward",
    )(x, xp, bm, bv, qk, rel, *pieces)


def ffn_both(R, x, u, h, cot, live, norms, bf, bo, pieces):
    T, D = x.shape
    FF = bf.shape[1]
    return pl.pallas_call(
        functools.partial(ffn_kernel, R, (D, FF)),
        grid=(T // R,),
        in_specs=[tile(R, D), tile(R, D), tile(R, D), tile(R, D), tile(R, 1), fixed(8, D), fixed(1, FF), fixed(1, D)]
        + any_specs(8),
        out_specs=[
            tile(R, D), tile(R, D), tile(R, FF), tile(R, D), tile(R, FF), tile(R, 2 * D), tile(R, D),
            fixed(8, D), fixed(1, FF),
        ],
        out_shape=[
            shape(T, D, BF16), shape(T, D, BF16), shape(T, FF, BF16), shape(T, D, BF16), shape(T, FF, BF16),
            shape(T, 2 * D, BF16), shape(T, D), shape(8, D), shape(1, FF),
        ],
        scratch_shapes=[
            pltpu.VMEM((D, FF), BF16), pltpu.VMEM((FF, D), BF16), pltpu.VMEM((R, FF), F32), pltpu.VMEM((R, D), F32),
            pltpu.VMEM((R, D), F32), pltpu.VMEM((R, 128), F32), pltpu.SemaphoreType.DMA((12,)),
        ],
        compiler_params=pltpu.CompilerParams(vmem_limit_bytes=VMEM_LIMIT),
        cost_estimate=cost_of(2 * T * D * 4 * FF, 50),
        name="ffn_both",
    )(x, u, h, cot, live, norms, bf, bo, *pieces)


def mix_backward(R, dum, dt, r, v, z, p, qk, sum_d, sum_f, pieces):
    T, D = dt.shape
    V = r.shape[1]
    Z = qk.shape[1]
    E = 2 * D + Z + V
    return pl.pallas_call(
        functools.partial(mix_bwd_kernel, R, (D, Z, V)),
        grid=(T // R,),
        in_specs=[
            tile(R, 2 * D), tile(R, D), tile(R, V), tile(R, V), tile(R, Z), tile(R, BLOCK), fixed(8, Z),
            fixed(8, D), fixed(1, sum_f.shape[1]),
        ]
        + any_specs(18),
        out_specs=[
            tile(R, Z + V), tile(R, V), tile(R, D), tile(R, D), fixed(16, D),
        ],
        out_shape=[
            shape(T, Z + V, BF16), shape(T, V, BF16), shape(T, D, BF16), shape(T, D), shape(16, D),
        ],
        scratch_shapes=[
            pltpu.VMEM((1, E), F32), pltpu.VMEM((1, V), F32), pltpu.VMEM((8, Z), F32), pltpu.VMEM((BLOCK, BLOCK), F32),
            pltpu.VMEM((D, E), BF16), pltpu.VMEM((D, V), BF16), pltpu.VMEM((V, D), BF16), pltpu.VMEM((R, D), F32),
            pltpu.SemaphoreType.DMA((18,)),
        ],
        compiler_params=pltpu.CompilerParams(vmem_limit_bytes=VMEM_LIMIT),
        cost_estimate=cost_of(2 * T * D * (E + 2 * V), 40),
        name="mix_backward",
    )(dum, dt, r, v, z, p, qk, sum_d, sum_f, *pieces)


def exchange(value, axis, step):
    return lax.ppermute(value, axis, [(k, k ^ step) for k in range(lax.axis_size(axis))])


def join(*values):
    return lax.optimization_barrier(values)


def own_half(own):
    half = own.shape[0] // 2
    return lax.dynamic_slice_in_dim(own, lax.rem(lax.axis_index("seq"), 2) * half, half, 0)


def over_x(value):
    return exchange(value, "wsh", 2)


def over_y(value):
    return exchange(value, "seq", 1)


def over_core(value):
    return exchange(value, "wsh", 1)


def gather_small(own):
    j = lax.axis_index("wsh")
    four = jnp.stack([own] + [exchange(own, "wsh", d) for d in range(1, 4)])
    return jnp.stack([lax.dynamic_index_in_dim(four, j ^ k, 0, False) for k in range(4)])


class Carry:
    def __init__(self, states, decay, reverse):
        self.entry, self.total = jnp.zeros_like(states), states
        self.own, self.window, self.reverse = jnp.ones_like(decay), decay, reverse

    def send(self, step):
        return exchange(self.total, "seq", step)

    def add(self, step, sent):
        bit = lax.rem(lax.axis_index("seq") // step, 2)
        later = (bit == 0) if self.reverse else (bit == 1)
        self.entry = jnp.where(later, self.entry + self.own * sent, self.entry)
        self.total = jnp.where(later, self.total + self.window * sent, sent + self.window * self.total)
        self.own = jnp.where(later, self.own * self.window, self.own)
        self.window = self.window * self.window


def pick(value, dim, bit):
    return lax.dynamic_index_in_dim(value, bit, dim, False)


def send_half(value, dim, mark):
    axis, step = mark
    bit = lax.rem(lax.axis_index(axis) // step, 2)
    return exchange(pick(value, dim, 1 - bit).astype(BF16), axis, step), pick(value, dim, bit)


def add_half(sent, kept):
    return kept + sent.astype(F32)


def seq_steps():
    return [2**k for k in range(lax.axis_size("seq").bit_length() - 1)]


def send_core(grad):
    rows, cols = grad.shape
    bits = (2,) * len(seq_steps())
    rest = rows // lax.axis_size("wsh") // lax.axis_size("seq")
    return send_half(grad.reshape((2, 2) + bits + (rest, cols)), 1, ("wsh", 1))


def merge(parts, cols):
    pieces = []
    for part in parts:
        for c in range(0, part.shape[-1], cols):
            pieces.append(part[..., c : c + cols])
    return jnp.concatenate(pieces, axis=-2)


class Sum:
    def __init__(self, value):
        self.value = value
        self.marks = [("wsh", 2)] + [("seq", s) for s in reversed(seq_steps())]

    def send(self, mark):
        dim = self.marks.index(mark)
        self.marks.pop(dim)
        sent, self.kept = send_half(self.value, dim, mark)
        return sent

    def add(self, sent):
        self.value = add_half(sent, self.kept)


def widen(block, other, step):
    bit = lax.rem(lax.axis_index("seq") // step, 2)
    first = jnp.where(bit == 0, block, other)
    second = jnp.where(bit == 0, other, block)
    return jnp.concatenate([first, second], axis=0)


def in_order(block):
    bits = block.shape[0].bit_length() - 1
    split = block.reshape((2,) * bits + block.shape[1:])
    turned = split.transpose(tuple(reversed(range(bits))) + (bits, bits + 1))
    return turned.reshape(block.shape)


def sum_over_wsh(value):
    j = lax.axis_index("wsh")
    total = lax.dynamic_index_in_dim(value, j, 0, False)
    for d in range(1, 4):
        total = total + exchange(lax.dynamic_index_in_dim(value, j ^ d, 0, False), "wsh", d)
    return total


def sum_over_seq(total):
    for step in reversed(seq_steps()):
        total = total + exchange(total, "seq", step)
    return total


def body(
    tokens, cotangent, lengths, ema_alpha, ema_delta, ema_beta, ema_eta, ema_omega, mix_weight, mix_bias,
    value_weight, value_bias, qk_gain, qk_bias, rel_bias, out_weight, norm_gain, norm_bias, ffn_in, ffn_in_bias,
    ffn_out, ffn_out_bias,
):
    micro, seqs, L, D = tokens.shape
    G = micro * seqs
    T = G * L
    H = ema_alpha.shape[1]
    R = min(512, T)
    n_wsh = lax.axis_size("wsh")
    i = lax.axis_index("seq")
    Z = qk_gain.shape[0] * n_wsh
    V = value_weight.shape[1]
    FF = ffn_in.shape[1]

    flat_parts = (mix_bias, value_bias, ffn_in_bias, rel_bias, qk_gain[:, 0], qk_gain[:, 1], qk_bias)
    flat = jnp.concatenate(flat_parts).reshape(ema_alpha.shape[0], -1)
    chan = jnp.concatenate(
        [ema_alpha, ema_delta, ema_beta, ema_eta, ema_omega[:, None], norm_gain, norm_bias, ffn_out_bias[:, None], flat],
        axis=1,
    )
    chan, o_mix, o_value, o_out, o_in, o_fout = join(chan, mix_weight, value_weight, out_weight, ffn_in, ffn_out)
    chan = gather_small(chan)
    flat = chan[:, :, 4 * H + 6 :].reshape(n_wsh, -1).astype(F32)
    chan = chan[:, :, : 4 * H + 6].reshape(D, -1).T.astype(F32)
    rate = jax.nn.sigmoid(chan[0:H])
    damp = jax.nn.sigmoid(chan[H : 2 * H])
    beta = chan[2 * H : 3 * H]
    eta = chan[3 * H : 4 * H]
    omega = chan[4 * H : 4 * H + 1]
    keep = 1.0 - rate * damp
    weight = eta * beta * rate
    decay = power(keep, L)
    inward = eta * beta * rate
    x3 = tokens.reshape(G, L, D)
    x = tokens.reshape(T, D)
    y_step, z_steps = ("seq", 1), [("seq", s) for s in seq_steps()[1:]]
    x_step = ("wsh", 2)
    sixth = D // LANES // 6
    steps = seq_steps()
    half = D // LANES // 2

    x_mix = over_x(own_half(o_mix))
    c_mix, c_value = over_core(o_mix), over_core(o_value)
    ends, slice_end = ema_ends(x3, keep)
    ends, slice_end, c_mix, c_value, o_value, o_out = join(ends, slice_end, c_mix, c_value, o_value, o_out)
    x_value, x_out = over_x(own_half(o_value)), over_x(own_half(o_out))
    entry = Carry(slice_end, decay, False)
    sent, x_mix, chan, flat, rate, damp, inward, keep_later, lengths = join(
        entry.send(steps[0]), x_mix, chan, flat, rate, damp, inward, keep, lengths
    )
    vectors, start = [], 0
    for part in flat_parts:
        vectors.append(flat[:, start : start + part.shape[0]].reshape(1, -1))
        start += part.shape[0]
    bm, bv, bf, rel, gain_q, gain_k, shift_q = vectors
    norms = jnp.concatenate([chan[4 * H + 1 : 4 * H + 5], jnp.zeros((4, D), F32)])
    bo = chan[4 * H + 5 : 4 * H + 6]
    qk = jnp.concatenate([gain_q, gain_k, shift_q, jnp.zeros((5, Z), F32)])
    rel_matrix = skew_matrix(jnp.roll(rel[0, ::-1], BLOCK))
    inverse = 1.0 / keep_later
    factors = jnp.concatenate(
        [
            inward * (1.0 - rate), -inward * (1.0 - rate) * damp * rate, -inward * rate * damp * (1.0 - damp),
            rate * eta, rate * beta,
        ]
    )
    position = i * L + jnp.arange(L, dtype=jnp.int32)
    live = (position[None, :] < lengths.reshape(G)[:, None]).astype(F32).reshape(T, 1)
    entry.add(steps[0], sent)
    y_mix, xc_mix = over_y(x_mix), over_core(x_mix)
    for step in steps[1:]:
        entry.add(step, entry.send(step))
    state_in, x_value, xc_mix, rel_matrix, norms, bo, qk, inverse, factors, live, bm = join(
        entry.entry, x_value, xc_mix, rel_matrix, norms, bo, qk, inverse, factors, live, bm
    )
    y_value, xc_value = over_y(x_value), over_core(x_value)
    so_far = ema_forward((0, half), (), x3, keep, weight, omega, ends, state_in)
    *so_far, y_mix, x_out, xc_value, o_out, o_in, o_fout = join(*so_far, y_mix, x_out, xc_value, o_out, o_in, o_fout)
    y_out, xc_out, yc_mix = over_y(x_out), over_core(x_out), over_core(y_mix)
    c_out = over_core(o_out)
    x_in = over_x(o_in)
    xp, pre, finals = ema_forward((half, half), tuple(so_far), x3, keep, weight, omega, ends, state_in)
    xp, y_value, y_out, xc_out, yc_mix, c_out, o_fout = join(xp, y_value, y_out, xc_out, yc_mix, c_out, o_fout)
    yc_value, yc_out = over_core(y_value), over_core(y_out)
    x_fout = over_x(o_fout)
    mix_pieces = (
        (o_mix, c_mix, x_mix, y_mix, xc_mix, yc_mix) + (o_value, c_value, x_value, y_value, xc_value, yc_value)
        + (o_out, c_out, x_out, y_out, xc_out, yc_out)
    )
    c_in, c_fout = over_core(o_in), over_core(o_fout)
    xp = xp.reshape(T, D)
    forward = mix_forward(min(256, T), x, xp, bm, bv, qk, rel_matrix, mix_pieces)
    (u, h, r, v, z, p, mixed), x_in, x_fout, c_in, c_fout = join(forward, x_in, x_fout, c_in, c_fout)
    ffn_pieces = (o_in, c_in, x_in, over_core(x_in)) + (o_fout, c_fout, x_fout, over_core(x_fout))
    output, h1, act, dg, df, dum, dt, sum_d, sum_f = ffn_both(
        R, x, u, h, cotangent.reshape(T, D), live, norms, bf, bo, ffn_pieces
    )

    (sent_1, kept_1), (sent_2, kept_2) = send_core(dot_rows(act, dg)), send_core(dot_rows(h1, df))
    (sent_3, kept_3), (sent_4, kept_4) = send_core(dot_rows(mixed, dum[:, D:])), send_core(dot_rows(xp, dum))
    kept_3, kept_4, sent_1, sent_2 = join(kept_3, kept_4, sent_1, sent_2)
    sum_a = Sum(merge([add_half(sent_1, kept_1), add_half(sent_2, kept_2)], D))
    over_a = sum_a.send(x_step)
    sum_b = Sum(merge([add_half(sent_3, kept_3), add_half(sent_4, kept_4)], D))
    over_b = sum_b.send(y_step)
    back = mix_backward(min(256, T), dum, dt, r, v, z, p, qk, sum_d, sum_f, mix_pieces)
    (db, dv, dxp, dtok, early), over_a, over_b = join(back, over_a, over_b)
    sum_a.add(over_a)
    sum_b.add(over_b)
    over_a, over_b = sum_a.send(y_step), sum_b.send(x_step)
    sent_1, kept_1 = send_core(dot_rows(xp, db))
    dxp, kept_1, over_a, over_b = join(dxp, kept_1, over_a, over_b)
    sum_a.add(over_a)
    sum_b.add(over_b)
    rows_a = sum_a.value.shape[-2]
    sum_a.value = jnp.concatenate([sum_a.value, sum_b.value], axis=-2)
    over_a = sum_a.send(z_steps[0])
    dpe, back_ends, slice_start = ema_back_ends(dxp.reshape(G, L, D), pre, keep)
    dpe, back_ends, slice_start, over_a, sent_1, dv = join(dpe, back_ends, slice_start, over_a, sent_1, dv)
    sum_a.add(over_a)
    sum_c = Sum(add_half(sent_1, kept_1))
    over_a = sum_a.send(z_steps[1])
    entry = Carry(slice_start, decay, True)
    sent = entry.send(steps[0])
    sent_2, kept_2 = send_core(dot_rows(x, dv))
    kept_2, sent, over_a = join(kept_2, sent, over_a)
    over_c = sum_c.send(x_step)
    entry.add(steps[0], sent)
    sent, sent_2 = join(entry.send(steps[1]), sent_2)
    entry.add(steps[1], sent)
    sum_d_ = Sum(add_half(sent_2, kept_2))
    over_d = sum_d_.send(y_step)
    for step in steps[2:]:
        entry.add(step, entry.send(step))
    state_in = entry.entry
    consts = (dpe, x3, keep, inverse, weight, omega, finals, back_ends, state_in, dtok.reshape(G, L, D), factors)
    order = list(reversed(steps))

    def back_part(k, so_far):
        return ema_backward((k * sixth, sixth), tuple(so_far), *consts)

    so_far = back_part(0, ())
    *so_far, over_a, over_c = join(*so_far, over_a, over_c)
    sum_a.add(over_a)
    for mark in z_steps[2:]:
        sum_a.add(sum_a.send(mark))
    sum_c.add(over_c)
    over_c = sum_c.send(y_step)
    block = sum_a.value.astype(BF16)[None]
    more = exchange(block, "seq", order[0])
    so_far = back_part(1, so_far)
    *so_far, over_c, over_d, more = join(*so_far, over_c, over_d, more)
    sum_c.add(over_c)
    sum_d_.add(over_d)
    over_d = sum_d_.send(x_step)
    block = widen(block, more, order[0])
    more = exchange(block, "seq", order[1])
    so_far = back_part(2, so_far)
    *so_far, over_d, more = join(*so_far, over_d, more)
    sum_d_.add(over_d)
    block = widen(block, more, order[1])
    more = exchange(block, "seq", order[2])
    cols_c = sum_c.value.shape[-1]
    sum_c.value = jnp.concatenate([sum_c.value, sum_d_.value], axis=-1)
    over_c = sum_c.send(z_steps[0])
    so_far = back_part(3, so_far)
    *so_far, over_c = join(*so_far, over_c)
    sum_c.add(over_c)
    over_c = sum_c.send(z_steps[1])
    so_far = back_part(4, so_far)
    *so_far, over_c = join(*so_far, over_c)
    sum_c.add(over_c)
    for mark in z_steps[2:]:
        sum_c.add(sum_c.send(mark))
    small = sum_c.value.astype(BF16)[None]
    over_c = exchange(small, "seq", order[0])
    so_far = back_part(5, so_far)
    *so_far, over_c, more = join(*so_far, over_c, more)
    small = widen(small, over_c, order[0])
    block = widen(block, more, order[2])
    for step in order[3:]:
        block = widen(block, exchange(block, "seq", step), step)
    input_grad, late = so_far
    over_c = exchange(small, "seq", order[1])
    late = late.reshape(-1, n_wsh, D // n_wsh).transpose(1, 0, 2)
    sides = jnp.concatenate([early[:, k : k + D // n_wsh] for k in range(0, D, D // n_wsh)])
    late = jnp.concatenate([late, jnp.broadcast_to(sides, (n_wsh,) + sides.shape)], axis=1)
    late, over_c = join(sum_over_wsh(late), over_c)
    small = widen(small, over_c, order[1])
    over_c = exchange(small, "seq", order[2])
    late, over_c = join(sum_over_seq(late), over_c)
    small = widen(small, over_c, order[2])
    for step in order[3:]:
        small = widen(small, exchange(small, "seq", step), step)
    block, small = in_order(block), in_order(small)
    g_a, g_b = block[:, :rows_a].reshape(-1, D).astype(F32), block[:, rows_a:].reshape(-1, D).astype(F32)
    small = small.reshape(-1, small.shape[-1]).astype(F32)
    g_c, g_d = small[:, :cols_c], small[:, cols_c:]
    input_grad = input_grad.reshape(tokens.shape)

    FF = ffn_in.shape[1]
    sides = late[4 * H + 8 :].reshape(n_wsh, 16, -1)
    early = jnp.concatenate([sides[k] for k in range(n_wsh)], axis=1)
    spans = {}
    for name, start, row, col, size in sum_spots(D, Z, V, FF):
        spans[name, start] = early[row, col : col + size]

    def span_of(name):
        return jnp.concatenate([spans[key] for key in sorted(spans) if key[0] == name])

    j = lax.axis_index("wsh")
    qk_sums, row_sums = span_of("qk"), span_of("rows")
    smalls = []
    for part in (
        span_of("mix"), span_of("value"), span_of("ffn"), span_of("rel"),
        *(qk_sums[k * Z : k * Z + Z] for k in range(3)), *(row_sums[k * D : k * D + D] for k in range(5)),
    ):
        size = part.shape[0] // n_wsh
        smalls.append(lax.dynamic_slice(part, (j * size,), (size,)))
    (
        g_mix_bias, g_value_bias, g_ffn_in_bias, g_rel, g_gain_q, g_gain_k, g_shift, gain_1, gain_2, shift_1, shift_2,
        g_ffn_out_bias,
    ) = smalls
    late = late[: 4 * H + 1].T
    tall_rows, wide_rows = ffn_out.shape[0], ffn_in.shape[0]
    n_seq = lax.axis_size("seq")
    first_rows = tall_rows // n_seq

    def unmerge(merged):
        parts = merged.reshape(n_seq, -1, D)
        top = parts[:, :first_rows].reshape(tall_rows, D)
        sides = parts[:, first_rows:].reshape(n_seq, 2, wide_rows // n_seq, D)
        return top, jnp.concatenate([sides[:, k].reshape(wide_rows, D) for k in range(2)], axis=1)

    g_ffn_out, g_ffn_in = unmerge(g_a)
    g_out, g_edges = unmerge(g_b)
    g_mix = jnp.concatenate([g_edges[:, :D], g_c, g_edges[:, D:]], axis=1)
    return (
        output.reshape(tokens.shape), input_grad,
        late[:, 0:H], late[:, H : 2 * H], late[:, 2 * H : 3 * H], late[:, 3 * H : 4 * H], late[:, 4 * H],
        g_mix, g_mix_bias, g_d, g_value_bias,
        jnp.stack([g_gain_q, g_gain_k], axis=1), g_shift, g_rel, g_out,
        jnp.stack([gain_1, gain_2], axis=1), jnp.stack([shift_1, shift_2], axis=1),
        g_ffn_in, g_ffn_in_bias, g_ffn_out, g_ffn_out_bias,
    )


def solution(mesh):
    in_specs = (
        P(None, "wsh", "seq", None),
        P(None, "wsh", "seq", None),
        P(None, "wsh"),
        P("wsh", None),
        P("wsh", None),
        P("wsh", None),
        P("wsh", None),
        P("wsh"),
        P("wsh", None),
        P("wsh"),
        P("wsh", None),
        P("wsh"),
        P("wsh", None),
        P("wsh"),
        P("wsh"),
        P("wsh", None),
        P("wsh", None),
        P("wsh", None),
        P("wsh", None),
        P("wsh"),
        P("wsh", None),
        P("wsh"),
    )
    out_specs = (
        P(None, "wsh", "seq", None),
        P(None, "wsh", "seq", None),
        P("wsh", None),
        P("wsh", None),
        P("wsh", None),
        P("wsh", None),
        P("wsh"),
        P("wsh", None),
        P("wsh"),
        P("wsh", None),
        P("wsh"),
        P("wsh", None),
        P("wsh"),
        P("wsh"),
        P("wsh", None),
        P("wsh", None),
        P("wsh", None),
        P("wsh", None),
        P("wsh"),
        P("wsh", None),
        P("wsh"),
    )
    return jax.shard_map(body, mesh=mesh, in_specs=in_specs, out_specs=out_specs, check_vma=False)
```

profile of v0, /device:TPU:0, one launch (start us, length us, event | category | flops | bytes accessed | tf_op | source)
XLA Modules:
  0.0 443.5 jit_solution(5294183525661273962)
XLA Ops:
  1.4 3.5 concatenate.79
  6.5 3.6 concatenate.80
  10.7 2.6 collective-permute-start.1
  15.1 1.7 collective-permute-start.6
  18.5 11.5 %ema_ends.1 = (f32[2,128,768]{2,1,0:T(8,128)}, f32[2,16,768]{2,1,0:T(8,128)}) custom-call(bf16[2,1024,768]{2,1,0:T(8,128)(2,1)} %bitcast.226, f32[16,768]{1,0:T(8,128)} %get-tuple-element.190.q_ref), custom_call_target="tpu_custom_call" | custom-call | bytes 39600000 | tf_op jit(solution)/shard_map/ema_ends/pallas_call | solution.py:182
  31.5 1.5 collective-permute-start.5
  34.9 1.3 collective-permute-start.12
  36.5 1.5 collective-permute-start.11
  38.5 1.6 collective-permute-start.7
  41.2 2.3 collective-permute-done.7
  43.5 2.7 collective-permute-start.8
  52.1 10.7 %ema_forward.2 = (bf16[2,1024,768]{2,1,0:T(8,128)(2,1)}, f32[2,1024,768]{2,1,0:T(8,128)}, f32[2,128,768]{2,1,0:T(8,128)}) custom-call(bf16[2,1024,768]{2,1,0:T(8,128)(2,1)} %bitcast.227, f32[16,768]{1,0:T(8,128)} %get-tuple-element.190.q_ref, f32[16,768]{1,0:T(8,128)} %copy-done.9, f32[1,768]{1,0:T(1,128)} %slice.330.om_ref, ...), custom_call_target="tpu_custom_call" | custom-call | bytes 32400000 | tf_op jit(solution)/shard_map/ema_forward/pallas_call | solution.py:199
  64.0 1.5 collective-permute-start.15
  65.5 10.7 %ema_forward.3 = (bf16[2,1024,768]{2,1,0:T(8,128)(2,1)}, f32[2,1024,768]{2,1,0:T(8,128)}, f32[2,128,768]{2,1,0:T(8,128)}) custom-call(bf16[2,1024,768]{2,1,0:T(8,128)(2,1)} %bitcast.228, f32[16,768]{1,0:T(8,128)} %get-tuple-element.190.q_ref, f32[16,768]{1,0:T(8,128)} %copy-done.9, ...), custom_call_target="tpu_custom_call", output_to_operand_aliasing={{0}: (6, {}), {1}: (7, {}), {2}: (8, {})} | custom-call | bytes 32400000 | tf_op jit(solution)/shard_map/ema_forward/pallas_call | solution.py:199
  76.2 3.2 collective-permute-done.15.refs_15_
  83.7 32.6 %mix_forward.1 = (f32[2048,768]{1,0:T(8,128)}, f32[2048,768]{1,0:T(8,128)}, f32[2048,1536]{1,0:T(8,128)}, f32[2048,1536]{1,0:T(8,128)}, f32[2048,128]{1,0:T(8,12...) custom-call(bf16[2048,768]{1,0:T(8,128)(2,1)} %bitcast.229, bf16[2048,768]{1,0:T(8,128)(2,1)} %bitcast.245, ...), custom_call_target="tpu_custom_call" | custom-call | flops 19730006016 | bytes 118800000 | tf_op jit(solution)/shard_map/mix_forward/pallas_call | solution.py:621
  117.6 1.3 copy.75.live_ref
  118.9 4.7 %copy.77 = bf16[768,2048]{1,0:T(8,128)(2,1)} copy(bf16[768,2048]{0,1:T(8,128)(2,1)} %bitcast.246) | data formatting | bytes 6291456 | tf_op jit(solution)/shard_map/ri,rj->ij/dot_general | solution.py:23
  124.5 42.6 %ffn_both.1 = (bf16[2048,768]{1,0:T(8,128)(2,1)}, bf16[2048,768]{1,0:T(8,128)(2,1)}, bf16[2048,1536]{1,0:T(8,128)(2,1)}, bf16[2048,768]{1,0:T(8,128)(2,1)}, bf16...) custom-call(bf16[2048,768]{1,0:T(8,128)(2,1)} %bitcast.230, ...), custom_call_target="tpu_custom_call" | custom-call | flops 19327352832 | bytes 180000000 | tf_op jit(solution)/shard_map/ffn_both/pallas_call | solution.py:643
  167.2 8.8 %fusion.91 = f32[768,1536]{1,0:T(8,128)S(1)} fusion(bf16[2048,768]{1,0:T(8,128)(2,1)} %get-tuple-element.259, bf16[2048,1536]{1,0:T(8,128)(2,1)} %get-tuple-element.260), kind=kOutput, calls=%fused_computation.267 | convolution fusion | flops 4831838208 | bytes 14155776 | tf_op jit(solution)/shard_map/ri,rj->ij/dot_general | solution.py:23
  176.5 5.1 %fusion.90 = f32[1536,768]{1,0:T(8,128)S(1)} fusion(bf16[2048,1536]{1,0:T(8,128)(2,1)S(1)} %copy-done.43, bf16[2048,768]{1,0:T(8,128)(2,1)S(1)} %copy-done.44), kind=kOutput, calls=%fused_computation.266 | convolution fusion | flops 4831838208 | bytes 14155776 | tf_op jit(solution)/shard_map/ri,rj->ij/dot_general | solution.py:23
  182.1 5.1 %fusion.2 = f32[2,2,2,2,2,24,1536]{6,5,4,3,2,1,0:T(8,128)S(1)} fusion(bf16[2,2,2,2,2,24,2048]{6,5,4,3,2,1,0:T(8,128)(2,1)S(1)} %bitcast.254, bf16[2048,1536]{1,0:T(8,128)(2,1)S(1)} %bitcast.297), kind=kOutput, calls=%fused_computation.2 | convolution fusion | flops 4831838208 | bytes 14155776 | tf_op jit(solution)/shard_map/ri,rj->ij/dot_general | solution.py:23
  187.7 8.4 %fusion.4 = f32[1536,768]{1,0:T(8,128)S(1)} fusion(bf16[2048,1536]{1,0:T(8,128)(2,1)} %get-tuple-element.258, bf16[2048,1536]{1,0:T(8,128)(2,1)} %get-tuple-element.243.dum_ref), kind=kOutput, calls=%fused_computation.6 | convolution fusion | flops 4831838208 | bytes 14155776 | tf_op jit(solution)/shard_map/ri,rj->ij/dot_general | solution.py:23
  197.6 1.6 collective-permute-done.30
  203.1 2.3 copy-done.2
  207.5 40.6 %mix_backward.1 = (bf16[2048,1664]{1,0:T(8,128)(2,1)}, bf16[2048,1536]{1,0:T(8,128)(2,1)}, bf16[2048,768]{1,0:T(8,128)(2,1)}, f32[2048,768]{1,0:T(8,128)}, f32[16,768]{1,0:T(8,128)}) custom-call(bf16[2048,1536]{1,0:T(8,128)(2,1)} %get-tuple-element.243.dum_ref, f32[2048,768]{1,0:T(8,128)} %get-tuple-element.244.dt_ref, ...), custom_call_target="tpu_custom_call" | custom-call | flops 19730006016 | bytes 144000000 | tf_op jit(solution)/shard_map/mix_backward/pallas_call | solution.py:671
  248.2 2.4 bitcast_add_fusion
  251.8 1.6 bitcast_add_fusion.1
  254.1 8.8 %fusion = f32[2,2,2,2,2,24,1664]{6,5,4,3,2,1,0:T(8,128)S(1)} fusion(bf16[2,2,2,2,2,24,2048]{6,5,4,3,2,1,0:T(8,128)(2,1)S(1)} %bitcast.255, bf16[2048,1664]{1,0:T(8,128)(2,1)} %get-tuple-element.266), kind=kOutput, calls=%fused_computation | convolution fusion | flops 5234491392 | bytes 15073280 | tf_op jit(solution)/shard_map/ri,rj->ij/dot_general | solution.py:23
  262.9 1.2 fusion.6
  264.1 1.7 dynamic-slice_bitcast_fusion
  265.9 2.6 collective-permute-done.33
  269.6 14.8 %ema_back_ends.1 = (f32[2,1024,768]{2,1,0:T(8,128)}, f32[2,128,768]{2,1,0:T(8,128)}, f32[2,16,768]{2,1,0:T(8,128)}) custom-call(bf16[2,1024,768]{2,1,0:T(8,128)(2,1)} %bitcast.256, f32[2,1024,768]{2,1,0:T(8,128)} %get-tuple-element.270.p_ref, f32[16,768]{1,0:T(8,128)} %get-tuple-element.190.q_ref), custom_call_target="tpu_custom_call" | custom-call | bytes 54000000 | tf_op jit(solution)/shard_map/ema_back_ends/pallas_call | solution.py:222
  285.5 3.4 collective-permute-start.38
  288.9 7.5 %fusion.92 = f32[1536,768]{0,1:T(8,128)S(1)} fusion(bf16[2048,1536]{1,0:T(8,128)(2,1)} %get-tuple-element.281, bf16[2048,768]{1,0:T(8,128)(2,1)S(1)} %bitcast.237), kind=kOutput, calls=%fused_computation.268 | convolution fusion | flops 4831838208 | bytes 14155776 | tf_op jit(solution)/shard_map/ri,rj->ij/dot_general | solution.py:23
  297.3 1.5 convert_add_fusion
  299.0 2.2 collective-permute-done.37
  302.5 3.4 collective-permute-done.39
  305.9 1.2 collective-permute-start.41
  307.5 1.4 copy-done.7
  310.3 1.9 collective-permute-done.41
  312.9 10.2 %ema_backward.6 = (bf16[2,1024,768]{2,1,0:T(8,128)(2,1)}, f32[72,768]{1,0:T(8,128)}) custom-call(f32[2,1024,768]{2,1,0:T(8,128)} %get-tuple-element.277.d_ref, bf16[2,1024,768]{2,1,0:T(8,128)(2,1)} %bitcast.231, f32[16,768]{1,0:T(8,128)} %get-tuple-element.190.q_ref, f32[16,768]{1,0:T(8,128)} %get-tuple-element.278.qi_ref, f32[16,768]{1,0:T(8,128)} %copy-done.9, ...), custom_call_target="tpu_custom_call" | custom-call | bytes 28800000 | tf_op jit(solution)/shard_map/ema_backward/pallas_call | solution.py:244
  323.2 1.3 bitcast_add_fusion.4
  327.1 10.0 %ema_backward.7 = (bf16[2,1024,768]{2,1,0:T(8,128)(2,1)}, f32[72,768]{1,0:T(8,128)}) custom-call(f32[2,1024,768]{2,1,0:T(8,128)} %get-tuple-element.277.d_ref, bf16[2,1024,768]{2,1,0:T(8,128)(2,1)} %bitcast.232, f32[16,768]{1,0:T(8,128)} %get-tuple-element.190.q_ref, ...), custom_call_target="tpu_custom_call", output_to_operand_aliasing={{0}: (11, {}), {1}: (12, {})} | custom-call | bytes 28800000 | tf_op jit(solution)/shard_map/ema_backward/pallas_call | solution.py:244
  337.1 2.3 collective-permute-done.45
  340.5 1.2 bitcast_add_fusion.5
  343.5 10.0 %ema_backward.8 = (bf16[2,1024,768]{2,1,0:T(8,128)(2,1)}, f32[72,768]{1,0:T(8,128)}) custom-call(f32[2,1024,768]{2,1,0:T(8,128)} %get-tuple-element.277.d_ref, bf16[2,1024,768]{2,1,0:T(8,128)(2,1)} %bitcast.233, f32[16,768]{1,0:T(8,128)} %get-tuple-element.190.q_ref, ...), custom_call_target="tpu_custom_call", output_to_operand_aliasing={{0}: (11, {}), {1}: (12, {})} | custom-call | bytes 28800000 | tf_op jit(solution)/shard_map/ema_backward/pallas_call | solution.py:244
  356.2 1.6 collective-permute-start.48
  357.8 10.0 %ema_backward.9 = (bf16[2,1024,768]{2,1,0:T(8,128)(2,1)}, f32[72,768]{1,0:T(8,128)}) custom-call(f32[2,1024,768]{2,1,0:T(8,128)} %get-tuple-element.277.d_ref, bf16[2,1024,768]{2,1,0:T(8,128)(2,1)} %bitcast.234, f32[16,768]{1,0:T(8,128)} %get-tuple-element.190.q_ref, ...), custom_call_target="tpu_custom_call", output_to_operand_aliasing={{0}: (11, {}), {1}: (12, {})} | custom-call | bytes 28800000 | tf_op jit(solution)/shard_map/ema_backward/pallas_call | solution.py:244
  371.0 1.4 collective-permute-start.51
  372.4 10.0 %ema_backward.10 = (bf16[2,1024,768]{2,1,0:T(8,128)(2,1)}, f32[72,768]{1,0:T(8,128)}) custom-call(f32[2,1024,768]{2,1,0:T(8,128)} %get-tuple-element.277.d_ref, bf16[2,1024,768]{2,1,0:T(8,128)(2,1)} %bitcast.235, f32[16,768]{1,0:T(8,128)} %get-tuple-element.190.q_ref, ...), custom_call_target="tpu_custom_call", output_to_operand_aliasing={{0}: (11, {}), {1}: (12, {})} | custom-call | bytes 28800000 | tf_op jit(solution)/shard_map/ema_backward/pallas_call | solution.py:244
  383.4 2.2 collective-permute-start.50
  385.7 10.1 %ema_backward.11 = (bf16[2,1024,768]{2,1,0:T(8,128)(2,1)}, f32[72,768]{1,0:T(8,128)}) custom-call(f32[2,1024,768]{2,1,0:T(8,128)} %get-tuple-element.277.d_ref, bf16[2,1024,768]{2,1,0:T(8,128)(2,1)} %bitcast.236, f32[16,768]{1,0:T(8,128)} %get-tuple-element.190.q_ref, ...), custom_call_target="tpu_custom_call", output_to_operand_aliasing={{0}: (11, {}), {1}: (12, {})} | custom-call | bytes 28800000 | tf_op jit(solution)/shard_map/ema_backward/pallas_call | solution.py:244
  395.8 1.8 collective-permute-done.51
  400.7 1.4 collective-permute-start.53
  403.7 1.2 fusion.78
  406.0 1.2 collective-permute-done.53
  407.2 2.2 collective-permute-done.54
  410.6 1.8 collective-permute-start.59
  412.4 1.8 collective-permute-start.56
  414.3 7.5 %collective-permute-done.56 = f32[136,192]{1,0:T(8,128)S(1)} collective-permute-done((f32[136,192]{1,0:T(8,128)S(1)}, f32[136,192]{1,0:T(8,128)S(1)}, u32[]{:S(2)}, u32[]{:S(2)}) %collective-permute-start.56) | collective-permute-done | bytes 104480 | tf_op jit(solution)/shard_map/ppermute | solution.py:697
  422.0 5.0 %collective-permute-done.57 = f32[136,192]{1,0:T(8,128)S(1)} collective-permute-done((f32[136,192]{1,0:T(8,128)S(1)}, f32[136,192]{1,0:T(8,128)S(1)}, u32[]{:S(2)}, u32[]{:S(2)}) %collective-permute-start.57) | collective-permute-done | bytes 104480 | tf_op jit(solution)/shard_map/ppermute | solution.py:697
  428.5 3.5 collective-permute-done.58
  441.4 1.6 pad_maximum_fusion.2
  (339 shorter events, 73.0 us)
Async XLA Ops:
  10.2 5.0 %collective-permute-start = (bf16[192,79]{0,1:T(8,128)(2,1)S(1)}, bf16[192,79]{0,1:T(8,128)(2,1)S(1)}, u32[]{:S(2)}, u32[]{:S(2)}) collective-permute-start(bf16[192,79]{0,1:T(8,128)(2,1)S(1)} %concatenate.80), channel_id=1, source_target_pairs={{0,1},{1,0},{2,3},{3,2},{4,5},{5,4},{6,7},{7,6},{8,9},{9,8},{10,11... | collective-permute-start | bytes 91016 | tf_op jit(solution)/shard_map/ppermute | solution.py:697
  10.7 6.2 %collective-permute-start.1 = (bf16[192,79]{0,1:T(8,128)(2,1)S(1)}, bf16[192,79]{0,1:T(8,128)(2,1)S(1)}, u32[]{:S(2)}, u32[]{:S(2)}) collective-permute-start(bf16[192,79]{0,1:T(8,128)(2,1)S(1)} %concatenate.80), channel_id=1, source_target_pairs={{0,2},{1,3},{2,0},{3,1},{4,6},{5,7},{6,4},{7,5},{8,10},{9,11},{10,... | collective-permute-start | bytes 91016 | tf_op jit(solution)/shard_map/ppermute | solution.py:697
  13.2 3.6 collective-permute-start.2
  13.3 17.4 %collective-permute-start.3 = (bf16[192,3200]{1,0:T(8,128)(2,1)}, bf16[192,3200]{1,0:T(8,128)(2,1)}, u32[]{:S(2)}, u32[]{:S(2)}) collective-permute-start(bf16[192,3200]{1,0:T(8,128)(2,1)} %refs_0_.2), channel_id=1, source_target_pairs={{0,1},{1,0},{2,3},{3,2},{4,5},{5,4},{6,7},{7,6},{8,9},{9,8},{10,11... | collective-permute-start | bytes 3686408 | tf_op jit(solution)/shard_map/ppermute | solution.py:697
  13.4 17.2 %collective-permute-start.4 = (bf16[192,1536]{1,0:T(8,128)(2,1)}, bf16[192,1536]{1,0:T(8,128)(2,1)S(1)}, u32[]{:S(2)}, u32[]{:S(2)}) collective-permute-start(bf16[192,1536]{1,0:T(8,128)(2,1)} %refs_6_.1), channel_id=1, source_target_pairs={{0,1},{1,0},{2,3},{3,2},{4,5},{5,4},{6,7},{7,6},{8,9},{9,8},{10,11... | collective-permute-start | bytes 1769480 | tf_op jit(solution)/shard_map/ppermute | solution.py:697
  15.1 21.1 %collective-permute-start.6 = (bf16[96,3200]{1,0:T(8,128)(2,1)S(1)}, bf16[96,3200]{1,0:T(8,128)(2,1)}, u32[]{:S(2)}, u32[]{:S(2)}) collective-permute-start(bf16[96,3200]{1,0:T(8,128)(2,1)S(1)} %constant_dynamic-slice_fusion.31), channel_id=1, source_target_pairs={{0,2},{1,3},{2,0},{3,1},{4,6},{5,7},{6,4},{7,5},{8,10},{9,11},{10,... | collective-permute-start | bytes 1843208 | tf_op jit(solution)/shard_map/ppermute | solution.py:697
  18.5 22.3 %copy-start.31 = (s32[2,1]{0,1:T(1,128)S(1)}, s32[2,1]{0,1:T(1,128)}, u32[]{:S(2)}) copy-start(s32[2,1]{0,1:T(1,128)} %param.24) | copy-start | bytes 28
  30.7 32.1 %copy-start.18 = (f32[16,768]{1,0:T(8,128)}, f32[16,768]{1,0:T(8,128)S(1)}, u32[]{:S(2)}) copy-start(f32[16,768]{1,0:T(8,128)S(1)} %get-tuple-element.441) | copy-start | bytes 147460
  30.7 32.1 %copy-start.20 = (f32[16,768]{1,0:T(8,128)}, f32[16,768]{1,0:T(8,128)S(1)}, u32[]{:S(2)}) copy-start(f32[16,768]{1,0:T(8,128)S(1)} %get-tuple-element.444) | copy-start | bytes 147460
  31.5 5.0 %collective-permute-start.5 = (f32[2,16,768]{2,1,0:T(8,128)}, f32[2,16,768]{2,1,0:T(8,128)S(1)}, u32[]{:S(2)}, u32[]{:S(2)}) collective-permute-start(f32[2,16,768]{2,1,0:T(8,128)} %get-tuple-element.184), channel_id=1, source_target_pairs={{0,4},{4,0},{8,12},{12,8},{16,20},{20,16},{24,28},{28,24},{1,5},{5... | collective-permute-start | bytes 294920 | tf_op jit(solution)/shard_map/ppermute | solution.py:697
  33.1 18.4 %collective-permute-start.9 = (bf16[96,1536]{1,0:T(8,128)(2,1)S(1)}, bf16[96,1536]{1,0:T(8,128)(2,1)}, u32[]{:S(2)}, u32[]{:S(2)}) collective-permute-start(bf16[96,1536]{1,0:T(8,128)(2,1)S(1)} %constant_dynamic-slice_fusion.30), channel_id=1, source_target_pairs={{0,2},{1,3},{2,0},{3,1},{4,6},{5,7},{6,4},{7,5},{8,10},{9,11},{10,... | collective-permute-start | bytes 884744 | tf_op jit(solution)/shard_map/ppermute | solution.py:697
  34.9 27.9 %collective-permute-start.12 = (bf16[192,768]{1,0:T(8,128)(2,1)S(1)}, bf16[192,768]{1,0:T(8,128)(2,1)}, u32[]{:S(2)}, u32[]{:S(2)}) collective-permute-start(bf16[192,768]{1,0:T(8,128)(2,1)S(1)} %constant_dynamic-slice_fusion.29), channel_id=1, source_target_pairs={{0,2},{1,3},{2,0},{3,1},{4,6},{5,7},{6,4},{7,5},{8,10},{9,11},{10,... | collective-permute-start | bytes 884744 | tf_op jit(solution)/shard_map/ppermute | solution.py:697
  36.5 15.0 %collective-permute-start.10 = (bf16[96,3200]{1,0:T(8,128)(2,1)}, bf16[96,3200]{1,0:T(8,128)(2,1)}, u32[]{:S(2)}, u32[]{:S(2)}) collective-permute-start(bf16[96,3200]{1,0:T(8,128)(2,1)} %collective-permute-done.6.refs_2_), channel_id=1, source_target_pairs={{0,1},{1,0},{2,3},{3,2},{4,5},{5,4},{6,7},{7,6},{8,9},{9,8},{10,11... | collective-permute-start | bytes 1843208 | tf_op jit(solution)/shard_map/ppermute | solution.py:697
  36.5 26.3 %collective-permute-start.11 = (bf16[96,3200]{1,0:T(8,128)(2,1)}, bf16[96,3200]{1,0:T(8,128)(2,1)}, u32[]{:S(2)}, u32[]{:S(2)}) collective-permute-start(bf16[96,3200]{1,0:T(8,128)(2,1)} %collective-permute-done.6.refs_2_), channel_id=1, source_target_pairs={{0,4},{4,0},{8,12},{12,8},{16,20},{20,16},{24,28},{28,24},{1,5},{5... | collective-permute-start | bytes 1843208 | tf_op jit(solution)/shard_map/ppermute | solution.py:697
  38.5 5.0 %collective-permute-start.7 = (f32[2,16,768]{2,1,0:T(8,128)S(1)}, f32[2,16,768]{2,1,0:T(8,128)S(1)}, u32[]{:S(2)}, u32[]{:S(2)}) collective-permute-start(f32[2,16,768]{2,1,0:T(8,128)S(1)} %add_select_fusion.7), channel_id=1, source_target_pairs={{0,8},{4,12},{8,0},{12,4},{16,24},{20,28},{24,16},{28,20},{1,9},{5... | collective-permute-start | bytes 294920 | tf_op jit(solution)/shard_map/ppermute | solution.py:697
  40.8 22.0 %copy-start.5 = (f32[80,768]{1,0:T(8,128)}, f32[80,768]{1,0:T(8,128)S(1)}, u32[]{:S(2)}) copy-start(f32[80,768]{1,0:T(8,128)S(1)} %get-tuple-element.287.k_ref) | copy-start | bytes 737284
  43.5 7.3 %collective-permute-start.8 = (f32[2,16,768]{2,1,0:T(8,128)S(1)}, f32[2,16,768]{2,1,0:T(8,128)S(1)}, u32[]{:S(2)}, u32[]{:S(2)}) collective-permute-start(f32[2,16,768]{2,1,0:T(8,128)S(1)} %add_select_fusion.6), channel_id=1, source_target_pairs={{0,16},{4,20},{8,24},{12,28},{16,0},{20,4},{24,8},{28,12},{1,17},{... | collective-permute-start | bytes 294920 | tf_op jit(solution)/shard_map/ppermute | solution.py:697
  51.5 11.3 %collective-permute-start.13 = (bf16[96,1536]{1,0:T(8,128)(2,1)}, bf16[96,1536]{1,0:T(8,128)(2,1)S(1)}, u32[]{:S(2)}, u32[]{:S(2)}) collective-permute-start(bf16[96,1536]{1,0:T(8,128)(2,1)} %collective-permute-done.9.refs_8_), channel_id=1, source_target_pairs={{0,1},{1,0},{2,3},{3,2},{4,5},{5,4},{6,7},{7,6},{8,9},{9,8},{10,11... | collective-permute-start | bytes 884744 | tf_op jit(solution)/shard_map/ppermute | solution.py:697
  62.8 16.6 %collective-permute-start.17 = (bf16[96,3200]{1,0:T(8,128)(2,1)}, bf16[96,3200]{1,0:T(8,128)(2,1)S(1)}, u32[]{:S(2)}, u32[]{:S(2)}) collective-permute-start(bf16[96,3200]{1,0:T(8,128)(2,1)} %collective-permute-done.11.refs_3_), channel_id=1, source_target_pairs={{0,1},{1,0},{2,3},{3,2},{4,5},{5,4},{6,7},{7,6},{8,9},{9,8},{10,11... | collective-permute-start | bytes 1843208 | tf_op jit(solution)/shard_map/ppermute | solution.py:697
  63.4 16.0 %collective-permute-start.18 = (bf16[384,768]{1,0:T(8,128)(2,1)S(1)}, bf16[384,768]{1,0:T(8,128)(2,1)S(1)}, u32[]{:S(2)}, u32[]{:S(2)}) collective-permute-start(bf16[384,768]{1,0:T(8,128)(2,1)S(1)} %copy-done.26), channel_id=1, source_target_pairs={{0,1},{1,0},{2,3},{3,2},{4,5},{5,4},{6,7},{7,6},{8,9},{9,8},{10,11... | collective-permute-start | bytes 1769480 | tf_op jit(solution)/shard_map/ppermute | solution.py:697
  63.5 12.7 %collective-permute-start.14 = (bf16[96,1536]{1,0:T(8,128)(2,1)}, bf16[96,1536]{1,0:T(8,128)(2,1)S(1)}, u32[]{:S(2)}, u32[]{:S(2)}) collective-permute-start(bf16[96,1536]{1,0:T(8,128)(2,1)} %collective-permute-done.9.refs_8_), channel_id=1, source_target_pairs={{0,4},{4,0},{8,12},{12,8},{16,20},{20,16},{24,28},{28,24},{1,5},{5... | collective-permute-start | bytes 884744 | tf_op jit(solution)/shard_map/ppermute | solution.py:697
  64.0 15.4 %collective-permute-start.15 = (bf16[192,768]{1,0:T(8,128)(2,1)}, bf16[192,768]{1,0:T(8,128)(2,1)S(1)}, u32[]{:S(2)}, u32[]{:S(2)}) collective-permute-start(bf16[192,768]{1,0:T(8,128)(2,1)} %collective-permute-done.12.refs_14_), channel_id=1, source_target_pairs={{0,4},{4,0},{8,12},{12,8},{16,20},{20,16},{24,28},{28,24},{1,5},{5... | collective-permute-start | bytes 884744 | tf_op jit(solution)/shard_map/ppermute | solution.py:697
  65.5 13.9 %collective-permute-start.16 = (bf16[192,768]{1,0:T(8,128)(2,1)}, bf16[192,768]{1,0:T(8,128)(2,1)S(1)}, u32[]{:S(2)}, u32[]{:S(2)}) collective-permute-start(bf16[192,768]{1,0:T(8,128)(2,1)} %collective-permute-done.12.refs_14_), channel_id=1, source_target_pairs={{0,1},{1,0},{2,3},{3,2},{4,5},{5,4},{6,7},{7,6},{8,9},{9,8},{10,11... | collective-permute-start | bytes 884744 | tf_op jit(solution)/shard_map/ppermute | solution.py:697
  79.4 3.3 collective-permute-start.19
  79.5 3.5 collective-permute-start.20
  80.7 35.7 %collective-permute-start.21 = (bf16[192,1536]{1,0:T(8,128)(2,1)}, bf16[192,1536]{1,0:T(8,128)(2,1)S(1)}, u32[]{:S(2)}, u32[]{:S(2)}) collective-permute-start(bf16[192,1536]{1,0:T(8,128)(2,1)} %refs_0_.1), channel_id=1, source_target_pairs={{0,2},{1,3},{2,0},{3,1},{4,6},{5,7},{6,4},{7,5},{8,10},{9,11},{10,... | collective-permute-start | bytes 1769480 | tf_op jit(solution)/shard_map/ppermute | solution.py:697
  81.6 34.8 %collective-permute-start.23 = (bf16[192,1536]{1,0:T(8,128)(2,1)}, bf16[192,1536]{1,0:T(8,128)(2,1)}, u32[]{:S(2)}, u32[]{:S(2)}) collective-permute-start(bf16[192,1536]{1,0:T(8,128)(2,1)} %refs_0_.1), channel_id=1, source_target_pairs={{0,1},{1,0},{2,3},{3,2},{4,5},{5,4},{6,7},{7,6},{8,9},{9,8},{10,11... | collective-permute-start | bytes 1769480 | tf_op jit(solution)/shard_map/ppermute | solution.py:697
  81.6 34.8 %collective-permute-start.22 = (bf16[384,768]{1,0:T(8,128)(2,1)}, bf16[384,768]{1,0:T(8,128)(2,1)}, u32[]{:S(2)}, u32[]{:S(2)}) collective-permute-start(bf16[384,768]{1,0:T(8,128)(2,1)} %refs_4_), channel_id=1, source_target_pairs={{0,2},{1,3},{2,0},{3,1},{4,6},{5,7},{6,4},{7,5},{8,10},{9,11},{10,... | collective-permute-start | bytes 1769480 | tf_op jit(solution)/shard_map/ppermute | solution.py:697
  82.7 33.7 %collective-permute-start.24 = (bf16[384,768]{1,0:T(8,128)(2,1)}, bf16[384,768]{1,0:T(8,128)(2,1)}, u32[]{:S(2)}, u32[]{:S(2)}) collective-permute-start(bf16[384,768]{1,0:T(8,128)(2,1)} %refs_4_), channel_id=1, source_target_pairs={{0,1},{1,0},{2,3},{3,2},{4,5},{5,4},{6,7},{7,6},{8,9},{9,8},{10,11... | collective-permute-start | bytes 1769480 | tf_op jit(solution)/shard_map/ppermute | solution.py:697
  116.4 7.3 %collective-permute-start.25 = (bf16[192,1536]{1,0:T(8,128)(2,1)S(1)}, bf16[192,1536]{1,0:T(8,128)(2,1)S(1)}, u32[]{:S(2)}, u32[]{:S(2)}) collective-permute-start(bf16[192,1536]{1,0:T(8,128)(2,1)S(1)} %collective-permute-done.21.refs_2_), channel_id=1, source_target_pairs={{0,1},{1,0},{2,3},{3,2},{4,5},{5,4},{6,7},{7,6},{8,9},{9,8},{10,11... | collective-permute-start | bytes 1769480 | tf_op jit(solution)/shard_map/ppermute | solution.py:697
  116.8 6.9 %collective-permute-start.26 = (bf16[384,768]{1,0:T(8,128)(2,1)}, bf16[384,768]{1,0:T(8,128)(2,1)}, u32[]{:S(2)}, u32[]{:S(2)}) collective-permute-start(bf16[384,768]{1,0:T(8,128)(2,1)} %collective-permute-done.22.refs_6_), channel_id=1, source_target_pairs={{0,1},{1,0},{2,3},{3,2},{4,5},{5,4},{6,7},{7,6},{8,9},{9,8},{10,11... | collective-permute-start | bytes 1769480 | tf_op jit(solution)/shard_map/ppermute | solution.py:697
  176.2 20.7 %collective-permute-start.28 = (bf16[2,2,2,2,24,1536]{5,4,3,2,1,0:T(8,128)(2,1)S(1)}, bf16[2,2,2,2,24,1536]{5,4,3,2,1,0:T(8,128)(2,1)S(1)}, u32[]{:S(2)}, u32[]{:S(2)}) collective-permute-start(bf16[2,2,2,2,24,1536]{5,4,3,2,1,0:T(8,128)(2,1)S(1)} %fusion.13), channel_id=1, source_target_pairs={{0,1},{1,0},{2,3},{3,2},{4,5},{5,4},{6,7},{7,6},{8,9},{9,8},{10,11... | collective-permute-start | bytes 3538952 | tf_op jit(solution)/shard_map/ppermute | solution.py:697
  181.8 15.1 %collective-permute-start.27 = (bf16[2,2,2,2,48,768]{5,4,3,2,1,0:T(8,128)(2,1)S(1)}, bf16[2,2,2,2,48,768]{5,4,3,2,1,0:T(8,128)(2,1)S(1)}, u32[]{:S(2)}, u32[]{:S(2)}) collective-permute-start(bf16[2,2,2,2,48,768]{5,4,3,2,1,0:T(8,128)(2,1)S(1)} %fusion.7), channel_id=1, source_target_pairs={{0,1},{1,0},{2,3},{3,2},{4,5},{5,4},{6,7},{7,6},{8,9},{9,8},{10,11... | collective-permute-start | bytes 3538952 | tf_op jit(solution)/shard_map/ppermute | solution.py:697
  187.4 9.6 %collective-permute-start.31 = (bf16[2,2,2,2,24,1536]{5,4,3,2,1,0:T(8,128)(2,1)S(1)}, bf16[2,2,2,2,24,1536]{5,4,3,2,1,0:T(8,128)(2,1)S(1)}, u32[]{:S(2)}, u32[]{:S(2)}) collective-permute-start(bf16[2,2,2,2,24,1536]{5,4,3,2,1,0:T(8,128)(2,1)S(1)} %fusion.9), channel_id=1, source_target_pairs={{0,1},{1,0},{2,3},{3,2},{4,5},{5,4},{6,7},{7,6},{8,9},{9,8},{10,11... | collective-permute-start | bytes 3538952 | tf_op jit(solution)/shard_map/ppermute | solution.py:697
  196.2 2.9 collective-permute-start.30
  200.0 48.1 %collective-permute-start.32 = (bf16[2,2,2,96,768]{4,3,2,1,0:T(8,128)(2,1)S(1)}, bf16[2,2,2,96,768]{4,3,2,1,0:T(8,128)(2,1)}, u32[]{:S(2)}, u32[]{:S(2)}) collective-permute-start(bf16[2,2,2,96,768]{4,3,2,1,0:T(8,128)(2,1)S(1)} %fusion.10), channel_id=1, source_target_pairs={{0,4},{4,0},{8,12},{12,8},{16,20},{20,16},{24,28},{28,24},{1,5},{5... | collective-permute-start | bytes 3538952 | tf_op jit(solution)/shard_map/ppermute | solution.py:697
  206.5 41.6 %collective-permute-start.29 = (bf16[2,2,2,96,768]{4,3,2,1,0:T(8,128)(2,1)}, bf16[2,2,2,96,768]{4,3,2,1,0:T(8,128)(2,1)}, u32[]{:S(2)}, u32[]{:S(2)}) collective-permute-start(bf16[2,2,2,96,768]{4,3,2,1,0:T(8,128)(2,1)} %fusion.8), channel_id=1, source_target_pairs={{0,2},{1,3},{2,0},{3,1},{4,6},{5,7},{6,4},{7,5},{8,10},{9,11},{10,... | collective-permute-start | bytes 3538952 | tf_op jit(solution)/shard_map/ppermute | solution.py:697
  250.7 15.3 %collective-permute-start.34 = (bf16[2,2,96,768]{3,2,1,0:T(8,128)(2,1)S(1)}, bf16[2,2,96,768]{3,2,1,0:T(8,128)(2,1)S(1)}, u32[]{:S(2)}, u32[]{:S(2)}) collective-permute-start(bf16[2,2,96,768]{3,2,1,0:T(8,128)(2,1)S(1)} %fusion.26), channel_id=1, source_target_pairs={{0,2},{1,3},{2,0},{3,1},{4,6},{5,7},{6,4},{7,5},{8,10},{9,11},{10,... | collective-permute-start | bytes 1769480 | tf_op jit(solution)/shard_map/ppermute | solution.py:697
  253.5 15.0 %collective-permute-start.33 = (bf16[2,2,96,768]{3,2,1,0:T(8,128)(2,1)S(1)}, bf16[2,2,96,768]{3,2,1,0:T(8,128)(2,1)S(1)}, u32[]{:S(2)}, u32[]{:S(2)}) collective-permute-start(bf16[2,2,96,768]{3,2,1,0:T(8,128)(2,1)S(1)} %fusion.25), channel_id=1, source_target_pairs={{0,4},{4,0},{8,12},{12,8},{16,20},{20,16},{24,28},{28,24},{1,5},{5... | collective-permute-start | bytes 1769480 | tf_op jit(solution)/shard_map/ppermute | solution.py:697
  264.1 20.3 %collective-permute-start.36 = (bf16[2,2,2,2,24,1664]{5,4,3,2,1,0:T(8,128)(2,1)}, bf16[2,2,2,2,24,1664]{5,4,3,2,1,0:T(8,128)(2,1)}, u32[]{:S(2)}, u32[]{:S(2)}) collective-permute-start(bf16[2,2,2,2,24,1664]{5,4,3,2,1,0:T(8,128)(2,1)} %fusion.6), channel_id=1, source_target_pairs={{0,1},{1,0},{2,3},{3,2},{4,5},{5,4},{6,7},{7,6},{8,9},{9,8},{10,11... | collective-permute-start | bytes 3833864 | tf_op jit(solution)/shard_map/ppermute | solution.py:697
  268.8 15.5 %collective-permute-start.35 = (bf16[2,192,768]{2,1,0:T(8,128)(2,1)S(1)}, bf16[2,192,768]{2,1,0:T(8,128)(2,1)S(1)}, u32[]{:S(2)}, u32[]{:S(2)}) collective-permute-start(bf16[2,192,768]{2,1,0:T(8,128)(2,1)S(1)} %fusion.28), channel_id=1, source_target_pairs={{0,8},{4,12},{8,0},{12,4},{16,24},{20,28},{24,16},{28,20},{1,9},{5... | collective-permute-start | bytes 1769480 | tf_op jit(solution)/shard_map/ppermute | solution.py:697
  285.5 15.6 %collective-permute-start.38 = (bf16[192,768]{1,0:T(8,128)(2,1)S(1)}, bf16[192,768]{1,0:T(8,128)(2,1)S(1)}, u32[]{:S(2)}, u32[]{:S(2)}) collective-permute-start(bf16[192,768]{1,0:T(8,128)(2,1)S(1)} %fusion.33), channel_id=1, source_target_pairs={{0,16},{4,20},{8,24},{12,28},{16,0},{20,4},{24,8},{28,12},{1,17},{... | collective-permute-start | bytes 884744 | tf_op jit(solution)/shard_map/ppermute | solution.py:697
  296.5 4.7 %collective-permute-start.37 = (f32[2,16,768]{2,1,0:T(8,128)S(1)}, f32[2,16,768]{2,1,0:T(8,128)S(1)}, u32[]{:S(2)}, u32[]{:S(2)}) collective-permute-start(f32[2,16,768]{2,1,0:T(8,128)S(1)} %copy-done.28), channel_id=1, source_target_pairs={{0,4},{4,0},{8,12},{12,8},{16,20},{20,16},{24,28},{28,24},{1,5},{5... | collective-permute-start | bytes 294920 | tf_op jit(solution)/shard_map/ppermute | solution.py:697
  297.2 8.7 %collective-permute-start.40 = (bf16[2,2,2,2,24,1536]{5,4,2,1,0,3:T(8,128)(2,1)S(1)}, bf16[2,2,2,2,24,1536]{5,4,2,1,0,3:T(8,128)(2,1)S(1)}, u32[]{:S(2)}, u32[]{:S(2)}) collective-permute-start(bf16[2,2,2,2,24,1536]{5,4,2,1,0,3:T(8,128)(2,1)S(1)} %fusion.12), channel_id=1, source_target_pairs={{0,1},{1,0},{2,3},{3,2},{4,5},{5,4},{6,7},{7,6},{8,9},{9,8},{10,11... | collective-permute-start | bytes 3538952 | tf_op jit(solution)/shard_map/ppermute | solution.py:697
  301.2 4.7 %collective-permute-start.39 = (f32[2,16,768]{2,1,0:T(8,128)S(1)}, f32[2,16,768]{2,1,0:T(8,128)S(1)}, u32[]{:S(2)}, u32[]{:S(2)}) collective-permute-start(f32[2,16,768]{2,1,0:T(8,128)S(1)} %add_select_fusion.5), channel_id=1, source_target_pairs={{0,8},{4,12},{8,0},{12,4},{16,24},{20,28},{24,16},{28,20},{1,9},{5... | collective-permute-start | bytes 294920 | tf_op jit(solution)/shard_map/ppermute | solution.py:697
  301.4 21.8 %collective-permute-start.42 = (bf16[2,2,2,24,1664]{4,3,2,1,0:T(8,128)(2,1)S(1)}, bf16[2,2,2,24,1664]{4,3,2,1,0:T(8,128)(2,1)}, u32[]{:S(2)}, u32[]{:S(2)}) collective-permute-start(bf16[2,2,2,24,1664]{4,3,2,1,0:T(8,128)(2,1)S(1)} %fusion.19), channel_id=1, source_target_pairs={{0,2},{1,3},{2,0},{3,1},{4,6},{5,7},{6,4},{7,5},{8,10},{9,11},{10,... | collective-permute-start | bytes 1916936 | tf_op jit(solution)/shard_map/ppermute | solution.py:697
  305.9 6.3 %collective-permute-start.41 = (f32[2,16,768]{2,1,0:T(8,128)S(1)}, f32[2,16,768]{2,1,0:T(8,128)S(1)}, u32[]{:S(2)}, u32[]{:S(2)}) collective-permute-start(f32[2,16,768]{2,1,0:T(8,128)S(1)} %add_select_fusion.4), channel_id=1, source_target_pairs={{0,16},{4,20},{8,24},{12,28},{16,0},{20,4},{24,8},{28,12},{1,17},{... | collective-permute-start | bytes 294920 | tf_op jit(solution)/shard_map/ppermute | solution.py:697
  309.8 29.7 %collective-permute-start.44 = (bf16[2,2,2,24,1536]{4,3,2,1,0:T(8,128)(2,1)}, bf16[2,2,2,24,1536]{4,3,2,1,0:T(8,128)(2,1)}, u32[]{:S(2)}, u32[]{:S(2)}) collective-permute-start(bf16[2,2,2,24,1536]{4,3,2,1,0:T(8,128)(2,1)} %fusion.27), channel_id=1, source_target_pairs={{0,4},{4,0},{8,12},{12,8},{16,20},{20,16},{24,28},{28,24},{1,5},{5... | collective-permute-start | bytes 1769480 | tf_op jit(solution)/shard_map/ppermute | solution.py:697
  325.6 13.9 %collective-permute-start.43 = (bf16[2,2,24,1664]{3,2,1,0:T(8,128)(2,1)S(1)}, bf16[2,2,24,1664]{3,2,1,0:T(8,128)(2,1)S(1)}, u32[]{:S(2)}, u32[]{:S(2)}) collective-permute-start(bf16[2,2,24,1664]{3,2,1,0:T(8,128)(2,1)S(1)} %fusion.30), channel_id=1, source_target_pairs={{0,4},{4,0},{8,12},{12,8},{16,20},{20,16},{24,28},{28,24},{1,5},{5... | collective-permute-start | bytes 958472 | tf_op jit(solution)/shard_map/ppermute | solution.py:697
  326.8 12.7 %collective-permute-start.45 = (bf16[1,192,768]{2,1,0:T(8,128)(2,1)S(1)}, bf16[1,192,768]{2,1,0:T(8,128)(2,1)S(1)}, u32[]{:S(2)}, u32[]{:S(2)}) collective-permute-start(bf16[1,192,768]{2,1,0:T(8,128)(2,1)S(1)} %fusion.35), channel_id=1, source_target_pairs={{0,16},{4,20},{8,24},{12,28},{16,0},{20,4},{24,8},{28,12},{1,17},{... | collective-permute-start | bytes 884744 | tf_op jit(solution)/shard_map/ppermute | solution.py:697
  340.5 14.6 %collective-permute-start.47 = (bf16[2,192,768]{2,1,0:T(8,128)(2,1)}, bf16[2,192,768]{2,1,0:T(8,128)(2,1)}, u32[]{:S(2)}, u32[]{:S(2)}) collective-permute-start(bf16[2,192,768]{2,1,0:T(8,128)(2,1)} %pad_maximum_fusion.8), channel_id=1, source_target_pairs={{0,8},{4,12},{8,0},{12,4},{16,24},{20,28},{24,16},{28,20},{1,9},{5... | collective-permute-start | bytes 1769480 | tf_op jit(solution)/shard_map/ppermute | solution.py:697
  342.4 12.1 %collective-permute-start.46 = (bf16[2,2,24,1536]{3,2,1,0:T(8,128)(2,1)}, bf16[2,2,24,1536]{3,2,1,0:T(8,128)(2,1)}, u32[]{:S(2)}, u32[]{:S(2)}) collective-permute-start(bf16[2,2,24,1536]{3,2,1,0:T(8,128)(2,1)} %fusion.34), channel_id=1, source_target_pairs={{0,2},{1,3},{2,0},{3,1},{4,6},{5,7},{6,4},{7,5},{8,10},{9,11},{10,... | collective-permute-start | bytes 884744 | tf_op jit(solution)/shard_map/ppermute | solution.py:697
  356.2 11.7 %collective-permute-start.48 = (bf16[2,24,3200]{2,1,0:T(8,128)(2,1)S(1)}, bf16[2,24,3200]{2,1,0:T(8,128)(2,1)S(1)}, u32[]{:S(2)}, u32[]{:S(2)}) collective-permute-start(bf16[2,24,3200]{2,1,0:T(8,128)(2,1)S(1)} %fusion.31), channel_id=1, source_target_pairs={{0,8},{4,12},{8,0},{12,4},{16,24},{20,28},{24,16},{28,20},{1,9},{5... | collective-permute-start | bytes 921608 | tf_op jit(solution)/shard_map/ppermute | solution.py:697
  367.9 14.5 %collective-permute-start.49 = (bf16[24,3200]{1,0:T(8,128)(2,1)S(1)}, bf16[24,3200]{1,0:T(8,128)(2,1)}, u32[]{:S(2)}, u32[]{:S(2)}) collective-permute-start(bf16[24,3200]{1,0:T(8,128)(2,1)S(1)} %fusion.36), channel_id=1, source_target_pairs={{0,16},{4,20},{8,24},{12,28},{16,0},{20,4},{24,8},{28,12},{1,17},{... | collective-permute-start | bytes 460808 | tf_op jit(solution)/shard_map/ppermute | solution.py:697
  371.0 26.5 %collective-permute-start.51 = (bf16[4,192,768]{2,1,0:T(8,128)(2,1)}, bf16[4,192,768]{2,1,0:T(8,128)(2,1)S(1)}, u32[]{:S(2)}, u32[]{:S(2)}) collective-permute-start(bf16[4,192,768]{2,1,0:T(8,128)(2,1)} %pad_maximum_fusion.5), channel_id=1, source_target_pairs={{0,4},{4,0},{8,12},{12,8},{16,20},{20,16},{24,28},{28,24},{1,5},{5... | collective-permute-start | bytes 3538952 | tf_op jit(solution)/shard_map/ppermute | solution.py:697
  383.4 12.4 %collective-permute-start.50 = (bf16[1,24,3200]{2,1,0:T(8,128)(2,1)S(1)}, bf16[1,24,3200]{2,1,0:T(8,128)(2,1)S(1)}, u32[]{:S(2)}, u32[]{:S(2)}) collective-permute-start(bf16[1,24,3200]{2,1,0:T(8,128)(2,1)S(1)} %fusion.37), channel_id=1, source_target_pairs={{0,16},{4,20},{8,24},{12,28},{16,0},{20,4},{24,8},{28,12},{1,17},{... | collective-permute-start | bytes 460808 | tf_op jit(solution)/shard_map/ppermute | solution.py:697
  398.3 11.2 %collective-permute-start.55 = (bf16[2,24,3200]{2,1,0:T(8,128)(2,1)}, bf16[2,24,3200]{2,1,0:T(8,128)(2,1)}, u32[]{:S(2)}, u32[]{:S(2)}) collective-permute-start(bf16[2,24,3200]{2,1,0:T(8,128)(2,1)} %pad_maximum_fusion.9), channel_id=1, source_target_pairs={{0,8},{4,12},{8,0},{12,4},{16,24},{20,28},{24,16},{28,20},{1,9},{5... | collective-permute-start | bytes 921608 | tf_op jit(solution)/shard_map/ppermute | solution.py:697
  400.6 5.5 %collective-permute-start.52 = (f32[136,192]{1,0:T(8,128)S(1)}, f32[136,192]{1,0:T(8,128)S(1)}, u32[]{:S(2)}, u32[]{:S(2)}) collective-permute-start(f32[136,192]{1,0:T(8,128)S(1)} %bitcast.280), channel_id=1, source_target_pairs={{0,1},{1,0},{2,3},{3,2},{4,5},{5,4},{6,7},{7,6},{8,9},{9,8},{10,11... | collective-permute-start | bytes 313352 | tf_op jit(solution)/shard_map/ppermute | solution.py:697
  400.7 6.5 %collective-permute-start.53 = (f32[136,192]{1,0:T(8,128)S(1)}, f32[136,192]{1,0:T(8,128)S(1)}, u32[]{:S(2)}, u32[]{:S(2)}) collective-permute-start(f32[136,192]{1,0:T(8,128)S(1)} %bitcast.281), channel_id=1, source_target_pairs={{0,2},{1,3},{2,0},{3,1},{4,6},{5,7},{6,4},{7,5},{8,10},{9,11},{10,... | collective-permute-start | bytes 313352 | tf_op jit(solution)/shard_map/ppermute | solution.py:697
  402.1 7.3 %collective-permute-start.54 = (f32[136,192]{1,0:T(8,128)S(1)}, f32[136,192]{1,0:T(8,128)S(1)}, u32[]{:S(2)}, u32[]{:S(2)}) collective-permute-start(f32[136,192]{1,0:T(8,128)S(1)} %bitcast.282), channel_id=1, source_target_pairs={{0,3},{1,2},{2,1},{3,0},{4,7},{5,6},{6,5},{7,4},{8,11},{9,10},{10,... | collective-permute-start | bytes 313352 | tf_op jit(solution)/shard_map/ppermute | solution.py:697
  410.6 21.5 %collective-permute-start.59 = (bf16[4,24,3200]{2,1,0:T(8,128)(2,1)S(1)}, bf16[4,24,3200]{2,1,0:T(8,128)(2,1)S(1)}, u32[]{:S(2)}, u32[]{:S(2)}) collective-permute-start(bf16[4,24,3200]{2,1,0:T(8,128)(2,1)S(1)} %pad_maximum_fusion.7), channel_id=1, source_target_pairs={{0,4},{4,0},{8,12},{12,8},{16,20},{20,16},{24,28},{28,24},{1,5},{5... | collective-permute-start | bytes 1843208 | tf_op jit(solution)/shard_map/ppermute | solution.py:697
  412.4 9.4 %collective-permute-start.56 = (f32[136,192]{1,0:T(8,128)S(1)}, f32[136,192]{1,0:T(8,128)S(1)}, u32[]{:S(2)}, u32[]{:S(2)}) collective-permute-start(f32[136,192]{1,0:T(8,128)S(1)} %fusion.43), channel_id=1, source_target_pairs={{0,16},{4,20},{8,24},{12,28},{16,0},{20,4},{24,8},{28,12},{1,17},{... | collective-permute-start | bytes 313352 | tf_op jit(solution)/shard_map/ppermute | solution.py:697
  421.8 5.1 %collective-permute-start.57 = (f32[136,192]{1,0:T(8,128)S(1)}, f32[136,192]{1,0:T(8,128)S(1)}, u32[]{:S(2)}, u32[]{:S(2)}) collective-permute-start(f32[136,192]{1,0:T(8,128)S(1)} %add.307), channel_id=1, source_target_pairs={{0,8},{4,12},{8,0},{12,4},{16,24},{20,28},{24,16},{28,20},{1,9},{5... | collective-permute-start | bytes 313352 | tf_op jit(solution)/shard_map/ppermute | solution.py:697
  427.0 5.1 %collective-permute-start.58 = (f32[136,192]{1,0:T(8,128)S(1)}, f32[136,192]{1,0:T(8,128)S(1)}, u32[]{:S(2)}, u32[]{:S(2)}) collective-permute-start(f32[136,192]{1,0:T(8,128)S(1)} %add.308), channel_id=1, source_target_pairs={{0,4},{4,0},{8,12},{12,8},{16,20},{20,16},{24,28},{28,24},{1,5},{5... | collective-permute-start | bytes 313352 | tf_op jit(solution)/shard_map/ppermute | solution.py:697
  (43 other events, 248.3 us)
where the time goes:
time: 452 us; the launch traced here: 443 us
  Pallas kernels  224 us (50%)
  local copies, waits for them, and re-layouts  49.7 us (11%)
  starting transfers between devices  48.1 us (11%)
  matrix products  43.7 us (10%)
  waiting for transfers between devices  42.6 us (9%)
  other arithmetic  33 us (7%)
    pallas_call x6, Pallas kernels, ema_backward(): pl.pallas_call(functools.partial(bwd_kernel, H, L // CH), grid=(count, G)...  60.4 us
    ppermute x60, starting transfers between devices, exchange(): lax.ppermute(value, axis, [(k, k ^ step) for k in range(lax.axis_size(axi...  48.1 us
    dot_general x6, matrix products, dot_rows(): jnp.einsum('ri,rj->ij', left_op, right_op, preferred_element_type=jnp.flo...  43.7 us
    pallas_call x1, Pallas kernels, ffn_both(): pl.pallas_call(functools.partial(ffn_kernel, R, (D, FF)), grid=(T // R,),...  42.6 us
    ppermute x60, waiting for transfers between devices, exchange(): lax.ppermute(value, axis, [(k, k ^ step) for k in range(lax.axis_size(axi...  42.6 us
    pallas_call x1, Pallas kernels, mix_backward(): pl.pallas_call(functools.partial(mix_bwd_kernel, R, (D, Z, V)), grid=(T /...  40.6 us
    pallas_call x1, Pallas kernels, mix_forward(): pl.pallas_call(functools.partial(mix_fwd_kernel, R, (D, Z, V)), grid=(T /...  32.6 us
    pallas_call x2, Pallas kernels, ema_forward(): pl.pallas_call(functools.partial(fwd_kernel, H, L // CH), grid=(count, G)...  21.3 us
  transfers between devices with their start and end apart: 60, of which 18 were waited for; matrix products, arithmetic and copies ran while one was open for 18% of the time, Pallas kernels for 41%

commit v1 on v0

--- a/solution.py
+++ b/solution.py
@@ -10,7 +10,7 @@
 BLOCK = 128
 LANES = 128
 CH = 8
-PAD = 8
+PAD = 1
 CHUNK = 768
 STRIP = 32
 EPSILON = 1e-05
@@ -46,20 +46,30 @@
 def collect(scr, T):
     return jnp.concatenate([scr[k*(T+PAD):k*(T+PAD)+T, :] for k in range(CH)], axis=0)
 
-def ends_kernel(H, T, x_ref, q_ref, e_ref, s_ref, scr):
-    spread(scr, x_ref[0].astype(F32), T)
+def ends_kernel(G, H, T, x_ref, q_ref, e_ref, s_ref, *scrs):
+    for g in range(G):
+        spread(scrs[g], x_ref[g].astype(F32), T)
+    chunk_ends(G, H, T, q_ref, e_ref, s_ref, scrs, False)
+
+
+def chunk_ends(G, H, T, q_ref, e_ref, s_ref, scrs, reverse):
     q = [jnp.broadcast_to(q_ref[h:h+1, :], (CH, LANES)) for h in range(H)]
-    def step(s, st):
-        xs = rows_of(scr, s, T)
-        return tuple(q[h]*st[h] + xs for h in range(H))
-    st = lax.fori_loop(0, T, step, tuple(jnp.zeros((CH,LANES),F32) for _ in range(H)), unroll=8)
-    for h in range(H):
-        e_ref[0, h*CH:(h+1)*CH, :] = st[h]
+
+    def step(s, states):
+        rows = [rows_of(scr, T - 1 - s if reverse else s, T) for scr in scrs]
+        return tuple(q[n % H] * states[n] + rows[n // H] for n in range(G * H))
+
+    zero = jnp.zeros((CH, LANES), F32)
+    states = lax.fori_loop(0, T, step, (zero,) * (G * H), unroll=min(T, 16))
+    for n in range(G * H):
+        e_ref[n // H, n % H * CH : (n % H + 1) * CH, :] = states[n]
     qT = power(q_ref[...], T)
-    c = jnp.zeros((H,LANES),F32)
-    for k in range(CH):
-        c = qT*c + e_ref[0, pl.ds(k,H,stride=CH), :]
-    s_ref[0] = c
+    for g in range(G):
+        c = jnp.zeros((H, LANES), F32)
+        for k in reversed(range(CH)) if reverse else range(CH):
+            c = qT * c + e_ref[g, pl.ds(k, H, stride=CH), :]
+        s_ref[g] = c
+
 
 def fwd_kernel(H, T, x_ref, q_ref, w_ref, om_ref, e_ref, c_ref, *refs):
     xp_ref, p_ref, f_ref, scr, cs, ps = refs[-6:]
@@ -80,31 +90,22 @@
             terms = [terms[i]+terms[i+1] for i in range(0,len(terms)-1,2)] + ([terms[-1]] if len(terms)%2 else [])
         ps[pl.ds(s, CH, stride=T+PAD), :] = terms[0] + om*xs
         return st
-    st = lax.fori_loop(0, T, step, tuple(cs[h*CH:(h+1)*CH, :] for h in range(H)), unroll=8)
+    st = lax.fori_loop(0, T, step, tuple(cs[h*CH:(h+1)*CH, :] for h in range(H)), unroll=min(T, 32))
     for h in range(H):
         f_ref[0, h*CH:(h+1)*CH, :] = st[h]
     p = collect(ps, T)
     p_ref[0] = p
     xp_ref[0] = (p*jax.nn.sigmoid(p)).astype(xp_ref.dtype)
 
-def bends_kernel(H, T, dxp_ref, p_ref, q_ref, d_ref, e_ref, s_ref, ds):
-    p = p_ref[0]
-    sg = jax.nn.sigmoid(p)
-    d = dxp_ref[0].astype(F32) * (sg*(1.0+p*(1.0-sg)))
-    d_ref[0] = d
-    spread(ds, d, T)
-    q = [jnp.broadcast_to(q_ref[h:h+1, :], (CH, LANES)) for h in range(H)]
-    def step(s, st):
-        xs = rows_of(ds, T-1-s, T)
-        return tuple(q[h]*st[h] + xs for h in range(H))
-    st = lax.fori_loop(0, T, step, tuple(jnp.zeros((CH,LANES),F32) for _ in range(H)), unroll=8)
-    for h in range(H):
-        e_ref[0, h*CH:(h+1)*CH, :] = st[h]
-    qT = power(q_ref[...], T)
-    c = jnp.zeros((H,LANES),F32)
-    for k in reversed(range(CH)):
-        c = qT*c + e_ref[0, pl.ds(k,H,stride=CH), :]
-    s_ref[0] = c
+def bends_kernel(G, H, T, dxp_ref, p_ref, q_ref, d_ref, e_ref, s_ref, *scrs):
+    for g in range(G):
+        p = p_ref[g]
+        sg = jax.nn.sigmoid(p)
+        d = dxp_ref[g].astype(F32) * (sg*(1.0+p*(1.0-sg)))
+        d_ref[g] = d
+        spread(scrs[g], d, T)
+    chunk_ends(G, H, T, q_ref, e_ref, s_ref, scrs, True)
+
 
 def bwd_kernel(H, T, d_ref, x_ref, q_ref, qi_ref, w_ref, om_ref, f_ref, e_ref, c_ref, t_ref, k_ref, *refs):
     dx_ref, out_ref, s1_ref, s3_ref, go_ref, scr, cs, dx, ds = refs[-9:]
@@ -150,7 +151,7 @@
                 dx[at, :] = dx[at, :] + terms[0]
             return l, st, a1, a3
         init = (tuple(cs[h*CH:(h+1)*CH,:] for h in hs), tuple(f_ref[0,h*CH:(h+1)*CH,:] for h in hs), (zero,)*HH, (zero,)*HH)
-        l, st, a1, a3 = lax.fori_loop(0, T, step, init, unroll=4)
+        l, st, a1, a3 = lax.fori_loop(0, T, step, init, unroll=min(T, 16))
         for i,h in enumerate(hs):
             s1_ref[h:h+1,:] += jnp.sum(a1[i],axis=0,keepdims=True)
             s3_ref[h:h+1,:] += jnp.sum(a3[i],axis=0,keepdims=True)
@@ -175,17 +176,25 @@
     return blk, par, one, st, car
 
 
+def all_specs(G, L, H):
+    blk = pl.BlockSpec((G, L, LANES), lambda c: (0, 0, c))
+    par = pl.BlockSpec((H, LANES), lambda c: (0, c))
+    st = pl.BlockSpec((G, H * CH, LANES), lambda c: (0, 0, c))
+    car = pl.BlockSpec((G, H, LANES), lambda c: (0, 0, c))
+    return blk, par, st, car
+
+
 def ema_ends(x, q):
     G, L, C = x.shape
     H = q.shape[0]
-    blk, par, one, st, car = specs(L, H)
+    blk, par, st, car = all_specs(G, L, H)
     return pl.pallas_call(
-        functools.partial(ends_kernel, H, L // CH),
-        grid=(C // LANES, G),
+        functools.partial(ends_kernel, G, H, L // CH),
+        grid=(C // LANES,),
         in_specs=[blk, par],
         out_specs=[st, car],
         out_shape=[jax.ShapeDtypeStruct((G, H * CH, C), F32), jax.ShapeDtypeStruct((G, H, C), F32)],
-        scratch_shapes=[pltpu.VMEM((L + CH * PAD, LANES), F32)],
+        scratch_shapes=[pltpu.VMEM((L + CH * PAD, LANES), F32)] * G,
         cost_estimate=cost_of(0, 11),
         name="ema_ends",
     )(x, q)
@@ -218,17 +227,17 @@
 def ema_back_ends(dxp, p, q):
     G, L, C = p.shape
     H = q.shape[0]
-    blk, par, one, st, car = specs(L, H)
+    blk, par, st, car = all_specs(G, L, H)
     return pl.pallas_call(
-        functools.partial(bends_kernel, H, L // CH),
-        grid=(C // LANES, G),
+        functools.partial(bends_kernel, G, H, L // CH),
+        grid=(C // LANES,),
         in_specs=[blk, blk, par],
         out_specs=[blk, st, car],
         out_shape=[
             jax.ShapeDtypeStruct((G, L, C), F32), jax.ShapeDtypeStruct((G, H * CH, C), F32),
             jax.ShapeDtypeStruct((G, H, C), F32),
         ],
-        scratch_shapes=[pltpu.VMEM((L + CH * PAD, LANES), F32)],
+        scratch_shapes=[pltpu.VMEM((L + CH * PAD, LANES), F32)] * G,
         cost_estimate=cost_of(0, 15),
         name="ema_back_ends",
     )(dxp, p, q)
@@ -321,10 +330,11 @@
 def mix_fwd_kernel(R, dims, x_ref, xp_ref, bm_ref, bv_ref, qk_ref, rel_ref, *refs):
     D, Z, V = dims
     pieces, refs = refs[:18], refs[18:]
-    u_ref, h_ref, r_ref, v_ref, z_ref, p_ref, m_ref, wm, wv, wo, sem = refs
+    u_ref, h_ref, r_ref, v_ref, z_ref, p_ref, m_ref, xt_ref, wm, wv, wo, sem = refs
     bring(((pieces[:6], wm), (pieces[6:12], wv), (pieces[12:], wo)), sem)
     xp = xp_ref[...]
     x = x_ref[...]
+    xt_ref[...] = xp.T
     z = dot_nn(xp, wm[:, D : D + Z]) + bm_ref[:, D : D + Z]
     z_ref[...] = z
     shared = z * sig(z)
@@ -365,8 +375,8 @@
     return jnp.mean(rows, axis=-1, keepdims=True)
 
 
-def ffn_kernel(R, dims, x_ref, u_ref, h_ref, cot_ref, live_ref, gn_ref, bf_ref, bo_ref, *refs):
-    D, FF = dims
+def ffn_kernel(R, dims, x_ref, u_ref, h_ref, cot_ref, len_ref, gn_ref, bf_ref, bo_ref, *refs):
+    D, FF, L = dims
     pieces, refs = refs[:8], refs[8:]
     (
         o_ref, h1_ref, act_ref, dg_ref, df_ref, dum_ref, dt_ref, sd_ref, sf_ref,
@@ -417,7 +427,10 @@
             center = y2 - mean_of(y2)
             inverse = lax.rsqrt(mean_of(center * center) + EPSILON)
             n2 = center * inverse
-            live = live_ref[at, :]
+            row = pl.program_id(0) * R + at.start
+            place = lax.rem(row, L) + lax.axis_index("seq") * L
+            place = place + lax.broadcasted_iota(jnp.int32, (STRIP, 1), 0)
+            live = (place < len_ref[row // L]).astype(F32)
             o_ref[at, :] = ((n2 * g2 + b2) * live).astype(BF16)
             dn = cot_ref[at, :].astype(F32) * live
             w = dn * g2
@@ -623,9 +636,13 @@
         grid=(T // R,),
         in_specs=[tile(R, D), tile(R, D), fixed(1, E), fixed(1, V), fixed(8, Z), fixed(BLOCK, BLOCK)]
         + any_specs(18),
-        out_specs=[tile(R, D), tile(R, D), tile(R, V), tile(R, V), tile(R, Z), tile(R, BLOCK), tile(R, V)],
+        out_specs=[
+            tile(R, D), tile(R, D), tile(R, V), tile(R, V), tile(R, Z), tile(R, BLOCK), tile(R, V),
+            pl.BlockSpec((D, R), lambda t: (0, t)),
+        ],
         out_shape=[
             shape(T, D), shape(T, D), shape(T, V), shape(T, V), shape(T, Z), shape(T, BLOCK), shape(T, V, BF16),
+            shape(D, T, BF16),
         ],
         scratch_shapes=[
             pltpu.VMEM((D, E), BF16), pltpu.VMEM((D, V), BF16), pltpu.VMEM((V, D), BF16),
@@ -637,13 +654,15 @@
     )(x, xp, bm, bv, qk, rel, *pieces)
 
 
-def ffn_both(R, x, u, h, cot, live, norms, bf, bo, pieces):
+def ffn_both(R, L, x, u, h, cot, lengths, norms, bf, bo, pieces):
     T, D = x.shape
     FF = bf.shape[1]
     return pl.pallas_call(
-        functools.partial(ffn_kernel, R, (D, FF)),
+        functools.partial(ffn_kernel, R, (D, FF, L)),
         grid=(T // R,),
-        in_specs=[tile(R, D), tile(R, D), tile(R, D), tile(R, D), tile(R, 1), fixed(8, D), fixed(1, FF), fixed(1, D)]
+        in_specs=[
+            tile(R, D), tile(R, D), tile(R, D), tile(R, D), pl.BlockSpec(memory_space=pltpu.SMEM),
+            fixed(8, D), fixed(1, FF), fixed(1, D)]
         + any_specs(8),
         out_specs=[
             tile(R, D), tile(R, D), tile(R, FF), tile(R, D), tile(R, FF), tile(R, 2 * D), tile(R, D),
@@ -660,7 +679,7 @@
         compiler_params=pltpu.CompilerParams(vmem_limit_bytes=VMEM_LIMIT),
         cost_estimate=cost_of(2 * T * D * 4 * FF, 50),
         name="ffn_both",
-    )(x, u, h, cot, live, norms, bf, bo, *pieces)
+    )(x, u, h, cot, lengths, norms, bf, bo, *pieces)
 
 
 def mix_backward(R, dum, dt, r, v, z, p, qk, sum_d, sum_f, pieces):
@@ -866,8 +885,8 @@
     ends, slice_end, c_mix, c_value, o_value, o_out = join(ends, slice_end, c_mix, c_value, o_value, o_out)
     x_value, x_out = over_x(own_half(o_value)), over_x(own_half(o_out))
     entry = Carry(slice_end, decay, False)
-    sent, x_mix, chan, flat, rate, damp, inward, keep_later, lengths = join(
-        entry.send(steps[0]), x_mix, chan, flat, rate, damp, inward, keep, lengths
+    sent, x_mix, chan, flat, rate, damp, inward, keep_later = join(
+        entry.send(steps[0]), x_mix, chan, flat, rate, damp, inward, keep
     )
     vectors, start = [], 0
     for part in flat_parts:
@@ -885,14 +904,12 @@
             rate * eta, rate * beta,
         ]
     )
-    position = i * L + jnp.arange(L, dtype=jnp.int32)
-    live = (position[None, :] < lengths.reshape(G)[:, None]).astype(F32).reshape(T, 1)
     entry.add(steps[0], sent)
     y_mix, xc_mix = over_y(x_mix), over_core(x_mix)
     for step in steps[1:]:
         entry.add(step, entry.send(step))
-    state_in, x_value, xc_mix, rel_matrix, norms, bo, qk, inverse, factors, live, bm = join(
-        entry.entry, x_value, xc_mix, rel_matrix, norms, bo, qk, inverse, factors, live, bm
+    state_in, x_value, xc_mix, rel_matrix, norms, bo, qk, inverse, factors, bm = join(
+        entry.entry, x_value, xc_mix, rel_matrix, norms, bo, qk, inverse, factors, bm
     )
     y_value, xc_value = over_y(x_value), over_core(x_value)
     so_far = ema_forward((0, half), (), x3, keep, weight, omega, ends, state_in)
@@ -911,14 +928,14 @@
     c_in, c_fout = over_core(o_in), over_core(o_fout)
     xp = xp.reshape(T, D)
     forward = mix_forward(min(256, T), x, xp, bm, bv, qk, rel_matrix, mix_pieces)
-    (u, h, r, v, z, p, mixed), x_in, x_fout, c_in, c_fout = join(forward, x_in, x_fout, c_in, c_fout)
+    (u, h, r, v, z, p, mixed, xt), x_in, x_fout, c_in, c_fout = join(forward, x_in, x_fout, c_in, c_fout)
     ffn_pieces = (o_in, c_in, x_in, over_core(x_in)) + (o_fout, c_fout, x_fout, over_core(x_fout))
     output, h1, act, dg, df, dum, dt, sum_d, sum_f = ffn_both(
-        R, x, u, h, cotangent.reshape(T, D), live, norms, bf, bo, ffn_pieces
+        R, L, x, u, h, cotangent.reshape(T, D), lengths.reshape(G), norms, bf, bo, ffn_pieces
     )
 
     (sent_1, kept_1), (sent_2, kept_2) = send_core(dot_rows(act, dg)), send_core(dot_rows(h1, df))
-    (sent_3, kept_3), (sent_4, kept_4) = send_core(dot_rows(mixed, dum[:, D:])), send_core(dot_rows(xp, dum))
+    (sent_3, kept_3), (sent_4, kept_4) = send_core(dot_rows(mixed, dum[:, D:])), send_core(dot_nn(xt, dum))
     kept_3, kept_4, sent_1, sent_2 = join(kept_3, kept_4, sent_1, sent_2)
     sum_a = Sum(merge([add_half(sent_1, kept_1), add_half(sent_2, kept_2)], D))
     over_a = sum_a.send(x_step)
@@ -929,7 +946,7 @@
     sum_a.add(over_a)
     sum_b.add(over_b)
     over_a, over_b = sum_a.send(y_step), sum_b.send(x_step)
-    sent_1, kept_1 = send_core(dot_rows(xp, db))
+    sent_1, kept_1 = send_core(dot_nn(xt, db))
     dxp, kept_1, over_a, over_b = join(dxp, kept_1, over_a, over_b)
     sum_a.add(over_a)
     sum_b.add(over_b)
@@ -979,7 +996,7 @@
     so_far = back_part(2, so_far)
     *so_far, over_d, more = join(*so_far, over_d, more)
     sum_d_.add(over_d)
-    block = widen(block, more, order[1])
+    *so_far, block = join(*so_far, widen(block, more, order[1]))
     more = exchange(block, "seq", order[2])
     cols_c = sum_c.value.shape[-1]
     sum_c.value = jnp.concatenate([sum_c.value, sum_d_.value], axis=-1)

time: 452 us -> 442 us (0.978)
  Pallas kernels: 224 us -> 211 us
  waiting for transfers between devices: 42.6 us -> 51 us
  local copies, waits for them, and re-layouts: 49.7 us -> 43.9 us
    dot_general x0 -> x2, matrix products: none -> 14.9 us  [dot_nn(): return jnp.dot(left_op, right_op, preferred_element_type=F32)]
    dot_general x6 -> x4, matrix products: 43.7 us -> 29.9 us  [dot_rows(): jnp.einsum('ri,rj->ij', left_op, right_op, preferred_element_type=jnp.flo...]
    ppermute x60, waiting for transfers between devices: 42.6 us -> 51 us  [exchange(): lax.ppermute(value, axis, [(k, k ^ step) for k in range(lax.axis_size(axi...]
    pallas_call x6, Pallas kernels: 60.4 us -> 53 us  [ema_backward(): pl.pallas_call(functools.partial(bwd_kernel, H, L // CH), grid=(count, G)...]
    dot_general x1 -> x0, local copies, waits for them, and re-layouts: 4.73 us -> none  [dot_rows(): jnp.einsum('ri,rj->ij', left_op, right_op, preferred_element_type=jnp.flo...]
    unnamed x107 -> x104, local copies, waits for them, and re-layouts: 11.1 us -> 11.4 us
  transfers between devices with their start and end apart: 60 -> 60, of which waited for: 18 -> 21; matrix products, arithmetic and copies ran while one was open for 18% -> 17% of each run, Pallas kernels for 41% -> 39%
where the time goes in v1:
time: 442 us; the launch traced here: 434 us
  Pallas kernels  211 us (48%)
  waiting for transfers between devices  51 us (12%)
  starting transfers between devices  49.9 us (11%)
  matrix products  44.7 us (10%)
  local copies, waits for them, and re-layouts  43.9 us (10%)
  other arithmetic  31.3 us (7%)
    pallas_call x6, Pallas kernels, ema_backward(): pl.pallas_call(functools.partial(bwd_kernel, H, L // CH), grid=(count, G)...  53 us
    ppermute x60, waiting for transfers between devices, exchange(): lax.ppermute(value, axis, [(k, k ^ step) for k in range(lax.axis_size(axi...  51 us
    ppermute x60, starting transfers between devices, exchange(): lax.ppermute(value, axis, [(k, k ^ step) for k in range(lax.axis_size(axi...  49.9 us
    pallas_call x1, Pallas kernels, ffn_both(): pl.pallas_call(functools.partial(ffn_kernel, R, (D, FF, L)), grid=(T // R...  43.1 us
    pallas_call x1, Pallas kernels, mix_backward(): pl.pallas_call(functools.partial(mix_bwd_kernel, R, (D, Z, V)), grid=(T /...  40.7 us
    pallas_call x1, Pallas kernels, mix_forward(): pl.pallas_call(functools.partial(mix_fwd_kernel, R, (D, Z, V)), grid=(T /...  32.7 us
    dot_general x4, matrix products, dot_rows(): jnp.einsum('ri,rj->ij', left_op, right_op, preferred_element_type=jnp.flo...  29.9 us
    pallas_call x2, Pallas kernels, ema_forward(): pl.pallas_call(functools.partial(fwd_kernel, H, L // CH), grid=(count, G)...  19.7 us
  transfers between devices with their start and end apart: 60, of which 21 were waited for; matrix products, arithmetic and copies ran while one was open for 17% of the time, Pallas kernels for 39%

profile of v1, /device:TPU:0, one launch (start us, length us, event | category | flops | bytes accessed | tf_op | source)
XLA Modules:
  0.0 434.1 jit_solution(13114898411683393086)
XLA Ops:
  1.4 3.5 concatenate.79
  6.5 3.6 concatenate.80
  10.7 2.6 collective-permute-start.1
  15.1 1.7 collective-permute-start.6
  18.5 9.3 %ema_ends.1 = (f32[2,128,768]{2,1,0:T(8,128)}, f32[2,16,768]{2,1,0:T(8,128)}) custom-call(bf16[2,1024,768]{2,1,0:T(8,128)(2,1)} %bitcast.212, f32[16,768]{1,0:T(8,128)} %get-tuple-element.193.q_ref), custom_call_target="tpu_custom_call" | custom-call | bytes 39600000 | tf_op jit(solution)/shard_map/ema_ends/pallas_call | solution.py:191
  29.3 1.5 collective-permute-start.5
  32.7 1.3 collective-permute-start.12
  34.3 1.5 collective-permute-start.11
  36.3 1.6 collective-permute-start.7
  38.9 2.4 collective-permute-done.7
  41.3 2.7 collective-permute-start.8
  49.9 9.9 %ema_forward.2 = (bf16[2,1024,768]{2,1,0:T(8,128)(2,1)}, f32[2,1024,768]{2,1,0:T(8,128)}, f32[2,128,768]{2,1,0:T(8,128)}) custom-call(bf16[2,1024,768]{2,1,0:T(8,128)(2,1)} %bitcast.213, f32[16,768]{1,0:T(8,128)} %get-tuple-element.193.q_ref, f32[16,768]{1,0:T(8,128)} %copy-done.9, f32[1,768]{1,0:T(1,128)} %slice.330.om_ref, ...), custom_call_target="tpu_custom_call" | custom-call | bytes 32400000 | tf_op jit(solution)/shard_map/ema_forward/pallas_call | solution.py:208
  61.0 1.5 collective-permute-start.15
  62.5 9.9 %ema_forward.3 = (bf16[2,1024,768]{2,1,0:T(8,128)(2,1)}, f32[2,1024,768]{2,1,0:T(8,128)}, f32[2,128,768]{2,1,0:T(8,128)}) custom-call(bf16[2,1024,768]{2,1,0:T(8,128)(2,1)} %bitcast.214, f32[16,768]{1,0:T(8,128)} %get-tuple-element.193.q_ref, f32[16,768]{1,0:T(8,128)} %copy-done.9, ...), custom_call_target="tpu_custom_call", output_to_operand_aliasing={{0}: (6, {}), {1}: (7, {}), {2}: (8, {})} | custom-call | bytes 32400000 | tf_op jit(solution)/shard_map/ema_forward/pallas_call | solution.py:208
  72.4 4.0 collective-permute-done.15.refs_15_
  81.2 32.7 %mix_forward.1 = (f32[2048,768]{1,0:T(8,128)}, f32[2048,768]{1,0:T(8,128)}, f32[2048,1536]{1,0:T(8,128)}, f32[2048,1536]{1,0:T(8,128)}, f32[2048,128]{1,0:T(8,12...) custom-call(bf16[2048,768]{1,0:T(8,128)(2,1)} %bitcast.215, ...), custom_call_target="tpu_custom_call" | custom-call | flops 19730006016 | bytes 118800000 | tf_op jit(solution)/shard_map/mix_forward/pallas_call | solution.py:634
  116.1 1.2 collective-permute-done.26.refs_7_
  117.3 43.1 %ffn_both.1 = (bf16[2048,768]{1,0:T(8,128)(2,1)}, bf16[2048,768]{1,0:T(8,128)(2,1)}, bf16[2048,1536]{1,0:T(8,128)(2,1)}, bf16[2048,768]{1,0:T(8,128)(2,1)}, bf16...) custom-call(bf16[2048,768]{1,0:T(8,128)(2,1)} %bitcast.216, ...), custom_call_target="tpu_custom_call" | custom-call | flops 19327352832 | bytes 180000000 | tf_op jit(solution)/shard_map/ffn_both/pallas_call | solution.py:660
  160.4 8.8 %fusion.87 = f32[768,1536]{1,0:T(8,128)S(1)} fusion(bf16[2048,768]{1,0:T(8,128)(2,1)} %get-tuple-element.262, bf16[2048,1536]{1,0:T(8,128)(2,1)} %get-tuple-element.263), kind=kOutput, calls=%fused_computation.262 | convolution fusion | flops 4831838208 | bytes 14155776 | tf_op jit(solution)/shard_map/ri,rj->ij/dot_general | solution.py:23
  169.8 5.1 %fusion.85 = f32[1536,768]{1,0:T(8,128)S(1)} fusion(bf16[2048,1536]{1,0:T(8,128)(2,1)S(1)} %copy-done.42, bf16[2048,768]{1,0:T(8,128)(2,1)S(1)} %copy-done.43), kind=kOutput, calls=%fused_computation.260 | convolution fusion | flops 4831838208 | bytes 14155776 | tf_op jit(solution)/shard_map/ri,rj->ij/dot_general | solution.py:23
  175.4 7.1 %fusion.86 = f32[768,1536]{1,0:T(8,128)S(1)} fusion(bf16[768,2048]{1,0:T(8,128)(2,1)S(1)} %copy-done.45, bf16[2048,1536]{1,0:T(8,128)(2,1)} %get-tuple-element.245.dum_ref), kind=kOutput, calls=%fused_computation.261 | convolution fusion | flops 4831838208 | bytes 14155776 | tf_op jit(solution)/shard_map/dot_general | solution.py:278
  183.0 8.4 %fusion = f32[1536,768]{1,0:T(8,128)S(1)} fusion(bf16[2048,1536]{1,0:T(8,128)(2,1)} %get-tuple-element.260, bf16[2048,1536]{1,0:T(8,128)(2,1)} %get-tuple-element.245.dum_ref), kind=kOutput, calls=%fused_computation.2 | convolution fusion | flops 4831838208 | bytes 14155776 | tf_op jit(solution)/shard_map/ri,rj->ij/dot_general | solution.py:23
  192.9 1.5 collective-permute-done.30
  198.4 2.3 copy-done.2
  202.8 40.7 %mix_backward.1 = (bf16[2048,1664]{1,0:T(8,128)(2,1)}, bf16[2048,1536]{1,0:T(8,128)(2,1)}, bf16[2048,768]{1,0:T(8,128)(2,1)}, f32[2048,768]{1,0:T(8,128)}, f32[16,768]{1,0:T(8,128)}) custom-call(bf16[2048,1536]{1,0:T(8,128)(2,1)} %get-tuple-element.245.dum_ref, f32[2048,768]{1,0:T(8,128)} %get-tuple-element.246.dt_ref, ...), custom_call_target="tpu_custom_call" | custom-call | flops 19730006016 | bytes 144000000 | tf_op jit(solution)/shard_map/mix_backward/pallas_call | solution.py:690
  243.4 2.4 bitcast_add_fusion
  247.1 2.1 bitcast_add_fusion.1
  249.8 7.7 %fusion.88 = f32[768,1664]{1,0:T(8,128)S(1)} fusion(bf16[768,2048]{1,0:T(8,128)(2,1)} %get-tuple-element.261, bf16[2048,1664]{1,0:T(8,128)(2,1)S(1)} %copy-done.44), kind=kOutput, calls=%fused_computation.263 | convolution fusion | flops 5234491392 | bytes 15073280 | tf_op jit(solution)/shard_map/dot_general | solution.py:278
  257.6 1.2 fusion.2
  258.8 1.7 dynamic-slice_bitcast_fusion
  261.3 2.9 collective-permute-done.33
  265.2 12.3 %ema_back_ends.1 = (f32[2,1024,768]{2,1,0:T(8,128)}, f32[2,128,768]{2,1,0:T(8,128)}, f32[2,16,768]{2,1,0:T(8,128)}) custom-call(bf16[2,1024,768]{2,1,0:T(8,128)(2,1)} %bitcast.238, f32[2,1024,768]{2,1,0:T(8,128)} %get-tuple-element.273.p_ref, f32[16,768]{1,0:T(8,128)} %get-tuple-element.193.q_ref), custom_call_target="tpu_custom_call" | custom-call | bytes 54000000 | tf_op jit(solution)/shard_map/ema_back_ends/pallas_call | solution.py:231
  279.7 2.4 collective-permute-start.38
  282.0 7.5 %fusion.89 = f32[1536,768]{0,1:T(8,128)S(1)} fusion(bf16[2048,1536]{1,0:T(8,128)(2,1)} %get-tuple-element.284, bf16[2048,768]{1,0:T(8,128)(2,1)S(1)} %bitcast.223), kind=kOutput, calls=%fused_computation.264 | convolution fusion | flops 4831838208 | bytes 14155776 | tf_op jit(solution)/shard_map/ri,rj->ij/dot_general | solution.py:23
  290.4 1.5 convert_add_fusion
  292.1 2.2 collective-permute-done.37
  294.3 1.8 collective-permute-start.39
  297.3 1.7 collective-permute-done.39
  299.0 1.5 collective-permute-start.41
  300.9 1.4 copy-done.7
  305.3 9.0 %ema_backward.6 = (bf16[2,1024,768]{2,1,0:T(8,128)(2,1)}, f32[72,768]{1,0:T(8,128)}) custom-call(f32[2,1024,768]{2,1,0:T(8,128)} %get-tuple-element.280.d_ref, bf16[2,1024,768]{2,1,0:T(8,128)(2,1)} %bitcast.217, f32[16,768]{1,0:T(8,128)} %get-tuple-element.193.q_ref, f32[16,768]{1,0:T(8,128)} %get-tuple-element.281.qi_ref, f32[16,768]{1,0:T(8,128)} %copy-done.9, ...), custom_call_target="tpu_custom_call" | custom-call | bytes 28800000 | tf_op jit(solution)/shard_map/ema_backward/pallas_call | solution.py:253
  314.3 1.3 bitcast_add_fusion.4
  316.7 2.1 collective-permute-start.43
  319.0 8.8 %ema_backward.7 = (bf16[2,1024,768]{2,1,0:T(8,128)(2,1)}, f32[72,768]{1,0:T(8,128)}) custom-call(f32[2,1024,768]{2,1,0:T(8,128)} %get-tuple-element.280.d_ref, bf16[2,1024,768]{2,1,0:T(8,128)(2,1)} %bitcast.218, f32[16,768]{1,0:T(8,128)} %get-tuple-element.193.q_ref, ...), custom_call_target="tpu_custom_call", output_to_operand_aliasing={{0}: (11, {}), {1}: (12, {})} | custom-call | bytes 28800000 | tf_op jit(solution)/shard_map/ema_backward/pallas_call | solution.py:253
  327.8 3.7 collective-permute-done.45
  332.5 1.2 bitcast_add_fusion.5
  335.6 8.8 %ema_backward.8 = (bf16[2,1024,768]{2,1,0:T(8,128)(2,1)}, f32[72,768]{1,0:T(8,128)}) custom-call(f32[2,1024,768]{2,1,0:T(8,128)} %get-tuple-element.280.d_ref, bf16[2,1024,768]{2,1,0:T(8,128)(2,1)} %bitcast.219, f32[16,768]{1,0:T(8,128)} %get-tuple-element.193.q_ref, ...), custom_call_target="tpu_custom_call", output_to_operand_aliasing={{0}: (11, {}), {1}: (12, {})} | custom-call | bytes 28800000 | tf_op jit(solution)/shard_map/ema_backward/pallas_call | solution.py:253
  345.5 1.2 collective-permute-done.47
  350.6 8.8 %ema_backward.9 = (bf16[2,1024,768]{2,1,0:T(8,128)(2,1)}, f32[72,768]{1,0:T(8,128)}) custom-call(f32[2,1024,768]{2,1,0:T(8,128)} %get-tuple-element.280.d_ref, bf16[2,1024,768]{2,1,0:T(8,128)(2,1)} %bitcast.220, f32[16,768]{1,0:T(8,128)} %get-tuple-element.193.q_ref, ...), custom_call_target="tpu_custom_call", output_to_operand_aliasing={{0}: (11, {}), {1}: (12, {})} | custom-call | bytes 28800000 | tf_op jit(solution)/shard_map/ema_backward/pallas_call | solution.py:253
  360.5 2.2 collective-permute-start.49
  362.7 1.8 collective-permute-start.51
  364.5 8.8 %ema_backward.10 = (bf16[2,1024,768]{2,1,0:T(8,128)(2,1)}, f32[72,768]{1,0:T(8,128)}) custom-call(f32[2,1024,768]{2,1,0:T(8,128)} %get-tuple-element.280.d_ref, bf16[2,1024,768]{2,1,0:T(8,128)(2,1)} %bitcast.221, f32[16,768]{1,0:T(8,128)} %get-tuple-element.193.q_ref, ...), custom_call_target="tpu_custom_call", output_to_operand_aliasing={{0}: (11, {}), {1}: (12, {})} | custom-call | bytes 28800000 | tf_op jit(solution)/shard_map/ema_backward/pallas_call | solution.py:253
  374.1 8.8 %ema_backward.11 = (bf16[2,1024,768]{2,1,0:T(8,128)(2,1)}, f32[72,768]{1,0:T(8,128)}) custom-call(f32[2,1024,768]{2,1,0:T(8,128)} %get-tuple-element.280.d_ref, bf16[2,1024,768]{2,1,0:T(8,128)(2,1)} %bitcast.222, f32[16,768]{1,0:T(8,128)} %get-tuple-element.193.q_ref, ...), custom_call_target="tpu_custom_call", output_to_operand_aliasing={{0}: (11, {}), {1}: (12, {})} | custom-call | bytes 28800000 | tf_op jit(solution)/shard_map/ema_backward/pallas_call | solution.py:253
  383.0 5.7 %collective-permute-done.51 = bf16[4,192,768]{2,1,0:T(8,128)(2,1)S(1)} collective-permute-done((bf16[4,192,768]{2,1,0:T(8,128)(2,1)S(1)}, bf16[4,192,768]{2,1,0:T(8,128)(2,1)S(1)}, u32[]{:S(2)}, u32[]{:S(2)}) %collective-permute-start.51) | collective-permute-done | bytes 1179680 | tf_op jit(solution)/shard_map/ppermute | solution.py:716
  392.5 1.5 collective-permute-start.53
  395.5 1.2 fusion.73
  397.8 1.2 collective-permute-done.53
  399.0 2.2 collective-permute-done.54
  401.4 1.8 collective-permute-start.59
  403.2 1.8 collective-permute-start.56
  405.1 7.5 %collective-permute-done.56 = f32[136,192]{1,0:T(8,128)S(1)} collective-permute-done((f32[136,192]{1,0:T(8,128)S(1)}, f32[136,192]{1,0:T(8,128)S(1)}, u32[]{:S(2)}, u32[]{:S(2)}) %collective-permute-start.56) | collective-permute-done | bytes 104480 | tf_op jit(solution)/shard_map/ppermute | solution.py:716
  412.8 5.0 %collective-permute-done.57 = f32[136,192]{1,0:T(8,128)S(1)} collective-permute-done((f32[136,192]{1,0:T(8,128)S(1)}, f32[136,192]{1,0:T(8,128)S(1)}, u32[]{:S(2)}, u32[]{:S(2)}) %collective-permute-start.57) | collective-permute-done | bytes 104480 | tf_op jit(solution)/shard_map/ppermute | solution.py:716
  419.4 3.5 collective-permute-done.58
  432.1 1.6 pad_maximum_fusion.2
  (330 shorter events, 74.1 us)
Async XLA Ops:
  10.2 4.9 %collective-permute-start = (bf16[192,79]{0,1:T(8,128)(2,1)S(1)}, bf16[192,79]{0,1:T(8,128)(2,1)S(1)}, u32[]{:S(2)}, u32[]{:S(2)}) collective-permute-start(bf16[192,79]{0,1:T(8,128)(2,1)S(1)} %concatenate.80), channel_id=1, source_target_pairs={{0,1},{1,0},{2,3},{3,2},{4,5},{5,4},{6,7},{7,6},{8,9},{9,8},{10,11... | collective-permute-start | bytes 91016 | tf_op jit(solution)/shard_map/ppermute | solution.py:716
  10.7 6.2 %collective-permute-start.1 = (bf16[192,79]{0,1:T(8,128)(2,1)S(1)}, bf16[192,79]{0,1:T(8,128)(2,1)S(1)}, u32[]{:S(2)}, u32[]{:S(2)}) collective-permute-start(bf16[192,79]{0,1:T(8,128)(2,1)S(1)} %concatenate.80), channel_id=1, source_target_pairs={{0,2},{1,3},{2,0},{3,1},{4,6},{5,7},{6,4},{7,5},{8,10},{9,11},{10,... | collective-permute-start | bytes 91016 | tf_op jit(solution)/shard_map/ppermute | solution.py:716
  13.2 3.6 collective-permute-start.2
  13.3 15.2 %collective-permute-start.3 = (bf16[192,3200]{1,0:T(8,128)(2,1)}, bf16[192,3200]{1,0:T(8,128)(2,1)}, u32[]{:S(2)}, u32[]{:S(2)}) collective-permute-start(bf16[192,3200]{1,0:T(8,128)(2,1)} %refs_0_.2), channel_id=1, source_target_pairs={{0,1},{1,0},{2,3},{3,2},{4,5},{5,4},{6,7},{7,6},{8,9},{9,8},{10,11... | collective-permute-start | bytes 3686408 | tf_op jit(solution)/shard_map/ppermute | solution.py:716
  13.4 15.1 %collective-permute-start.4 = (bf16[192,1536]{1,0:T(8,128)(2,1)}, bf16[192,1536]{1,0:T(8,128)(2,1)S(1)}, u32[]{:S(2)}, u32[]{:S(2)}) collective-permute-start(bf16[192,1536]{1,0:T(8,128)(2,1)} %refs_6_.1), channel_id=1, source_target_pairs={{0,1},{1,0},{2,3},{3,2},{4,5},{5,4},{6,7},{7,6},{8,9},{9,8},{10,11... | collective-permute-start | bytes 1769480 | tf_op jit(solution)/shard_map/ppermute | solution.py:716
  15.1 18.9 %collective-permute-start.6 = (bf16[96,3200]{1,0:T(8,128)(2,1)S(1)}, bf16[96,3200]{1,0:T(8,128)(2,1)}, u32[]{:S(2)}, u32[]{:S(2)}) collective-permute-start(bf16[96,3200]{1,0:T(8,128)(2,1)S(1)} %constant_dynamic-slice_fusion.33), channel_id=1, source_target_pairs={{0,2},{1,3},{2,0},{3,1},{4,6},{5,7},{6,4},{7,5},{8,10},{9,11},{10,... | collective-permute-start | bytes 1843208 | tf_op jit(solution)/shard_map/ppermute | solution.py:716
  18.0 17.8 %copy-start.9 = (f32[16,768]{1,0:T(8,128)}, f32[16,768]{1,0:T(8,128)S(1)}, u32[]{:S(2)}) copy-start(f32[16,768]{1,0:T(8,128)S(1)} %get-tuple-element.194.w_ref) | copy-start | bytes 147460
  28.5 31.3 %copy-start.18 = (f32[16,768]{1,0:T(8,128)}, f32[16,768]{1,0:T(8,128)S(1)}, u32[]{:S(2)}) copy-start(f32[16,768]{1,0:T(8,128)S(1)} %get-tuple-element.447) | copy-start | bytes 147460
  28.5 31.3 %copy-start.20 = (f32[16,768]{1,0:T(8,128)}, f32[16,768]{1,0:T(8,128)S(1)}, u32[]{:S(2)}) copy-start(f32[16,768]{1,0:T(8,128)S(1)} %get-tuple-element.450) | copy-start | bytes 147460
  29.3 5.0 %collective-permute-start.5 = (f32[2,16,768]{2,1,0:T(8,128)}, f32[2,16,768]{2,1,0:T(8,128)S(1)}, u32[]{:S(2)}, u32[]{:S(2)}) collective-permute-start(f32[2,16,768]{2,1,0:T(8,128)} %get-tuple-element.187), channel_id=1, source_target_pairs={{0,4},{4,0},{8,12},{12,8},{16,20},{20,16},{24,28},{28,24},{1,5},{5... | collective-permute-start | bytes 294920 | tf_op jit(solution)/shard_map/ppermute | solution.py:716
  30.9 18.4 %collective-permute-start.9 = (bf16[96,1536]{1,0:T(8,128)(2,1)S(1)}, bf16[96,1536]{1,0:T(8,128)(2,1)}, u32[]{:S(2)}, u32[]{:S(2)}) collective-permute-start(bf16[96,1536]{1,0:T(8,128)(2,1)S(1)} %constant_dynamic-slice_fusion.32), channel_id=1, source_target_pairs={{0,2},{1,3},{2,0},{3,1},{4,6},{5,7},{6,4},{7,5},{8,10},{9,11},{10,... | collective-permute-start | bytes 884744 | tf_op jit(solution)/shard_map/ppermute | solution.py:716
  32.7 27.1 %collective-permute-start.12 = (bf16[192,768]{1,0:T(8,128)(2,1)S(1)}, bf16[192,768]{1,0:T(8,128)(2,1)}, u32[]{:S(2)}, u32[]{:S(2)}) collective-permute-start(bf16[192,768]{1,0:T(8,128)(2,1)S(1)} %constant_dynamic-slice_fusion.31), channel_id=1, source_target_pairs={{0,2},{1,3},{2,0},{3,1},{4,6},{5,7},{6,4},{7,5},{8,10},{9,11},{10,... | collective-permute-start | bytes 884744 | tf_op jit(solution)/shard_map/ppermute | solution.py:716
  34.3 15.0 %collective-permute-start.10 = (bf16[96,3200]{1,0:T(8,128)(2,1)}, bf16[96,3200]{1,0:T(8,128)(2,1)}, u32[]{:S(2)}, u32[]{:S(2)}) collective-permute-start(bf16[96,3200]{1,0:T(8,128)(2,1)} %collective-permute-done.6.refs_2_), channel_id=1, source_target_pairs={{0,1},{1,0},{2,3},{3,2},{4,5},{5,4},{6,7},{7,6},{8,9},{9,8},{10,11... | collective-permute-start | bytes 1843208 | tf_op jit(solution)/shard_map/ppermute | solution.py:716
  34.3 25.5 %collective-permute-start.11 = (bf16[96,3200]{1,0:T(8,128)(2,1)}, bf16[96,3200]{1,0:T(8,128)(2,1)}, u32[]{:S(2)}, u32[]{:S(2)}) collective-permute-start(bf16[96,3200]{1,0:T(8,128)(2,1)} %collective-permute-done.6.refs_2_), channel_id=1, source_target_pairs={{0,4},{4,0},{8,12},{12,8},{16,20},{20,16},{24,28},{28,24},{1,5},{5... | collective-permute-start | bytes 1843208 | tf_op jit(solution)/shard_map/ppermute | solution.py:716
  36.3 5.0 %collective-permute-start.7 = (f32[2,16,768]{2,1,0:T(8,128)S(1)}, f32[2,16,768]{2,1,0:T(8,128)S(1)}, u32[]{:S(2)}, u32[]{:S(2)}) collective-permute-start(f32[2,16,768]{2,1,0:T(8,128)S(1)} %add_select_fusion.7), channel_id=1, source_target_pairs={{0,8},{4,12},{8,0},{12,4},{16,24},{20,28},{24,16},{28,20},{1,9},{5... | collective-permute-start | bytes 294920 | tf_op jit(solution)/shard_map/ppermute | solution.py:716
  38.6 21.2 %copy-start.5 = (f32[80,768]{1,0:T(8,128)}, f32[80,768]{1,0:T(8,128)S(1)}, u32[]{:S(2)}) copy-start(f32[80,768]{1,0:T(8,128)S(1)} %get-tuple-element.290.k_ref) | copy-start | bytes 737284
  41.3 7.3 %collective-permute-start.8 = (f32[2,16,768]{2,1,0:T(8,128)S(1)}, f32[2,16,768]{2,1,0:T(8,128)S(1)}, u32[]{:S(2)}, u32[]{:S(2)}) collective-permute-start(f32[2,16,768]{2,1,0:T(8,128)S(1)} %add_select_fusion.6), channel_id=1, source_target_pairs={{0,16},{4,20},{8,24},{12,28},{16,0},{20,4},{24,8},{28,12},{1,17},{... | collective-permute-start | bytes 294920 | tf_op jit(solution)/shard_map/ppermute | solution.py:716
  49.3 10.5 %collective-permute-start.13 = (bf16[96,1536]{1,0:T(8,128)(2,1)}, bf16[96,1536]{1,0:T(8,128)(2,1)S(1)}, u32[]{:S(2)}, u32[]{:S(2)}) collective-permute-start(bf16[96,1536]{1,0:T(8,128)(2,1)} %collective-permute-done.9.refs_8_), channel_id=1, source_target_pairs={{0,1},{1,0},{2,3},{3,2},{4,5},{5,4},{6,7},{7,6},{8,9},{9,8},{10,11... | collective-permute-start | bytes 884744 | tf_op jit(solution)/shard_map/ppermute | solution.py:716
  59.8 16.6 %collective-permute-start.17 = (bf16[96,3200]{1,0:T(8,128)(2,1)}, bf16[96,3200]{1,0:T(8,128)(2,1)S(1)}, u32[]{:S(2)}, u32[]{:S(2)}) collective-permute-start(bf16[96,3200]{1,0:T(8,128)(2,1)} %collective-permute-done.11.refs_3_), channel_id=1, source_target_pairs={{0,1},{1,0},{2,3},{3,2},{4,5},{5,4},{6,7},{7,6},{8,9},{9,8},{10,11... | collective-permute-start | bytes 1843208 | tf_op jit(solution)/shard_map/ppermute | solution.py:716
  60.4 16.0 %collective-permute-start.18 = (bf16[384,768]{1,0:T(8,128)(2,1)S(1)}, bf16[384,768]{1,0:T(8,128)(2,1)S(1)}, u32[]{:S(2)}, u32[]{:S(2)}) collective-permute-start(bf16[384,768]{1,0:T(8,128)(2,1)S(1)} %copy-done.26), channel_id=1, source_target_pairs={{0,1},{1,0},{2,3},{3,2},{4,5},{5,4},{6,7},{7,6},{8,9},{9,8},{10,11... | collective-permute-start | bytes 1769480 | tf_op jit(solution)/shard_map/ppermute | solution.py:716
  60.5 11.9 %collective-permute-start.14 = (bf16[96,1536]{1,0:T(8,128)(2,1)}, bf16[96,1536]{1,0:T(8,128)(2,1)S(1)}, u32[]{:S(2)}, u32[]{:S(2)}) collective-permute-start(bf16[96,1536]{1,0:T(8,128)(2,1)} %collective-permute-done.9.refs_8_), channel_id=1, source_target_pairs={{0,4},{4,0},{8,12},{12,8},{16,20},{20,16},{24,28},{28,24},{1,5},{5... | collective-permute-start | bytes 884744 | tf_op jit(solution)/shard_map/ppermute | solution.py:716
  61.0 15.4 %collective-permute-start.15 = (bf16[192,768]{1,0:T(8,128)(2,1)}, bf16[192,768]{1,0:T(8,128)(2,1)S(1)}, u32[]{:S(2)}, u32[]{:S(2)}) collective-permute-start(bf16[192,768]{1,0:T(8,128)(2,1)} %collective-permute-done.12.refs_14_), channel_id=1, source_target_pairs={{0,4},{4,0},{8,12},{12,8},{16,20},{20,16},{24,28},{28,24},{1,5},{5... | collective-permute-start | bytes 884744 | tf_op jit(solution)/shard_map/ppermute | solution.py:716
  62.5 13.9 %collective-permute-start.16 = (bf16[192,768]{1,0:T(8,128)(2,1)}, bf16[192,768]{1,0:T(8,128)(2,1)S(1)}, u32[]{:S(2)}, u32[]{:S(2)}) collective-permute-start(bf16[192,768]{1,0:T(8,128)(2,1)} %collective-permute-done.12.refs_14_), channel_id=1, source_target_pairs={{0,1},{1,0},{2,3},{3,2},{4,5},{5,4},{6,7},{7,6},{8,9},{9,8},{10,11... | collective-permute-start | bytes 884744 | tf_op jit(solution)/shard_map/ppermute | solution.py:716
  76.4 3.4 collective-permute-start.19
  76.5 3.6 collective-permute-start.20
  77.7 36.2 %collective-permute-start.21 = (bf16[192,1536]{1,0:T(8,128)(2,1)}, bf16[192,1536]{1,0:T(8,128)(2,1)S(1)}, u32[]{:S(2)}, u32[]{:S(2)}) collective-permute-start(bf16[192,1536]{1,0:T(8,128)(2,1)} %refs_0_.1), channel_id=1, source_target_pairs={{0,2},{1,3},{2,0},{3,1},{4,6},{5,7},{6,4},{7,5},{8,10},{9,11},{10,... | collective-permute-start | bytes 1769480 | tf_op jit(solution)/shard_map/ppermute | solution.py:716
  78.7 35.2 %collective-permute-start.23 = (bf16[192,1536]{1,0:T(8,128)(2,1)}, bf16[192,1536]{1,0:T(8,128)(2,1)S(1)}, u32[]{:S(2)}, u32[]{:S(2)}) collective-permute-start(bf16[192,1536]{1,0:T(8,128)(2,1)} %refs_0_.1), channel_id=1, source_target_pairs={{0,1},{1,0},{2,3},{3,2},{4,5},{5,4},{6,7},{7,6},{8,9},{9,8},{10,11... | collective-permute-start | bytes 1769480 | tf_op jit(solution)/shard_map/ppermute | solution.py:716
  78.7 35.3 %collective-permute-start.22 = (bf16[384,768]{1,0:T(8,128)(2,1)}, bf16[384,768]{1,0:T(8,128)(2,1)}, u32[]{:S(2)}, u32[]{:S(2)}) collective-permute-start(bf16[384,768]{1,0:T(8,128)(2,1)} %refs_4_), channel_id=1, source_target_pairs={{0,2},{1,3},{2,0},{3,1},{4,6},{5,7},{6,4},{7,5},{8,10},{9,11},{10,... | collective-permute-start | bytes 1769480 | tf_op jit(solution)/shard_map/ppermute | solution.py:716
  79.8 34.2 %collective-permute-start.24 = (bf16[384,768]{1,0:T(8,128)(2,1)}, bf16[384,768]{1,0:T(8,128)(2,1)}, u32[]{:S(2)}, u32[]{:S(2)}) collective-permute-start(bf16[384,768]{1,0:T(8,128)(2,1)} %refs_4_), channel_id=1, source_target_pairs={{0,1},{1,0},{2,3},{3,2},{4,5},{5,4},{6,7},{7,6},{8,9},{9,8},{10,11... | collective-permute-start | bytes 1769480 | tf_op jit(solution)/shard_map/ppermute | solution.py:716
  114.0 2.1 collective-permute-start.25
  114.3 2.9 collective-permute-start.26
  169.4 22.8 %collective-permute-start.28 = (bf16[2,2,2,2,24,1536]{5,4,3,2,1,0:T(8,128)(2,1)S(1)}, bf16[2,2,2,2,24,1536]{5,4,3,2,1,0:T(8,128)(2,1)S(1)}, u32[]{:S(2)}, u32[]{:S(2)}) collective-permute-start(bf16[2,2,2,2,24,1536]{5,4,3,2,1,0:T(8,128)(2,1)S(1)} %fusion.9), channel_id=1, source_target_pairs={{0,1},{1,0},{2,3},{3,2},{4,5},{5,4},{6,7},{7,6},{8,9},{9,8},{10,11... | collective-permute-start | bytes 3538952 | tf_op jit(solution)/shard_map/ppermute | solution.py:716
  175.0 17.2 %collective-permute-start.27 = (bf16[2,2,2,2,48,768]{5,4,3,2,1,0:T(8,128)(2,1)S(1)}, bf16[2,2,2,2,48,768]{5,4,3,2,1,0:T(8,128)(2,1)S(1)}, u32[]{:S(2)}, u32[]{:S(2)}) collective-permute-start(bf16[2,2,2,2,48,768]{5,4,3,2,1,0:T(8,128)(2,1)S(1)} %fusion.3), channel_id=1, source_target_pairs={{0,1},{1,0},{2,3},{3,2},{4,5},{5,4},{6,7},{7,6},{8,9},{9,8},{10,11... | collective-permute-start | bytes 3538952 | tf_op jit(solution)/shard_map/ppermute | solution.py:716
  182.7 9.6 %collective-permute-start.31 = (bf16[2,2,2,2,24,1536]{5,4,2,1,0,3:T(8,128)(2,1)S(1)}, bf16[2,2,2,2,24,1536]{5,4,2,1,0,3:T(8,128)(2,1)S(1)}, u32[]{:S(2)}, u32[]{:S(2)}) collective-permute-start(bf16[2,2,2,2,24,1536]{5,4,2,1,0,3:T(8,128)(2,1)S(1)} %fusion.7), channel_id=1, source_target_pairs={{0,1},{1,0},{2,3},{3,2},{4,5},{5,4},{6,7},{7,6},{8,9},{9,8},{10,11... | collective-permute-start | bytes 3538952 | tf_op jit(solution)/shard_map/ppermute | solution.py:716
  191.5 2.9 collective-permute-start.30
  195.3 48.1 %collective-permute-start.32 = (bf16[2,2,2,96,768]{4,3,2,1,0:T(8,128)(2,1)S(1)}, bf16[2,2,2,96,768]{4,3,2,1,0:T(8,128)(2,1)}, u32[]{:S(2)}, u32[]{:S(2)}) collective-permute-start(bf16[2,2,2,96,768]{4,3,2,1,0:T(8,128)(2,1)S(1)} %fusion.5), channel_id=1, source_target_pairs={{0,4},{4,0},{8,12},{12,8},{16,20},{20,16},{24,28},{28,24},{1,5},{5... | collective-permute-start | bytes 3538952 | tf_op jit(solution)/shard_map/ppermute | solution.py:716
  201.8 41.6 %collective-permute-start.29 = (bf16[2,2,2,96,768]{4,3,2,1,0:T(8,128)(2,1)}, bf16[2,2,2,96,768]{4,3,2,1,0:T(8,128)(2,1)}, u32[]{:S(2)}, u32[]{:S(2)}) collective-permute-start(bf16[2,2,2,96,768]{4,3,2,1,0:T(8,128)(2,1)} %fusion.4), channel_id=1, source_target_pairs={{0,2},{1,3},{2,0},{3,1},{4,6},{5,7},{6,4},{7,5},{8,10},{9,11},{10,... | collective-permute-start | bytes 3538952 | tf_op jit(solution)/shard_map/ppermute | solution.py:716
  246.0 15.3 %collective-permute-start.34 = (bf16[2,2,96,768]{3,2,1,0:T(8,128)(2,1)S(1)}, bf16[2,2,96,768]{3,2,1,0:T(8,128)(2,1)S(1)}, u32[]{:S(2)}, u32[]{:S(2)}) collective-permute-start(bf16[2,2,96,768]{3,2,1,0:T(8,128)(2,1)S(1)} %fusion.22), channel_id=1, source_target_pairs={{0,2},{1,3},{2,0},{3,1},{4,6},{5,7},{6,4},{7,5},{8,10},{9,11},{10,... | collective-permute-start | bytes 1769480 | tf_op jit(solution)/shard_map/ppermute | solution.py:716
  249.2 15.0 %collective-permute-start.33 = (bf16[2,2,96,768]{3,2,1,0:T(8,128)(2,1)S(1)}, bf16[2,2,96,768]{3,2,1,0:T(8,128)(2,1)S(1)}, u32[]{:S(2)}, u32[]{:S(2)}) collective-permute-start(bf16[2,2,96,768]{3,2,1,0:T(8,128)(2,1)S(1)} %fusion.21), channel_id=1, source_target_pairs={{0,4},{4,0},{8,12},{12,8},{16,20},{20,16},{24,28},{28,24},{1,5},{5... | collective-permute-start | bytes 1769480 | tf_op jit(solution)/shard_map/ppermute | solution.py:716
  258.8 19.8 %collective-permute-start.36 = (bf16[2,2,2,2,24,1664]{5,4,3,2,1,0:T(8,128)(2,1)}, bf16[2,2,2,2,24,1664]{5,4,3,2,1,0:T(8,128)(2,1)}, u32[]{:S(2)}, u32[]{:S(2)}) collective-permute-start(bf16[2,2,2,2,24,1664]{5,4,3,2,1,0:T(8,128)(2,1)} %fusion.2), channel_id=1, source_target_pairs={{0,1},{1,0},{2,3},{3,2},{4,5},{5,4},{6,7},{7,6},{8,9},{9,8},{10,11... | collective-permute-start | bytes 3833864 | tf_op jit(solution)/shard_map/ppermute | solution.py:716
  264.5 14.1 %collective-permute-start.35 = (bf16[2,192,768]{2,1,0:T(8,128)(2,1)S(1)}, bf16[2,192,768]{2,1,0:T(8,128)(2,1)S(1)}, u32[]{:S(2)}, u32[]{:S(2)}) collective-permute-start(bf16[2,192,768]{2,1,0:T(8,128)(2,1)S(1)} %fusion.24), channel_id=1, source_target_pairs={{0,8},{4,12},{8,0},{12,4},{16,24},{20,28},{24,16},{28,20},{1,9},{5... | collective-permute-start | bytes 1769480 | tf_op jit(solution)/shard_map/ppermute | solution.py:716
  279.7 14.6 %collective-permute-start.38 = (bf16[192,768]{1,0:T(8,128)(2,1)S(1)}, bf16[192,768]{1,0:T(8,128)(2,1)S(1)}, u32[]{:S(2)}, u32[]{:S(2)}) collective-permute-start(bf16[192,768]{1,0:T(8,128)(2,1)S(1)} %fusion.29), channel_id=1, source_target_pairs={{0,16},{4,20},{8,24},{12,28},{16,0},{20,4},{24,8},{28,12},{1,17},{... | collective-permute-start | bytes 884744 | tf_op jit(solution)/shard_map/ppermute | solution.py:716
  289.6 4.7 %collective-permute-start.37 = (f32[2,16,768]{2,1,0:T(8,128)S(1)}, f32[2,16,768]{2,1,0:T(8,128)S(1)}, u32[]{:S(2)}, u32[]{:S(2)}) collective-permute-start(f32[2,16,768]{2,1,0:T(8,128)S(1)} %copy-done.28), channel_id=1, source_target_pairs={{0,4},{4,0},{8,12},{12,8},{16,20},{20,16},{24,28},{28,24},{1,5},{5... | collective-permute-start | bytes 294920 | tf_op jit(solution)/shard_map/ppermute | solution.py:716
  290.3 8.7 %collective-permute-start.40 = (bf16[2,2,2,2,24,1536]{5,4,2,1,0,3:T(8,128)(2,1)S(1)}, bf16[2,2,2,2,24,1536]{5,4,2,1,0,3:T(8,128)(2,1)S(1)}, u32[]{:S(2)}, u32[]{:S(2)}) collective-permute-start(bf16[2,2,2,2,24,1536]{5,4,2,1,0,3:T(8,128)(2,1)S(1)} %fusion.8), channel_id=1, source_target_pairs={{0,1},{1,0},{2,3},{3,2},{4,5},{5,4},{6,7},{7,6},{8,9},{9,8},{10,11... | collective-permute-start | bytes 3538952 | tf_op jit(solution)/shard_map/ppermute | solution.py:716
  294.3 4.7 %collective-permute-start.39 = (f32[2,16,768]{2,1,0:T(8,128)S(1)}, f32[2,16,768]{2,1,0:T(8,128)S(1)}, u32[]{:S(2)}, u32[]{:S(2)}) collective-permute-start(f32[2,16,768]{2,1,0:T(8,128)S(1)} %add_select_fusion.5), channel_id=1, source_target_pairs={{0,8},{4,12},{8,0},{12,4},{16,24},{20,28},{24,16},{28,20},{1,9},{5... | collective-permute-start | bytes 294920 | tf_op jit(solution)/shard_map/ppermute | solution.py:716
  296.1 18.2 %collective-permute-start.42 = (bf16[2,2,2,24,1664]{4,3,2,1,0:T(8,128)(2,1)S(1)}, bf16[2,2,2,24,1664]{4,3,2,1,0:T(8,128)(2,1)}, u32[]{:S(2)}, u32[]{:S(2)}) collective-permute-start(bf16[2,2,2,24,1664]{4,3,2,1,0:T(8,128)(2,1)S(1)} %fusion.15), channel_id=1, source_target_pairs={{0,2},{1,3},{2,0},{3,1},{4,6},{5,7},{6,4},{7,5},{8,10},{9,11},{10,... | collective-permute-start | bytes 1916936 | tf_op jit(solution)/shard_map/ppermute | solution.py:716
  299.0 5.6 %collective-permute-start.41 = (f32[2,16,768]{2,1,0:T(8,128)S(1)}, f32[2,16,768]{2,1,0:T(8,128)S(1)}, u32[]{:S(2)}, u32[]{:S(2)}) collective-permute-start(f32[2,16,768]{2,1,0:T(8,128)S(1)} %add_select_fusion.4), channel_id=1, source_target_pairs={{0,16},{4,20},{8,24},{12,28},{16,0},{20,4},{24,8},{28,12},{1,17},{... | collective-permute-start | bytes 294920 | tf_op jit(solution)/shard_map/ppermute | solution.py:716
  303.2 28.3 %collective-permute-start.44 = (bf16[2,2,2,24,1536]{4,3,2,1,0:T(8,128)(2,1)}, bf16[2,2,2,24,1536]{4,3,2,1,0:T(8,128)(2,1)}, u32[]{:S(2)}, u32[]{:S(2)}) collective-permute-start(bf16[2,2,2,24,1536]{4,3,2,1,0:T(8,128)(2,1)} %fusion.23), channel_id=1, source_target_pairs={{0,4},{4,0},{8,12},{12,8},{16,20},{20,16},{24,28},{28,24},{1,5},{5... | collective-permute-start | bytes 1769480 | tf_op jit(solution)/shard_map/ppermute | solution.py:716
  316.7 14.8 %collective-permute-start.43 = (bf16[2,2,24,1664]{3,2,1,0:T(8,128)(2,1)S(1)}, bf16[2,2,24,1664]{3,2,1,0:T(8,128)(2,1)S(1)}, u32[]{:S(2)}, u32[]{:S(2)}) collective-permute-start(bf16[2,2,24,1664]{3,2,1,0:T(8,128)(2,1)S(1)} %fusion.26), channel_id=1, source_target_pairs={{0,4},{4,0},{8,12},{12,8},{16,20},{20,16},{24,28},{28,24},{1,5},{5... | collective-permute-start | bytes 958472 | tf_op jit(solution)/shard_map/ppermute | solution.py:716
  318.8 12.6 %collective-permute-start.45 = (bf16[1,192,768]{2,1,0:T(8,128)(2,1)S(1)}, bf16[1,192,768]{2,1,0:T(8,128)(2,1)S(1)}, u32[]{:S(2)}, u32[]{:S(2)}) collective-permute-start(bf16[1,192,768]{2,1,0:T(8,128)(2,1)S(1)} %fusion.31), channel_id=1, source_target_pairs={{0,16},{4,20},{8,24},{12,28},{16,0},{20,4},{24,8},{28,12},{1,17},{... | collective-permute-start | bytes 884744 | tf_op jit(solution)/shard_map/ppermute | solution.py:716
  332.5 14.2 %collective-permute-start.47 = (bf16[2,192,768]{2,1,0:T(8,128)(2,1)}, bf16[2,192,768]{2,1,0:T(8,128)(2,1)}, u32[]{:S(2)}, u32[]{:S(2)}) collective-permute-start(bf16[2,192,768]{2,1,0:T(8,128)(2,1)} %pad_maximum_fusion.8), channel_id=1, source_target_pairs={{0,8},{4,12},{8,0},{12,4},{16,24},{20,28},{24,16},{28,20},{1,9},{5... | collective-permute-start | bytes 1769480 | tf_op jit(solution)/shard_map/ppermute | solution.py:716
  334.5 11.1 %collective-permute-start.46 = (bf16[2,2,24,1536]{3,2,1,0:T(8,128)(2,1)}, bf16[2,2,24,1536]{3,2,1,0:T(8,128)(2,1)}, u32[]{:S(2)}, u32[]{:S(2)}) collective-permute-start(bf16[2,2,24,1536]{3,2,1,0:T(8,128)(2,1)} %fusion.30), channel_id=1, source_target_pairs={{0,2},{1,3},{2,0},{3,1},{4,6},{5,7},{6,4},{7,5},{8,10},{9,11},{10,... | collective-permute-start | bytes 884744 | tf_op jit(solution)/shard_map/ppermute | solution.py:716
  348.5 10.9 %collective-permute-start.48 = (bf16[2,24,3200]{2,1,0:T(8,128)(2,1)}, bf16[2,24,3200]{2,1,0:T(8,128)(2,1)}, u32[]{:S(2)}, u32[]{:S(2)}) collective-permute-start(bf16[2,24,3200]{2,1,0:T(8,128)(2,1)} %fusion.27), channel_id=1, source_target_pairs={{0,8},{4,12},{8,0},{12,4},{16,24},{20,28},{24,16},{28,20},{1,9},{5... | collective-permute-start | bytes 921608 | tf_op jit(solution)/shard_map/ppermute | solution.py:716
  360.5 12.8 %collective-permute-start.49 = (bf16[24,3200]{1,0:T(8,128)(2,1)S(1)}, bf16[24,3200]{1,0:T(8,128)(2,1)S(1)}, u32[]{:S(2)}, u32[]{:S(2)}) collective-permute-start(bf16[24,3200]{1,0:T(8,128)(2,1)S(1)} %fusion.32), channel_id=1, source_target_pairs={{0,16},{4,20},{8,24},{12,28},{16,0},{20,4},{24,8},{28,12},{1,17},{... | collective-permute-start | bytes 460808 | tf_op jit(solution)/shard_map/ppermute | solution.py:716
  362.7 26.0 %collective-permute-start.51 = (bf16[4,192,768]{2,1,0:T(8,128)(2,1)S(1)}, bf16[4,192,768]{2,1,0:T(8,128)(2,1)S(1)}, u32[]{:S(2)}, u32[]{:S(2)}) collective-permute-start(bf16[4,192,768]{2,1,0:T(8,128)(2,1)S(1)} %pad_maximum_fusion.5), channel_id=1, source_target_pairs={{0,4},{4,0},{8,12},{12,8},{16,20},{20,16},{24,28},{28,24},{1,5},{5... | collective-permute-start | bytes 3538952 | tf_op jit(solution)/shard_map/ppermute | solution.py:716
  373.3 9.6 %collective-permute-start.50 = (bf16[1,24,3200]{2,1,0:T(8,128)(2,1)S(1)}, bf16[1,24,3200]{2,1,0:T(8,128)(2,1)S(1)}, u32[]{:S(2)}, u32[]{:S(2)}) collective-permute-start(bf16[1,24,3200]{2,1,0:T(8,128)(2,1)S(1)} %fusion.33), channel_id=1, source_target_pairs={{0,16},{4,20},{8,24},{12,28},{16,0},{20,4},{24,8},{28,12},{1,17},{... | collective-permute-start | bytes 460808 | tf_op jit(solution)/shard_map/ppermute | solution.py:716
  389.8 11.4 %collective-permute-start.55 = (bf16[2,24,3200]{2,1,0:T(8,128)(2,1)S(1)}, bf16[2,24,3200]{2,1,0:T(8,128)(2,1)S(1)}, u32[]{:S(2)}, u32[]{:S(2)}) collective-permute-start(bf16[2,24,3200]{2,1,0:T(8,128)(2,1)S(1)} %pad_maximum_fusion.9), channel_id=1, source_target_pairs={{0,8},{4,12},{8,0},{12,4},{16,24},{20,28},{24,16},{28,20},{1,9},{5... | collective-permute-start | bytes 921608 | tf_op jit(solution)/shard_map/ppermute | solution.py:716
  392.4 5.5 %collective-permute-start.52 = (f32[136,192]{1,0:T(8,128)S(1)}, f32[136,192]{1,0:T(8,128)S(1)}, u32[]{:S(2)}, u32[]{:S(2)}) collective-permute-start(f32[136,192]{1,0:T(8,128)S(1)} %bitcast.267), channel_id=1, source_target_pairs={{0,1},{1,0},{2,3},{3,2},{4,5},{5,4},{6,7},{7,6},{8,9},{9,8},{10,11... | collective-permute-start | bytes 313352 | tf_op jit(solution)/shard_map/ppermute | solution.py:716
  392.5 6.5 %collective-permute-start.53 = (f32[136,192]{1,0:T(8,128)S(1)}, f32[136,192]{1,0:T(8,128)S(1)}, u32[]{:S(2)}, u32[]{:S(2)}) collective-permute-start(f32[136,192]{1,0:T(8,128)S(1)} %bitcast.268), channel_id=1, source_target_pairs={{0,2},{1,3},{2,0},{3,1},{4,6},{5,7},{6,4},{7,5},{8,10},{9,11},{10,... | collective-permute-start | bytes 313352 | tf_op jit(solution)/shard_map/ppermute | solution.py:716
  394.0 7.2 %collective-permute-start.54 = (f32[136,192]{1,0:T(8,128)S(1)}, f32[136,192]{1,0:T(8,128)S(1)}, u32[]{:S(2)}, u32[]{:S(2)}) collective-permute-start(f32[136,192]{1,0:T(8,128)S(1)} %bitcast.269), channel_id=1, source_target_pairs={{0,3},{1,2},{2,1},{3,0},{4,7},{5,6},{6,5},{7,4},{8,11},{9,10},{10,... | collective-permute-start | bytes 313352 | tf_op jit(solution)/shard_map/ppermute | solution.py:716
  401.4 21.5 %collective-permute-start.59 = (bf16[4,24,3200]{2,1,0:T(8,128)(2,1)S(1)}, bf16[4,24,3200]{2,1,0:T(8,128)(2,1)S(1)}, u32[]{:S(2)}, u32[]{:S(2)}) collective-permute-start(bf16[4,24,3200]{2,1,0:T(8,128)(2,1)S(1)} %pad_maximum_fusion.7), channel_id=1, source_target_pairs={{0,4},{4,0},{8,12},{12,8},{16,20},{20,16},{24,28},{28,24},{1,5},{5... | collective-permute-start | bytes 1843208 | tf_op jit(solution)/shard_map/ppermute | solution.py:716
  403.2 9.4 %collective-permute-start.56 = (f32[136,192]{1,0:T(8,128)S(1)}, f32[136,192]{1,0:T(8,128)S(1)}, u32[]{:S(2)}, u32[]{:S(2)}) collective-permute-start(f32[136,192]{1,0:T(8,128)S(1)} %fusion.39), channel_id=1, source_target_pairs={{0,16},{4,20},{8,24},{12,28},{16,0},{20,4},{24,8},{28,12},{1,17},{... | collective-permute-start | bytes 313352 | tf_op jit(solution)/shard_map/ppermute | solution.py:716
  412.7 5.1 %collective-permute-start.57 = (f32[136,192]{1,0:T(8,128)S(1)}, f32[136,192]{1,0:T(8,128)S(1)}, u32[]{:S(2)}, u32[]{:S(2)}) collective-permute-start(f32[136,192]{1,0:T(8,128)S(1)} %add.295), channel_id=1, source_target_pairs={{0,8},{4,12},{8,0},{12,4},{16,24},{20,28},{24,16},{28,20},{1,9},{5... | collective-permute-start | bytes 313352 | tf_op jit(solution)/shard_map/ppermute | solution.py:716
  417.8 5.1 %collective-permute-start.58 = (f32[136,192]{1,0:T(8,128)S(1)}, f32[136,192]{1,0:T(8,128)S(1)}, u32[]{:S(2)}, u32[]{:S(2)}) collective-permute-start(f32[136,192]{1,0:T(8,128)S(1)} %add.296), channel_id=1, source_target_pairs={{0,4},{4,0},{8,12},{12,8},{16,20},{20,16},{24,28},{28,24},{1,5},{5... | collective-permute-start | bytes 313352 | tf_op jit(solution)/shard_map/ppermute | solution.py:716
  (42 other events, 209.0 us)

commit v2 on v1

--- a/solution.py
+++ b/solution.py
@@ -877,7 +877,7 @@
     x_step = ("wsh", 2)
     sixth = D // LANES // 6
     steps = seq_steps()
-    half = D // LANES // 2
+    third = D // LANES // 3
 
     x_mix = over_x(own_half(o_mix))
     c_mix, c_value = over_core(o_mix), over_core(o_value)
@@ -912,12 +912,12 @@
         entry.entry, x_value, xc_mix, rel_matrix, norms, bo, qk, inverse, factors, bm
     )
     y_value, xc_value = over_y(x_value), over_core(x_value)
-    so_far = ema_forward((0, half), (), x3, keep, weight, omega, ends, state_in)
+    so_far = ema_forward((0, third), (), x3, keep, weight, omega, ends, state_in)
     *so_far, y_mix, x_out, xc_value, o_out, o_in, o_fout = join(*so_far, y_mix, x_out, xc_value, o_out, o_in, o_fout)
     y_out, xc_out, yc_mix = over_y(x_out), over_core(x_out), over_core(y_mix)
     c_out = over_core(o_out)
     x_in = over_x(o_in)
-    xp, pre, finals = ema_forward((half, half), tuple(so_far), x3, keep, weight, omega, ends, state_in)
+    xp, pre, finals = ema_forward((third, 2 * third), tuple(so_far), x3, keep, weight, omega, ends, state_in)
     xp, y_value, y_out, xc_out, yc_mix, c_out, o_fout = join(xp, y_value, y_out, xc_out, yc_mix, c_out, o_fout)
     yc_value, yc_out = over_core(y_value), over_core(y_out)
     x_fout = over_x(o_fout)

time: 442 us -> 440 us (level)
  no operation moved by 1% of the time
where the time goes in v2:
time: 440 us; the launch traced here: 432 us
  Pallas kernels  211 us (48%)
  starting transfers between devices  50.8 us (12%)
  waiting for transfers between devices  47.6 us (11%)
  matrix products  44.7 us (10%)
  local copies, waits for them, and re-layouts  43.9 us (10%)
  other arithmetic  31.3 us (7%)
    pallas_call x6, Pallas kernels, ema_backward(): pl.pallas_call(functools.partial(bwd_kernel, H, L // CH), grid=(count, G)...  53 us
    ppermute x60, starting transfers between devices, exchange(): lax.ppermute(value, axis, [(k, k ^ step) for k in range(lax.axis_size(axi...  50.8 us
    ppermute x60, waiting for transfers between devices, exchange(): lax.ppermute(value, axis, [(k, k ^ step) for k in range(lax.axis_size(axi...  47.6 us
    pallas_call x1, Pallas kernels, ffn_both(): pl.pallas_call(functools.partial(ffn_kernel, R, (D, FF, L)), grid=(T // R...  43.1 us
    pallas_call x1, Pallas kernels, mix_backward(): pl.pallas_call(functools.partial(mix_bwd_kernel, R, (D, Z, V)), grid=(T /...  40.7 us
    pallas_call x1, Pallas kernels, mix_forward(): pl.pallas_call(functools.partial(mix_fwd_kernel, R, (D, Z, V)), grid=(T /...  32.7 us
    dot_general x4, matrix products, dot_rows(): jnp.einsum('ri,rj->ij', left_op, right_op, preferred_element_type=jnp.flo...  29.9 us
    pallas_call x2, Pallas kernels, ema_forward(): pl.pallas_call(functools.partial(fwd_kernel, H, L // CH), grid=(count, G)...  19.7 us
  transfers between devices with their start and end apart: 60, of which 21 were waited for; matrix products, arithmetic and copies ran while one was open for 17% of the time, Pallas kernels for 39%

profile of v2, /device:TPU:0, one launch (start us, length us, event | category | flops | bytes accessed | tf_op | source)
XLA Modules:
  0.0 431.6 jit_solution(14258212119211931808)
XLA Ops:
  1.4 3.5 concatenate.79
  6.5 3.6 concatenate.80
  10.7 2.6 collective-permute-start.1
  15.1 1.7 collective-permute-start.6
  18.5 9.3 %ema_ends.1 = (f32[2,128,768]{2,1,0:T(8,128)}, f32[2,16,768]{2,1,0:T(8,128)}) custom-call(bf16[2,1024,768]{2,1,0:T(8,128)(2,1)} %bitcast.212, f32[16,768]{1,0:T(8,128)} %get-tuple-element.193.q_ref), custom_call_target="tpu_custom_call" | custom-call | bytes 39600000 | tf_op jit(solution)/shard_map/ema_ends/pallas_call | solution.py:191
  29.3 1.5 collective-permute-start.5
  32.7 1.3 collective-permute-start.12
  34.3 1.5 collective-permute-start.11
  36.3 1.6 collective-permute-start.7
  38.9 2.4 collective-permute-done.7
  41.3 2.7 collective-permute-start.8
  49.9 7.2 %ema_forward.2 = (bf16[2,1024,768]{2,1,0:T(8,128)(2,1)}, f32[2,1024,768]{2,1,0:T(8,128)}, f32[2,128,768]{2,1,0:T(8,128)}) custom-call(bf16[2,1024,768]{2,1,0:T(8,128)(2,1)} %bitcast.213, f32[16,768]{1,0:T(8,128)} %get-tuple-element.193.q_ref, f32[16,768]{1,0:T(8,128)} %copy-done.9, f32[1,768]{1,0:T(1,128)} %slice.330.om_ref, ...), custom_call_target="tpu_custom_call" | custom-call | bytes 21600000 | tf_op jit(solution)/shard_map/ema_forward/pallas_call | solution.py:208
  58.3 1.5 collective-permute-start.15
  59.8 12.6 %ema_forward.3 = (bf16[2,1024,768]{2,1,0:T(8,128)(2,1)}, f32[2,1024,768]{2,1,0:T(8,128)}, f32[2,128,768]{2,1,0:T(8,128)}) custom-call(bf16[2,1024,768]{2,1,0:T(8,128)(2,1)} %bitcast.214, f32[16,768]{1,0:T(8,128)} %get-tuple-element.193.q_ref, f32[16,768]{1,0:T(8,128)} %copy-done.9, ...), custom_call_target="tpu_custom_call", output_to_operand_aliasing={{0}: (6, {}), {1}: (7, {}), {2}: (8, {})} | custom-call | bytes 43200000 | tf_op jit(solution)/shard_map/ema_forward/pallas_call | solution.py:208
  72.4 1.3 collective-permute-done.15.refs_15_
  78.5 32.7 %mix_forward.1 = (f32[2048,768]{1,0:T(8,128)}, f32[2048,768]{1,0:T(8,128)}, f32[2048,1536]{1,0:T(8,128)}, f32[2048,1536]{1,0:T(8,128)}, f32[2048,128]{1,0:T(8,12...) custom-call(bf16[2048,768]{1,0:T(8,128)(2,1)} %bitcast.215, ...), custom_call_target="tpu_custom_call" | custom-call | flops 19730006016 | bytes 118800000 | tf_op jit(solution)/shard_map/mix_forward/pallas_call | solution.py:634
  113.4 1.2 collective-permute-done.26.refs_7_
  114.6 43.1 %ffn_both.1 = (bf16[2048,768]{1,0:T(8,128)(2,1)}, bf16[2048,768]{1,0:T(8,128)(2,1)}, bf16[2048,1536]{1,0:T(8,128)(2,1)}, bf16[2048,768]{1,0:T(8,128)(2,1)}, bf16...) custom-call(bf16[2048,768]{1,0:T(8,128)(2,1)} %bitcast.216, ...), custom_call_target="tpu_custom_call" | custom-call | flops 19327352832 | bytes 180000000 | tf_op jit(solution)/shard_map/ffn_both/pallas_call | solution.py:660
  157.7 8.8 %fusion.87 = f32[768,1536]{1,0:T(8,128)S(1)} fusion(bf16[2048,768]{1,0:T(8,128)(2,1)} %get-tuple-element.262, bf16[2048,1536]{1,0:T(8,128)(2,1)} %get-tuple-element.263), kind=kOutput, calls=%fused_computation.262 | convolution fusion | flops 4831838208 | bytes 14155776 | tf_op jit(solution)/shard_map/ri,rj->ij/dot_general | solution.py:23
  167.1 5.1 %fusion.85 = f32[1536,768]{1,0:T(8,128)S(1)} fusion(bf16[2048,1536]{1,0:T(8,128)(2,1)S(1)} %copy-done.42, bf16[2048,768]{1,0:T(8,128)(2,1)S(1)} %copy-done.43), kind=kOutput, calls=%fused_computation.260 | convolution fusion | flops 4831838208 | bytes 14155776 | tf_op jit(solution)/shard_map/ri,rj->ij/dot_general | solution.py:23
  172.7 7.1 %fusion.86 = f32[768,1536]{1,0:T(8,128)S(1)} fusion(bf16[768,2048]{1,0:T(8,128)(2,1)S(1)} %copy-done.45, bf16[2048,1536]{1,0:T(8,128)(2,1)} %get-tuple-element.245.dum_ref), kind=kOutput, calls=%fused_computation.261 | convolution fusion | flops 4831838208 | bytes 14155776 | tf_op jit(solution)/shard_map/dot_general | solution.py:278
  180.3 8.4 %fusion = f32[1536,768]{1,0:T(8,128)S(1)} fusion(bf16[2048,1536]{1,0:T(8,128)(2,1)} %get-tuple-element.260, bf16[2048,1536]{1,0:T(8,128)(2,1)} %get-tuple-element.245.dum_ref), kind=kOutput, calls=%fused_computation.2 | convolution fusion | flops 4831838208 | bytes 14155776 | tf_op jit(solution)/shard_map/ri,rj->ij/dot_general | solution.py:23
  190.2 1.5 collective-permute-done.30
  195.7 2.3 copy-done.2
  200.1 40.7 %mix_backward.1 = (bf16[2048,1664]{1,0:T(8,128)(2,1)}, bf16[2048,1536]{1,0:T(8,128)(2,1)}, bf16[2048,768]{1,0:T(8,128)(2,1)}, f32[2048,768]{1,0:T(8,128)}, f32[16,768]{1,0:T(8,128)}) custom-call(bf16[2048,1536]{1,0:T(8,128)(2,1)} %get-tuple-element.245.dum_ref, f32[2048,768]{1,0:T(8,128)} %get-tuple-element.246.dt_ref, ...), custom_call_target="tpu_custom_call" | custom-call | flops 19730006016 | bytes 144000000 | tf_op jit(solution)/shard_map/mix_backward/pallas_call | solution.py:690
  240.8 2.4 bitcast_add_fusion
  244.4 2.1 bitcast_add_fusion.1
  247.2 7.7 %fusion.88 = f32[768,1664]{1,0:T(8,128)S(1)} fusion(bf16[768,2048]{1,0:T(8,128)(2,1)} %get-tuple-element.261, bf16[2048,1664]{1,0:T(8,128)(2,1)S(1)} %copy-done.44), kind=kOutput, calls=%fused_computation.263 | convolution fusion | flops 5234491392 | bytes 15073280 | tf_op jit(solution)/shard_map/dot_general | solution.py:278
  254.9 1.2 fusion.2
  256.1 1.7 dynamic-slice_bitcast_fusion
  258.6 2.9 collective-permute-done.33
  262.5 12.3 %ema_back_ends.1 = (f32[2,1024,768]{2,1,0:T(8,128)}, f32[2,128,768]{2,1,0:T(8,128)}, f32[2,16,768]{2,1,0:T(8,128)}) custom-call(bf16[2,1024,768]{2,1,0:T(8,128)(2,1)} %bitcast.238, f32[2,1024,768]{2,1,0:T(8,128)} %get-tuple-element.273.p_ref, f32[16,768]{1,0:T(8,128)} %get-tuple-element.193.q_ref), custom_call_target="tpu_custom_call" | custom-call | bytes 54000000 | tf_op jit(solution)/shard_map/ema_back_ends/pallas_call | solution.py:231
  276.9 2.4 collective-permute-start.38
  279.4 7.5 %fusion.89 = f32[1536,768]{0,1:T(8,128)S(1)} fusion(bf16[2048,1536]{1,0:T(8,128)(2,1)} %get-tuple-element.284, bf16[2048,768]{1,0:T(8,128)(2,1)S(1)} %bitcast.223), kind=kOutput, calls=%fused_computation.264 | convolution fusion | flops 4831838208 | bytes 14155776 | tf_op jit(solution)/shard_map/ri,rj->ij/dot_general | solution.py:23
  287.7 1.5 convert_add_fusion
  289.4 2.2 collective-permute-done.37
  291.6 1.7 collective-permute-start.39
  293.4 1.2 collective-permute-start.42
  294.6 1.6 collective-permute-done.39
  296.3 1.4 collective-permute-start.41
  298.1 1.4 copy-done.7
  302.6 9.0 %ema_backward.6 = (bf16[2,1024,768]{2,1,0:T(8,128)(2,1)}, f32[72,768]{1,0:T(8,128)}) custom-call(f32[2,1024,768]{2,1,0:T(8,128)} %get-tuple-element.280.d_ref, bf16[2,1024,768]{2,1,0:T(8,128)(2,1)} %bitcast.217, f32[16,768]{1,0:T(8,128)} %get-tuple-element.193.q_ref, f32[16,768]{1,0:T(8,128)} %get-tuple-element.281.qi_ref, f32[16,768]{1,0:T(8,128)} %copy-done.9, ...), custom_call_target="tpu_custom_call" | custom-call | bytes 28800000 | tf_op jit(solution)/shard_map/ema_backward/pallas_call | solution.py:253
  311.6 1.3 bitcast_add_fusion.4
  314.0 2.0 collective-permute-start.43
  316.3 8.8 %ema_backward.7 = (bf16[2,1024,768]{2,1,0:T(8,128)(2,1)}, f32[72,768]{1,0:T(8,128)}) custom-call(f32[2,1024,768]{2,1,0:T(8,128)} %get-tuple-element.280.d_ref, bf16[2,1024,768]{2,1,0:T(8,128)(2,1)} %bitcast.218, f32[16,768]{1,0:T(8,128)} %get-tuple-element.193.q_ref, ...), custom_call_target="tpu_custom_call", output_to_operand_aliasing={{0}: (11, {}), {1}: (12, {})} | custom-call | bytes 28800000 | tf_op jit(solution)/shard_map/ema_backward/pallas_call | solution.py:253
  325.1 3.6 collective-permute-done.45
  329.7 1.2 bitcast_add_fusion.5
  331.7 1.4 collective-permute-start.46
  333.1 8.8 %ema_backward.8 = (bf16[2,1024,768]{2,1,0:T(8,128)(2,1)}, f32[72,768]{1,0:T(8,128)}) custom-call(f32[2,1024,768]{2,1,0:T(8,128)} %get-tuple-element.280.d_ref, bf16[2,1024,768]{2,1,0:T(8,128)(2,1)} %bitcast.219, f32[16,768]{1,0:T(8,128)} %get-tuple-element.193.q_ref, ...), custom_call_target="tpu_custom_call", output_to_operand_aliasing={{0}: (11, {}), {1}: (12, {})} | custom-call | bytes 28800000 | tf_op jit(solution)/shard_map/ema_backward/pallas_call | solution.py:253
  348.0 8.8 %ema_backward.9 = (bf16[2,1024,768]{2,1,0:T(8,128)(2,1)}, f32[72,768]{1,0:T(8,128)}) custom-call(f32[2,1024,768]{2,1,0:T(8,128)} %get-tuple-element.280.d_ref, bf16[2,1024,768]{2,1,0:T(8,128)(2,1)} %bitcast.220, f32[16,768]{1,0:T(8,128)} %get-tuple-element.193.q_ref, ...), custom_call_target="tpu_custom_call", output_to_operand_aliasing={{0}: (11, {}), {1}: (12, {})} | custom-call | bytes 28800000 | tf_op jit(solution)/shard_map/ema_backward/pallas_call | solution.py:253
  357.9 2.1 collective-permute-start.49
  360.0 1.9 collective-permute-start.51
  361.9 8.8 %ema_backward.10 = (bf16[2,1024,768]{2,1,0:T(8,128)(2,1)}, f32[72,768]{1,0:T(8,128)}) custom-call(f32[2,1024,768]{2,1,0:T(8,128)} %get-tuple-element.280.d_ref, bf16[2,1024,768]{2,1,0:T(8,128)(2,1)} %bitcast.221, f32[16,768]{1,0:T(8,128)} %get-tuple-element.193.q_ref, ...), custom_call_target="tpu_custom_call", output_to_operand_aliasing={{0}: (11, {}), {1}: (12, {})} | custom-call | bytes 28800000 | tf_op jit(solution)/shard_map/ema_backward/pallas_call | solution.py:253
  371.6 8.8 %ema_backward.11 = (bf16[2,1024,768]{2,1,0:T(8,128)(2,1)}, f32[72,768]{1,0:T(8,128)}) custom-call(f32[2,1024,768]{2,1,0:T(8,128)} %get-tuple-element.280.d_ref, bf16[2,1024,768]{2,1,0:T(8,128)(2,1)} %bitcast.222, f32[16,768]{1,0:T(8,128)} %get-tuple-element.193.q_ref, ...), custom_call_target="tpu_custom_call", output_to_operand_aliasing={{0}: (11, {}), {1}: (12, {})} | custom-call | bytes 28800000 | tf_op jit(solution)/shard_map/ema_backward/pallas_call | solution.py:253
  380.5 5.7 %collective-permute-done.51 = bf16[4,192,768]{2,1,0:T(8,128)(2,1)S(1)} collective-permute-done((bf16[4,192,768]{2,1,0:T(8,128)(2,1)S(1)}, bf16[4,192,768]{2,1,0:T(8,128)(2,1)S(1)}, u32[]{:S(2)}, u32[]{:S(2)}) %collective-permute-start.51) | collective-permute-done | bytes 1179680 | tf_op jit(solution)/shard_map/ppermute | solution.py:716
  390.0 1.3 collective-permute-start.53
  395.3 1.2 collective-permute-done.53
  396.5 2.2 collective-permute-done.54
  398.9 1.8 collective-permute-start.59
  400.7 2.1 collective-permute-start.56
  402.8 7.3 %collective-permute-done.56 = f32[136,192]{1,0:T(8,128)S(1)} collective-permute-done((f32[136,192]{1,0:T(8,128)S(1)}, f32[136,192]{1,0:T(8,128)S(1)}, u32[]{:S(2)}, u32[]{:S(2)}) %collective-permute-start.56) | collective-permute-done | bytes 104480 | tf_op jit(solution)/shard_map/ppermute | solution.py:716
  410.3 5.0 %collective-permute-done.57 = f32[136,192]{1,0:T(8,128)S(1)} collective-permute-done((f32[136,192]{1,0:T(8,128)S(1)}, f32[136,192]{1,0:T(8,128)S(1)}, u32[]{:S(2)}, u32[]{:S(2)}) %collective-permute-start.57) | collective-permute-done | bytes 104480 | tf_op jit(solution)/shard_map/ppermute | solution.py:716
  416.8 3.5 collective-permute-done.58
  429.5 1.6 pad_maximum_fusion.2
  (330 shorter events, 74.5 us)
Async XLA Ops:
  10.2 4.9 %collective-permute-start = (bf16[192,79]{0,1:T(8,128)(2,1)S(1)}, bf16[192,79]{0,1:T(8,128)(2,1)S(1)}, u32[]{:S(2)}, u32[]{:S(2)}) collective-permute-start(bf16[192,79]{0,1:T(8,128)(2,1)S(1)} %concatenate.80), channel_id=1, source_target_pairs={{0,1},{1,0},{2,3},{3,2},{4,5},{5,4},{6,7},{7,6},{8,9},{9,8},{10,11... | collective-permute-start | bytes 91016 | tf_op jit(solution)/shard_map/ppermute | solution.py:716
  10.7 6.2 %collective-permute-start.1 = (bf16[192,79]{0,1:T(8,128)(2,1)S(1)}, bf16[192,79]{0,1:T(8,128)(2,1)S(1)}, u32[]{:S(2)}, u32[]{:S(2)}) collective-permute-start(bf16[192,79]{0,1:T(8,128)(2,1)S(1)} %concatenate.80), channel_id=1, source_target_pairs={{0,2},{1,3},{2,0},{3,1},{4,6},{5,7},{6,4},{7,5},{8,10},{9,11},{10,... | collective-permute-start | bytes 91016 | tf_op jit(solution)/shard_map/ppermute | solution.py:716
  13.2 3.6 collective-permute-start.2
  13.3 15.2 %collective-permute-start.3 = (bf16[192,3200]{1,0:T(8,128)(2,1)}, bf16[192,3200]{1,0:T(8,128)(2,1)}, u32[]{:S(2)}, u32[]{:S(2)}) collective-permute-start(bf16[192,3200]{1,0:T(8,128)(2,1)} %refs_0_.2), channel_id=1, source_target_pairs={{0,1},{1,0},{2,3},{3,2},{4,5},{5,4},{6,7},{7,6},{8,9},{9,8},{10,11... | collective-permute-start | bytes 3686408 | tf_op jit(solution)/shard_map/ppermute | solution.py:716
  13.4 15.1 %collective-permute-start.4 = (bf16[192,1536]{1,0:T(8,128)(2,1)}, bf16[192,1536]{1,0:T(8,128)(2,1)S(1)}, u32[]{:S(2)}, u32[]{:S(2)}) collective-permute-start(bf16[192,1536]{1,0:T(8,128)(2,1)} %refs_6_.1), channel_id=1, source_target_pairs={{0,1},{1,0},{2,3},{3,2},{4,5},{5,4},{6,7},{7,6},{8,9},{9,8},{10,11... | collective-permute-start | bytes 1769480 | tf_op jit(solution)/shard_map/ppermute | solution.py:716
  15.1 18.9 %collective-permute-start.6 = (bf16[96,3200]{1,0:T(8,128)(2,1)S(1)}, bf16[96,3200]{1,0:T(8,128)(2,1)}, u32[]{:S(2)}, u32[]{:S(2)}) collective-permute-start(bf16[96,3200]{1,0:T(8,128)(2,1)S(1)} %constant_dynamic-slice_fusion.33), channel_id=1, source_target_pairs={{0,2},{1,3},{2,0},{3,1},{4,6},{5,7},{6,4},{7,5},{8,10},{9,11},{10,... | collective-permute-start | bytes 1843208 | tf_op jit(solution)/shard_map/ppermute | solution.py:716
  18.0 17.8 %copy-start.9 = (f32[16,768]{1,0:T(8,128)}, f32[16,768]{1,0:T(8,128)S(1)}, u32[]{:S(2)}) copy-start(f32[16,768]{1,0:T(8,128)S(1)} %get-tuple-element.194.w_ref) | copy-start | bytes 147460
  28.5 28.6 %copy-start.18 = (f32[16,768]{1,0:T(8,128)}, f32[16,768]{1,0:T(8,128)S(1)}, u32[]{:S(2)}) copy-start(f32[16,768]{1,0:T(8,128)S(1)} %get-tuple-element.447) | copy-start | bytes 147460
  28.5 28.6 %copy-start.20 = (f32[16,768]{1,0:T(8,128)}, f32[16,768]{1,0:T(8,128)S(1)}, u32[]{:S(2)}) copy-start(f32[16,768]{1,0:T(8,128)S(1)} %get-tuple-element.450) | copy-start | bytes 147460
  29.3 5.0 %collective-permute-start.5 = (f32[2,16,768]{2,1,0:T(8,128)}, f32[2,16,768]{2,1,0:T(8,128)S(1)}, u32[]{:S(2)}, u32[]{:S(2)}) collective-permute-start(f32[2,16,768]{2,1,0:T(8,128)} %get-tuple-element.187), channel_id=1, source_target_pairs={{0,4},{4,0},{8,12},{12,8},{16,20},{20,16},{24,28},{28,24},{1,5},{5... | collective-permute-start | bytes 294920 | tf_op jit(solution)/shard_map/ppermute | solution.py:716
  30.9 18.4 %collective-permute-start.9 = (bf16[96,1536]{1,0:T(8,128)(2,1)S(1)}, bf16[96,1536]{1,0:T(8,128)(2,1)}, u32[]{:S(2)}, u32[]{:S(2)}) collective-permute-start(bf16[96,1536]{1,0:T(8,128)(2,1)S(1)} %constant_dynamic-slice_fusion.32), channel_id=1, source_target_pairs={{0,2},{1,3},{2,0},{3,1},{4,6},{5,7},{6,4},{7,5},{8,10},{9,11},{10,... | collective-permute-start | bytes 884744 | tf_op jit(solution)/shard_map/ppermute | solution.py:716
  32.7 24.4 %collective-permute-start.12 = (bf16[192,768]{1,0:T(8,128)(2,1)S(1)}, bf16[192,768]{1,0:T(8,128)(2,1)}, u32[]{:S(2)}, u32[]{:S(2)}) collective-permute-start(bf16[192,768]{1,0:T(8,128)(2,1)S(1)} %constant_dynamic-slice_fusion.31), channel_id=1, source_target_pairs={{0,2},{1,3},{2,0},{3,1},{4,6},{5,7},{6,4},{7,5},{8,10},{9,11},{10,... | collective-permute-start | bytes 884744 | tf_op jit(solution)/shard_map/ppermute | solution.py:716
  34.3 15.0 %collective-permute-start.10 = (bf16[96,3200]{1,0:T(8,128)(2,1)}, bf16[96,3200]{1,0:T(8,128)(2,1)}, u32[]{:S(2)}, u32[]{:S(2)}) collective-permute-start(bf16[96,3200]{1,0:T(8,128)(2,1)} %collective-permute-done.6.refs_2_), channel_id=1, source_target_pairs={{0,1},{1,0},{2,3},{3,2},{4,5},{5,4},{6,7},{7,6},{8,9},{9,8},{10,11... | collective-permute-start | bytes 1843208 | tf_op jit(solution)/shard_map/ppermute | solution.py:716
  34.3 22.8 %collective-permute-start.11 = (bf16[96,3200]{1,0:T(8,128)(2,1)}, bf16[96,3200]{1,0:T(8,128)(2,1)}, u32[]{:S(2)}, u32[]{:S(2)}) collective-permute-start(bf16[96,3200]{1,0:T(8,128)(2,1)} %collective-permute-done.6.refs_2_), channel_id=1, source_target_pairs={{0,4},{4,0},{8,12},{12,8},{16,20},{20,16},{24,28},{28,24},{1,5},{5... | collective-permute-start | bytes 1843208 | tf_op jit(solution)/shard_map/ppermute | solution.py:716
  36.3 5.0 %collective-permute-start.7 = (f32[2,16,768]{2,1,0:T(8,128)S(1)}, f32[2,16,768]{2,1,0:T(8,128)S(1)}, u32[]{:S(2)}, u32[]{:S(2)}) collective-permute-start(f32[2,16,768]{2,1,0:T(8,128)S(1)} %add_select_fusion.7), channel_id=1, source_target_pairs={{0,8},{4,12},{8,0},{12,4},{16,24},{20,28},{24,16},{28,20},{1,9},{5... | collective-permute-start | bytes 294920 | tf_op jit(solution)/shard_map/ppermute | solution.py:716
  38.6 18.5 %copy-start.5 = (f32[80,768]{1,0:T(8,128)}, f32[80,768]{1,0:T(8,128)S(1)}, u32[]{:S(2)}) copy-start(f32[80,768]{1,0:T(8,128)S(1)} %get-tuple-element.290.k_ref) | copy-start | bytes 737284
  41.3 7.3 %collective-permute-start.8 = (f32[2,16,768]{2,1,0:T(8,128)S(1)}, f32[2,16,768]{2,1,0:T(8,128)S(1)}, u32[]{:S(2)}, u32[]{:S(2)}) collective-permute-start(f32[2,16,768]{2,1,0:T(8,128)S(1)} %add_select_fusion.6), channel_id=1, source_target_pairs={{0,16},{4,20},{8,24},{12,28},{16,0},{20,4},{24,8},{28,12},{1,17},{... | collective-permute-start | bytes 294920 | tf_op jit(solution)/shard_map/ppermute | solution.py:716
  49.3 7.8 %collective-permute-start.13 = (bf16[96,1536]{1,0:T(8,128)(2,1)}, bf16[96,1536]{1,0:T(8,128)(2,1)S(1)}, u32[]{:S(2)}, u32[]{:S(2)}) collective-permute-start(bf16[96,1536]{1,0:T(8,128)(2,1)} %collective-permute-done.9.refs_8_), channel_id=1, source_target_pairs={{0,1},{1,0},{2,3},{3,2},{4,5},{5,4},{6,7},{7,6},{8,9},{9,8},{10,11... | collective-permute-start | bytes 884744 | tf_op jit(solution)/shard_map/ppermute | solution.py:716
  57.1 16.6 %collective-permute-start.17 = (bf16[96,3200]{1,0:T(8,128)(2,1)}, bf16[96,3200]{1,0:T(8,128)(2,1)S(1)}, u32[]{:S(2)}, u32[]{:S(2)}) collective-permute-start(bf16[96,3200]{1,0:T(8,128)(2,1)} %collective-permute-done.11.refs_3_), channel_id=1, source_target_pairs={{0,1},{1,0},{2,3},{3,2},{4,5},{5,4},{6,7},{7,6},{8,9},{9,8},{10,11... | collective-permute-start | bytes 1843208 | tf_op jit(solution)/shard_map/ppermute | solution.py:716
  57.7 16.0 %collective-permute-start.18 = (bf16[384,768]{1,0:T(8,128)(2,1)S(1)}, bf16[384,768]{1,0:T(8,128)(2,1)S(1)}, u32[]{:S(2)}, u32[]{:S(2)}) collective-permute-start(bf16[384,768]{1,0:T(8,128)(2,1)S(1)} %copy-done.26), channel_id=1, source_target_pairs={{0,1},{1,0},{2,3},{3,2},{4,5},{5,4},{6,7},{7,6},{8,9},{9,8},{10,11... | collective-permute-start | bytes 1769480 | tf_op jit(solution)/shard_map/ppermute | solution.py:716
  57.8 14.6 %collective-permute-start.14 = (bf16[96,1536]{1,0:T(8,128)(2,1)}, bf16[96,1536]{1,0:T(8,128)(2,1)S(1)}, u32[]{:S(2)}, u32[]{:S(2)}) collective-permute-start(bf16[96,1536]{1,0:T(8,128)(2,1)} %collective-permute-done.9.refs_8_), channel_id=1, source_target_pairs={{0,4},{4,0},{8,12},{12,8},{16,20},{20,16},{24,28},{28,24},{1,5},{5... | collective-permute-start | bytes 884744 | tf_op jit(solution)/shard_map/ppermute | solution.py:716
  58.3 15.4 %collective-permute-start.15 = (bf16[192,768]{1,0:T(8,128)(2,1)}, bf16[192,768]{1,0:T(8,128)(2,1)S(1)}, u32[]{:S(2)}, u32[]{:S(2)}) collective-permute-start(bf16[192,768]{1,0:T(8,128)(2,1)} %collective-permute-done.12.refs_14_), channel_id=1, source_target_pairs={{0,4},{4,0},{8,12},{12,8},{16,20},{20,16},{24,28},{28,24},{1,5},{5... | collective-permute-start | bytes 884744 | tf_op jit(solution)/shard_map/ppermute | solution.py:716
  59.8 13.9 %collective-permute-start.16 = (bf16[192,768]{1,0:T(8,128)(2,1)}, bf16[192,768]{1,0:T(8,128)(2,1)S(1)}, u32[]{:S(2)}, u32[]{:S(2)}) collective-permute-start(bf16[192,768]{1,0:T(8,128)(2,1)} %collective-permute-done.12.refs_14_), channel_id=1, source_target_pairs={{0,1},{1,0},{2,3},{3,2},{4,5},{5,4},{6,7},{7,6},{8,9},{9,8},{10,11... | collective-permute-start | bytes 884744 | tf_op jit(solution)/shard_map/ppermute | solution.py:716
  73.7 3.4 collective-permute-start.19
  73.8 3.6 collective-permute-start.20
  75.0 36.2 %collective-permute-start.21 = (bf16[192,1536]{1,0:T(8,128)(2,1)}, bf16[192,1536]{1,0:T(8,128)(2,1)S(1)}, u32[]{:S(2)}, u32[]{:S(2)}) collective-permute-start(bf16[192,1536]{1,0:T(8,128)(2,1)} %refs_0_.1), channel_id=1, source_target_pairs={{0,2},{1,3},{2,0},{3,1},{4,6},{5,7},{6,4},{7,5},{8,10},{9,11},{10,... | collective-permute-start | bytes 1769480 | tf_op jit(solution)/shard_map/ppermute | solution.py:716
  76.0 35.2 %collective-permute-start.23 = (bf16[192,1536]{1,0:T(8,128)(2,1)}, bf16[192,1536]{1,0:T(8,128)(2,1)S(1)}, u32[]{:S(2)}, u32[]{:S(2)}) collective-permute-start(bf16[192,1536]{1,0:T(8,128)(2,1)} %refs_0_.1), channel_id=1, source_target_pairs={{0,1},{1,0},{2,3},{3,2},{4,5},{5,4},{6,7},{7,6},{8,9},{9,8},{10,11... | collective-permute-start | bytes 1769480 | tf_op jit(solution)/shard_map/ppermute | solution.py:716
  76.0 35.3 %collective-permute-start.22 = (bf16[384,768]{1,0:T(8,128)(2,1)}, bf16[384,768]{1,0:T(8,128)(2,1)}, u32[]{:S(2)}, u32[]{:S(2)}) collective-permute-start(bf16[384,768]{1,0:T(8,128)(2,1)} %refs_4_), channel_id=1, source_target_pairs={{0,2},{1,3},{2,0},{3,1},{4,6},{5,7},{6,4},{7,5},{8,10},{9,11},{10,... | collective-permute-start | bytes 1769480 | tf_op jit(solution)/shard_map/ppermute | solution.py:716
  77.1 34.2 %collective-permute-start.24 = (bf16[384,768]{1,0:T(8,128)(2,1)}, bf16[384,768]{1,0:T(8,128)(2,1)}, u32[]{:S(2)}, u32[]{:S(2)}) collective-permute-start(bf16[384,768]{1,0:T(8,128)(2,1)} %refs_4_), channel_id=1, source_target_pairs={{0,1},{1,0},{2,3},{3,2},{4,5},{5,4},{6,7},{7,6},{8,9},{9,8},{10,11... | collective-permute-start | bytes 1769480 | tf_op jit(solution)/shard_map/ppermute | solution.py:716
  111.3 2.1 collective-permute-start.25
  111.6 2.9 collective-permute-start.26
  166.8 22.8 %collective-permute-start.28 = (bf16[2,2,2,2,24,1536]{5,4,3,2,1,0:T(8,128)(2,1)S(1)}, bf16[2,2,2,2,24,1536]{5,4,3,2,1,0:T(8,128)(2,1)S(1)}, u32[]{:S(2)}, u32[]{:S(2)}) collective-permute-start(bf16[2,2,2,2,24,1536]{5,4,3,2,1,0:T(8,128)(2,1)S(1)} %fusion.9), channel_id=1, source_target_pairs={{0,1},{1,0},{2,3},{3,2},{4,5},{5,4},{6,7},{7,6},{8,9},{9,8},{10,11... | collective-permute-start | bytes 3538952 | tf_op jit(solution)/shard_map/ppermute | solution.py:716
  172.4 17.2 %collective-permute-start.27 = (bf16[2,2,2,2,48,768]{5,4,3,2,1,0:T(8,128)(2,1)S(1)}, bf16[2,2,2,2,48,768]{5,4,3,2,1,0:T(8,128)(2,1)S(1)}, u32[]{:S(2)}, u32[]{:S(2)}) collective-permute-start(bf16[2,2,2,2,48,768]{5,4,3,2,1,0:T(8,128)(2,1)S(1)} %fusion.3), channel_id=1, source_target_pairs={{0,1},{1,0},{2,3},{3,2},{4,5},{5,4},{6,7},{7,6},{8,9},{9,8},{10,11... | collective-permute-start | bytes 3538952 | tf_op jit(solution)/shard_map/ppermute | solution.py:716
  180.0 9.6 %collective-permute-start.31 = (bf16[2,2,2,2,24,1536]{5,4,2,1,0,3:T(8,128)(2,1)S(1)}, bf16[2,2,2,2,24,1536]{5,4,2,1,0,3:T(8,128)(2,1)S(1)}, u32[]{:S(2)}, u32[]{:S(2)}) collective-permute-start(bf16[2,2,2,2,24,1536]{5,4,2,1,0,3:T(8,128)(2,1)S(1)} %fusion.7), channel_id=1, source_target_pairs={{0,1},{1,0},{2,3},{3,2},{4,5},{5,4},{6,7},{7,6},{8,9},{9,8},{10,11... | collective-permute-start | bytes 3538952 | tf_op jit(solution)/shard_map/ppermute | solution.py:716
  188.8 2.9 collective-permute-start.30
  192.6 48.1 %collective-permute-start.32 = (bf16[2,2,2,96,768]{4,3,2,1,0:T(8,128)(2,1)S(1)}, bf16[2,2,2,96,768]{4,3,2,1,0:T(8,128)(2,1)}, u32[]{:S(2)}, u32[]{:S(2)}) collective-permute-start(bf16[2,2,2,96,768]{4,3,2,1,0:T(8,128)(2,1)S(1)} %fusion.5), channel_id=1, source_target_pairs={{0,4},{4,0},{8,12},{12,8},{16,20},{20,16},{24,28},{28,24},{1,5},{5... | collective-permute-start | bytes 3538952 | tf_op jit(solution)/shard_map/ppermute | solution.py:716
  199.1 41.6 %collective-permute-start.29 = (bf16[2,2,2,96,768]{4,3,2,1,0:T(8,128)(2,1)}, bf16[2,2,2,96,768]{4,3,2,1,0:T(8,128)(2,1)}, u32[]{:S(2)}, u32[]{:S(2)}) collective-permute-start(bf16[2,2,2,96,768]{4,3,2,1,0:T(8,128)(2,1)} %fusion.4), channel_id=1, source_target_pairs={{0,2},{1,3},{2,0},{3,1},{4,6},{5,7},{6,4},{7,5},{8,10},{9,11},{10,... | collective-permute-start | bytes 3538952 | tf_op jit(solution)/shard_map/ppermute | solution.py:716
  243.3 15.3 %collective-permute-start.34 = (bf16[2,2,96,768]{3,2,1,0:T(8,128)(2,1)S(1)}, bf16[2,2,96,768]{3,2,1,0:T(8,128)(2,1)S(1)}, u32[]{:S(2)}, u32[]{:S(2)}) collective-permute-start(bf16[2,2,96,768]{3,2,1,0:T(8,128)(2,1)S(1)} %fusion.22), channel_id=1, source_target_pairs={{0,2},{1,3},{2,0},{3,1},{4,6},{5,7},{6,4},{7,5},{8,10},{9,11},{10,... | collective-permute-start | bytes 1769480 | tf_op jit(solution)/shard_map/ppermute | solution.py:716
  246.5 14.9 %collective-permute-start.33 = (bf16[2,2,96,768]{3,2,1,0:T(8,128)(2,1)S(1)}, bf16[2,2,96,768]{3,2,1,0:T(8,128)(2,1)S(1)}, u32[]{:S(2)}, u32[]{:S(2)}) collective-permute-start(bf16[2,2,96,768]{3,2,1,0:T(8,128)(2,1)S(1)} %fusion.21), channel_id=1, source_target_pairs={{0,4},{4,0},{8,12},{12,8},{16,20},{20,16},{24,28},{28,24},{1,5},{5... | collective-permute-start | bytes 1769480 | tf_op jit(solution)/shard_map/ppermute | solution.py:716
  256.1 19.7 %collective-permute-start.36 = (bf16[2,2,2,2,24,1664]{5,4,3,2,1,0:T(8,128)(2,1)}, bf16[2,2,2,2,24,1664]{5,4,3,2,1,0:T(8,128)(2,1)}, u32[]{:S(2)}, u32[]{:S(2)}) collective-permute-start(bf16[2,2,2,2,24,1664]{5,4,3,2,1,0:T(8,128)(2,1)} %fusion.2), channel_id=1, source_target_pairs={{0,1},{1,0},{2,3},{3,2},{4,5},{5,4},{6,7},{7,6},{8,9},{9,8},{10,11... | collective-permute-start | bytes 3833864 | tf_op jit(solution)/shard_map/ppermute | solution.py:716
  261.8 14.0 %collective-permute-start.35 = (bf16[2,192,768]{2,1,0:T(8,128)(2,1)S(1)}, bf16[2,192,768]{2,1,0:T(8,128)(2,1)S(1)}, u32[]{:S(2)}, u32[]{:S(2)}) collective-permute-start(bf16[2,192,768]{2,1,0:T(8,128)(2,1)S(1)} %fusion.24), channel_id=1, source_target_pairs={{0,8},{4,12},{8,0},{12,4},{16,24},{20,28},{24,16},{28,20},{1,9},{5... | collective-permute-start | bytes 1769480 | tf_op jit(solution)/shard_map/ppermute | solution.py:716
  276.9 14.6 %collective-permute-start.38 = (bf16[192,768]{1,0:T(8,128)(2,1)S(1)}, bf16[192,768]{1,0:T(8,128)(2,1)S(1)}, u32[]{:S(2)}, u32[]{:S(2)}) collective-permute-start(bf16[192,768]{1,0:T(8,128)(2,1)S(1)} %fusion.29), channel_id=1, source_target_pairs={{0,16},{4,20},{8,24},{12,28},{16,0},{20,4},{24,8},{28,12},{1,17},{... | collective-permute-start | bytes 884744 | tf_op jit(solution)/shard_map/ppermute | solution.py:716
  286.9 4.7 %collective-permute-start.37 = (f32[2,16,768]{2,1,0:T(8,128)S(1)}, f32[2,16,768]{2,1,0:T(8,128)S(1)}, u32[]{:S(2)}, u32[]{:S(2)}) collective-permute-start(f32[2,16,768]{2,1,0:T(8,128)S(1)} %copy-done.28), channel_id=1, source_target_pairs={{0,4},{4,0},{8,12},{12,8},{16,20},{20,16},{24,28},{28,24},{1,5},{5... | collective-permute-start | bytes 294920 | tf_op jit(solution)/shard_map/ppermute | solution.py:716
  287.6 8.7 %collective-permute-start.40 = (bf16[2,2,2,2,24,1536]{5,4,2,1,0,3:T(8,128)(2,1)S(1)}, bf16[2,2,2,2,24,1536]{5,4,2,1,0,3:T(8,128)(2,1)S(1)}, u32[]{:S(2)}, u32[]{:S(2)}) collective-permute-start(bf16[2,2,2,2,24,1536]{5,4,2,1,0,3:T(8,128)(2,1)S(1)} %fusion.8), channel_id=1, source_target_pairs={{0,1},{1,0},{2,3},{3,2},{4,5},{5,4},{6,7},{7,6},{8,9},{9,8},{10,11... | collective-permute-start | bytes 3538952 | tf_op jit(solution)/shard_map/ppermute | solution.py:716
  291.6 4.7 %collective-permute-start.39 = (f32[2,16,768]{2,1,0:T(8,128)S(1)}, f32[2,16,768]{2,1,0:T(8,128)S(1)}, u32[]{:S(2)}, u32[]{:S(2)}) collective-permute-start(f32[2,16,768]{2,1,0:T(8,128)S(1)} %add_select_fusion.5), channel_id=1, source_target_pairs={{0,8},{4,12},{8,0},{12,4},{16,24},{20,28},{24,16},{28,20},{1,9},{5... | collective-permute-start | bytes 294920 | tf_op jit(solution)/shard_map/ppermute | solution.py:716
  293.4 18.2 %collective-permute-start.42 = (bf16[2,2,2,24,1664]{4,3,2,1,0:T(8,128)(2,1)S(1)}, bf16[2,2,2,24,1664]{4,3,2,1,0:T(8,128)(2,1)}, u32[]{:S(2)}, u32[]{:S(2)}) collective-permute-start(bf16[2,2,2,24,1664]{4,3,2,1,0:T(8,128)(2,1)S(1)} %fusion.15), channel_id=1, source_target_pairs={{0,2},{1,3},{2,0},{3,1},{4,6},{5,7},{6,4},{7,5},{8,10},{9,11},{10,... | collective-permute-start | bytes 1916936 | tf_op jit(solution)/shard_map/ppermute | solution.py:716
  296.3 5.6 %collective-permute-start.41 = (f32[2,16,768]{2,1,0:T(8,128)S(1)}, f32[2,16,768]{2,1,0:T(8,128)S(1)}, u32[]{:S(2)}, u32[]{:S(2)}) collective-permute-start(f32[2,16,768]{2,1,0:T(8,128)S(1)} %add_select_fusion.4), channel_id=1, source_target_pairs={{0,16},{4,20},{8,24},{12,28},{16,0},{20,4},{24,8},{28,12},{1,17},{... | collective-permute-start | bytes 294920 | tf_op jit(solution)/shard_map/ppermute | solution.py:716
  300.4 28.3 %collective-permute-start.44 = (bf16[2,2,2,24,1536]{4,3,2,1,0:T(8,128)(2,1)}, bf16[2,2,2,24,1536]{4,3,2,1,0:T(8,128)(2,1)}, u32[]{:S(2)}, u32[]{:S(2)}) collective-permute-start(bf16[2,2,2,24,1536]{4,3,2,1,0:T(8,128)(2,1)} %fusion.23), channel_id=1, source_target_pairs={{0,4},{4,0},{8,12},{12,8},{16,20},{20,16},{24,28},{28,24},{1,5},{5... | collective-permute-start | bytes 1769480 | tf_op jit(solution)/shard_map/ppermute | solution.py:716
  314.0 14.6 %collective-permute-start.43 = (bf16[2,2,24,1664]{3,2,1,0:T(8,128)(2,1)S(1)}, bf16[2,2,24,1664]{3,2,1,0:T(8,128)(2,1)S(1)}, u32[]{:S(2)}, u32[]{:S(2)}) collective-permute-start(bf16[2,2,24,1664]{3,2,1,0:T(8,128)(2,1)S(1)} %fusion.26), channel_id=1, source_target_pairs={{0,4},{4,0},{8,12},{12,8},{16,20},{20,16},{24,28},{28,24},{1,5},{5... | collective-permute-start | bytes 958472 | tf_op jit(solution)/shard_map/ppermute | solution.py:716
  316.1 12.6 %collective-permute-start.45 = (bf16[1,192,768]{2,1,0:T(8,128)(2,1)S(1)}, bf16[1,192,768]{2,1,0:T(8,128)(2,1)S(1)}, u32[]{:S(2)}, u32[]{:S(2)}) collective-permute-start(bf16[1,192,768]{2,1,0:T(8,128)(2,1)S(1)} %fusion.31), channel_id=1, source_target_pairs={{0,16},{4,20},{8,24},{12,28},{16,0},{20,4},{24,8},{28,12},{1,17},{... | collective-permute-start | bytes 884744 | tf_op jit(solution)/shard_map/ppermute | solution.py:716
  329.7 14.2 %collective-permute-start.47 = (bf16[2,192,768]{2,1,0:T(8,128)(2,1)}, bf16[2,192,768]{2,1,0:T(8,128)(2,1)}, u32[]{:S(2)}, u32[]{:S(2)}) collective-permute-start(bf16[2,192,768]{2,1,0:T(8,128)(2,1)} %pad_maximum_fusion.8), channel_id=1, source_target_pairs={{0,8},{4,12},{8,0},{12,4},{16,24},{20,28},{24,16},{28,20},{1,9},{5... | collective-permute-start | bytes 1769480 | tf_op jit(solution)/shard_map/ppermute | solution.py:716
  331.7 11.3 %collective-permute-start.46 = (bf16[2,2,24,1536]{3,2,1,0:T(8,128)(2,1)}, bf16[2,2,24,1536]{3,2,1,0:T(8,128)(2,1)}, u32[]{:S(2)}, u32[]{:S(2)}) collective-permute-start(bf16[2,2,24,1536]{3,2,1,0:T(8,128)(2,1)} %fusion.30), channel_id=1, source_target_pairs={{0,2},{1,3},{2,0},{3,1},{4,6},{5,7},{6,4},{7,5},{8,10},{9,11},{10,... | collective-permute-start | bytes 884744 | tf_op jit(solution)/shard_map/ppermute | solution.py:716
  345.6 11.2 %collective-permute-start.48 = (bf16[2,24,3200]{2,1,0:T(8,128)(2,1)}, bf16[2,24,3200]{2,1,0:T(8,128)(2,1)}, u32[]{:S(2)}, u32[]{:S(2)}) collective-permute-start(bf16[2,24,3200]{2,1,0:T(8,128)(2,1)} %fusion.27), channel_id=1, source_target_pairs={{0,8},{4,12},{8,0},{12,4},{16,24},{20,28},{24,16},{28,20},{1,9},{5... | collective-permute-start | bytes 921608 | tf_op jit(solution)/shard_map/ppermute | solution.py:716
  357.9 12.8 %collective-permute-start.49 = (bf16[24,3200]{1,0:T(8,128)(2,1)S(1)}, bf16[24,3200]{1,0:T(8,128)(2,1)S(1)}, u32[]{:S(2)}, u32[]{:S(2)}) collective-permute-start(bf16[24,3200]{1,0:T(8,128)(2,1)S(1)} %fusion.32), channel_id=1, source_target_pairs={{0,16},{4,20},{8,24},{12,28},{16,0},{20,4},{24,8},{28,12},{1,17},{... | collective-permute-start | bytes 460808 | tf_op jit(solution)/shard_map/ppermute | solution.py:716
  360.0 26.2 %collective-permute-start.51 = (bf16[4,192,768]{2,1,0:T(8,128)(2,1)S(1)}, bf16[4,192,768]{2,1,0:T(8,128)(2,1)S(1)}, u32[]{:S(2)}, u32[]{:S(2)}) collective-permute-start(bf16[4,192,768]{2,1,0:T(8,128)(2,1)S(1)} %pad_maximum_fusion.5), channel_id=1, source_target_pairs={{0,4},{4,0},{8,12},{12,8},{16,20},{20,16},{24,28},{28,24},{1,5},{5... | collective-permute-start | bytes 3538952 | tf_op jit(solution)/shard_map/ppermute | solution.py:716
  370.7 9.7 %collective-permute-start.50 = (bf16[1,24,3200]{2,1,0:T(8,128)(2,1)S(1)}, bf16[1,24,3200]{2,1,0:T(8,128)(2,1)S(1)}, u32[]{:S(2)}, u32[]{:S(2)}) collective-permute-start(bf16[1,24,3200]{2,1,0:T(8,128)(2,1)S(1)} %fusion.33), channel_id=1, source_target_pairs={{0,16},{4,20},{8,24},{12,28},{16,0},{20,4},{24,8},{28,12},{1,17},{... | collective-permute-start | bytes 460808 | tf_op jit(solution)/shard_map/ppermute | solution.py:716
  387.3 11.4 %collective-permute-start.55 = (bf16[2,24,3200]{2,1,0:T(8,128)(2,1)S(1)}, bf16[2,24,3200]{2,1,0:T(8,128)(2,1)S(1)}, u32[]{:S(2)}, u32[]{:S(2)}) collective-permute-start(bf16[2,24,3200]{2,1,0:T(8,128)(2,1)S(1)} %pad_maximum_fusion.9), channel_id=1, source_target_pairs={{0,8},{4,12},{8,0},{12,4},{16,24},{20,28},{24,16},{28,20},{1,9},{5... | collective-permute-start | bytes 921608 | tf_op jit(solution)/shard_map/ppermute | solution.py:716
  389.9 5.5 %collective-permute-start.52 = (f32[136,192]{1,0:T(8,128)S(1)}, f32[136,192]{1,0:T(8,128)S(1)}, u32[]{:S(2)}, u32[]{:S(2)}) collective-permute-start(f32[136,192]{1,0:T(8,128)S(1)} %bitcast.267), channel_id=1, source_target_pairs={{0,1},{1,0},{2,3},{3,2},{4,5},{5,4},{6,7},{7,6},{8,9},{9,8},{10,11... | collective-permute-start | bytes 313352 | tf_op jit(solution)/shard_map/ppermute | solution.py:716
  390.0 6.5 %collective-permute-start.53 = (f32[136,192]{1,0:T(8,128)S(1)}, f32[136,192]{1,0:T(8,128)S(1)}, u32[]{:S(2)}, u32[]{:S(2)}) collective-permute-start(f32[136,192]{1,0:T(8,128)S(1)} %bitcast.268), channel_id=1, source_target_pairs={{0,2},{1,3},{2,0},{3,1},{4,6},{5,7},{6,4},{7,5},{8,10},{9,11},{10,... | collective-permute-start | bytes 313352 | tf_op jit(solution)/shard_map/ppermute | solution.py:716
  391.2 7.4 %collective-permute-start.54 = (f32[136,192]{1,0:T(8,128)S(1)}, f32[136,192]{1,0:T(8,128)S(1)}, u32[]{:S(2)}, u32[]{:S(2)}) collective-permute-start(f32[136,192]{1,0:T(8,128)S(1)} %bitcast.269), channel_id=1, source_target_pairs={{0,3},{1,2},{2,1},{3,0},{4,7},{5,6},{6,5},{7,4},{8,11},{9,10},{10,... | collective-permute-start | bytes 313352 | tf_op jit(solution)/shard_map/ppermute | solution.py:716
  398.9 21.5 %collective-permute-start.59 = (bf16[4,24,3200]{2,1,0:T(8,128)(2,1)S(1)}, bf16[4,24,3200]{2,1,0:T(8,128)(2,1)S(1)}, u32[]{:S(2)}, u32[]{:S(2)}) collective-permute-start(bf16[4,24,3200]{2,1,0:T(8,128)(2,1)S(1)} %pad_maximum_fusion.7), channel_id=1, source_target_pairs={{0,4},{4,0},{8,12},{12,8},{16,20},{20,16},{24,28},{28,24},{1,5},{5... | collective-permute-start | bytes 1843208 | tf_op jit(solution)/shard_map/ppermute | solution.py:716
  400.7 9.4 %collective-permute-start.56 = (f32[136,192]{1,0:T(8,128)S(1)}, f32[136,192]{1,0:T(8,128)S(1)}, u32[]{:S(2)}, u32[]{:S(2)}) collective-permute-start(f32[136,192]{1,0:T(8,128)S(1)} %fusion.39), channel_id=1, source_target_pairs={{0,16},{4,20},{8,24},{12,28},{16,0},{20,4},{24,8},{28,12},{1,17},{... | collective-permute-start | bytes 313352 | tf_op jit(solution)/shard_map/ppermute | solution.py:716
  410.1 5.1 %collective-permute-start.57 = (f32[136,192]{1,0:T(8,128)S(1)}, f32[136,192]{1,0:T(8,128)S(1)}, u32[]{:S(2)}, u32[]{:S(2)}) collective-permute-start(f32[136,192]{1,0:T(8,128)S(1)} %add.295), channel_id=1, source_target_pairs={{0,8},{4,12},{8,0},{12,4},{16,24},{20,28},{24,16},{28,20},{1,9},{5... | collective-permute-start | bytes 313352 | tf_op jit(solution)/shard_map/ppermute | solution.py:716
  415.3 5.1 %collective-permute-start.58 = (f32[136,192]{1,0:T(8,128)S(1)}, f32[136,192]{1,0:T(8,128)S(1)}, u32[]{:S(2)}, u32[]{:S(2)}) collective-permute-start(f32[136,192]{1,0:T(8,128)S(1)} %add.296), channel_id=1, source_target_pairs={{0,4},{4,0},{8,12},{12,8},{16,20},{20,16},{24,28},{28,24},{1,5},{5... | collective-permute-start | bytes 313352 | tf_op jit(solution)/shard_map/ppermute | solution.py:716
  (42 other events, 206.6 us)

commit v3 on v2

--- a/solution.py
+++ b/solution.py
@@ -967,7 +967,7 @@
     sent, sent_2 = join(entry.send(steps[1]), sent_2)
     entry.add(steps[1], sent)
     sum_d_ = Sum(add_half(sent_2, kept_2))
-    over_d = sum_d_.send(y_step)
+    over_d = sum_d_.send(x_step)
     for step in steps[2:]:
         entry.add(step, entry.send(step))
     state_in = entry.entry
@@ -990,7 +990,7 @@
     *so_far, over_c, over_d, more = join(*so_far, over_c, over_d, more)
     sum_c.add(over_c)
     sum_d_.add(over_d)
-    over_d = sum_d_.send(x_step)
+    over_d = sum_d_.send(y_step)
     block = widen(block, more, order[0])
     more = exchange(block, "seq", order[1])
     so_far = back_part(2, so_far)

time: 440 us -> 440 us (level)
  no operation moved by 1% of the time
where the time goes in v3:
time: 440 us; the launch traced here: 432 us
  Pallas kernels  211 us (48%)
  waiting for transfers between devices  49.9 us (11%)
  starting transfers between devices  48.8 us (11%)
  matrix products  44.7 us (10%)
  local copies, waits for them, and re-layouts  43.9 us (10%)
  other arithmetic  31.3 us (7%)
    pallas_call x6, Pallas kernels, ema_backward(): pl.pallas_call(functools.partial(bwd_kernel, H, L // CH), grid=(count, G)...  53 us
    ppermute x60, waiting for transfers between devices, exchange(): lax.ppermute(value, axis, [(k, k ^ step) for k in range(lax.axis_size(axi...  49.9 us
    ppermute x60, starting transfers between devices, exchange(): lax.ppermute(value, axis, [(k, k ^ step) for k in range(lax.axis_size(axi...  48.8 us
    pallas_call x1, Pallas kernels, ffn_both(): pl.pallas_call(functools.partial(ffn_kernel, R, (D, FF, L)), grid=(T // R...  43.1 us
    pallas_call x1, Pallas kernels, mix_backward(): pl.pallas_call(functools.partial(mix_bwd_kernel, R, (D, Z, V)), grid=(T /...  40.7 us
    pallas_call x1, Pallas kernels, mix_forward(): pl.pallas_call(functools.partial(mix_fwd_kernel, R, (D, Z, V)), grid=(T /...  32.7 us
    dot_general x4, matrix products, dot_rows(): jnp.einsum('ri,rj->ij', left_op, right_op, preferred_element_type=jnp.flo...  29.9 us
    pallas_call x2, Pallas kernels, ema_forward(): pl.pallas_call(functools.partial(fwd_kernel, H, L // CH), grid=(count, G)...  19.7 us
  transfers between devices with their start and end apart: 60, of which 21 were waited for; matrix products, arithmetic and copies ran while one was open for 17% of the time, Pallas kernels for 39%

profile of v3, /device:TPU:0, one launch (start us, length us, event | category | flops | bytes accessed | tf_op | source)
XLA Modules:
  0.0 431.8 jit_solution(15356846144630773165)
XLA Ops:
  1.4 3.5 concatenate.79
  6.5 3.6 concatenate.80
  10.7 2.6 collective-permute-start.1
  15.1 1.7 collective-permute-start.6
  18.5 9.3 %ema_ends.1 = (f32[2,128,768]{2,1,0:T(8,128)}, f32[2,16,768]{2,1,0:T(8,128)}) custom-call(bf16[2,1024,768]{2,1,0:T(8,128)(2,1)} %bitcast.212, f32[16,768]{1,0:T(8,128)} %get-tuple-element.193.q_ref), custom_call_target="tpu_custom_call" | custom-call | bytes 39600000 | tf_op jit(solution)/shard_map/ema_ends/pallas_call | solution.py:191
  29.3 1.5 collective-permute-start.5
  32.7 1.3 collective-permute-start.12
  34.3 1.5 collective-permute-start.11
  36.3 1.6 collective-permute-start.7
  38.9 2.4 collective-permute-done.7
  41.3 2.7 collective-permute-start.8
  49.9 7.2 %ema_forward.2 = (bf16[2,1024,768]{2,1,0:T(8,128)(2,1)}, f32[2,1024,768]{2,1,0:T(8,128)}, f32[2,128,768]{2,1,0:T(8,128)}) custom-call(bf16[2,1024,768]{2,1,0:T(8,128)(2,1)} %bitcast.213, f32[16,768]{1,0:T(8,128)} %get-tuple-element.193.q_ref, f32[16,768]{1,0:T(8,128)} %copy-done.9, f32[1,768]{1,0:T(1,128)} %slice.330.om_ref, ...), custom_call_target="tpu_custom_call" | custom-call | bytes 21600000 | tf_op jit(solution)/shard_map/ema_forward/pallas_call | solution.py:208
  58.3 1.5 collective-permute-start.15
  59.8 12.6 %ema_forward.3 = (bf16[2,1024,768]{2,1,0:T(8,128)(2,1)}, f32[2,1024,768]{2,1,0:T(8,128)}, f32[2,128,768]{2,1,0:T(8,128)}) custom-call(bf16[2,1024,768]{2,1,0:T(8,128)(2,1)} %bitcast.214, f32[16,768]{1,0:T(8,128)} %get-tuple-element.193.q_ref, f32[16,768]{1,0:T(8,128)} %copy-done.9, ...), custom_call_target="tpu_custom_call", output_to_operand_aliasing={{0}: (6, {}), {1}: (7, {}), {2}: (8, {})} | custom-call | bytes 43200000 | tf_op jit(solution)/shard_map/ema_forward/pallas_call | solution.py:208
  72.4 1.3 collective-permute-done.15.refs_15_
  78.5 32.7 %mix_forward.1 = (f32[2048,768]{1,0:T(8,128)}, f32[2048,768]{1,0:T(8,128)}, f32[2048,1536]{1,0:T(8,128)}, f32[2048,1536]{1,0:T(8,128)}, f32[2048,128]{1,0:T(8,12...) custom-call(bf16[2048,768]{1,0:T(8,128)(2,1)} %bitcast.215, ...), custom_call_target="tpu_custom_call" | custom-call | flops 19730006016 | bytes 118800000 | tf_op jit(solution)/shard_map/mix_forward/pallas_call | solution.py:634
  113.4 1.2 collective-permute-done.26.refs_7_
  114.6 43.1 %ffn_both.1 = (bf16[2048,768]{1,0:T(8,128)(2,1)}, bf16[2048,768]{1,0:T(8,128)(2,1)}, bf16[2048,1536]{1,0:T(8,128)(2,1)}, bf16[2048,768]{1,0:T(8,128)(2,1)}, bf16...) custom-call(bf16[2048,768]{1,0:T(8,128)(2,1)} %bitcast.216, ...), custom_call_target="tpu_custom_call" | custom-call | flops 19327352832 | bytes 180000000 | tf_op jit(solution)/shard_map/ffn_both/pallas_call | solution.py:660
  157.7 8.8 %fusion.87 = f32[768,1536]{1,0:T(8,128)S(1)} fusion(bf16[2048,768]{1,0:T(8,128)(2,1)} %get-tuple-element.262, bf16[2048,1536]{1,0:T(8,128)(2,1)} %get-tuple-element.263), kind=kOutput, calls=%fused_computation.262 | convolution fusion | flops 4831838208 | bytes 14155776 | tf_op jit(solution)/shard_map/ri,rj->ij/dot_general | solution.py:23
  167.1 5.1 %fusion.85 = f32[1536,768]{1,0:T(8,128)S(1)} fusion(bf16[2048,1536]{1,0:T(8,128)(2,1)S(1)} %copy-done.42, bf16[2048,768]{1,0:T(8,128)(2,1)S(1)} %copy-done.43), kind=kOutput, calls=%fused_computation.260 | convolution fusion | flops 4831838208 | bytes 14155776 | tf_op jit(solution)/shard_map/ri,rj->ij/dot_general | solution.py:23
  172.7 7.1 %fusion.86 = f32[768,1536]{1,0:T(8,128)S(1)} fusion(bf16[768,2048]{1,0:T(8,128)(2,1)S(1)} %copy-done.45, bf16[2048,1536]{1,0:T(8,128)(2,1)} %get-tuple-element.245.dum_ref), kind=kOutput, calls=%fused_computation.261 | convolution fusion | flops 4831838208 | bytes 14155776 | tf_op jit(solution)/shard_map/dot_general | solution.py:278
  180.3 8.4 %fusion = f32[1536,768]{1,0:T(8,128)S(1)} fusion(bf16[2048,1536]{1,0:T(8,128)(2,1)} %get-tuple-element.260, bf16[2048,1536]{1,0:T(8,128)(2,1)} %get-tuple-element.245.dum_ref), kind=kOutput, calls=%fused_computation.2 | convolution fusion | flops 4831838208 | bytes 14155776 | tf_op jit(solution)/shard_map/ri,rj->ij/dot_general | solution.py:23
  190.2 1.5 collective-permute-done.30
  195.7 2.3 copy-done.2
  200.1 40.7 %mix_backward.1 = (bf16[2048,1664]{1,0:T(8,128)(2,1)}, bf16[2048,1536]{1,0:T(8,128)(2,1)}, bf16[2048,768]{1,0:T(8,128)(2,1)}, f32[2048,768]{1,0:T(8,128)}, f32[16,768]{1,0:T(8,128)}) custom-call(bf16[2048,1536]{1,0:T(8,128)(2,1)} %get-tuple-element.245.dum_ref, f32[2048,768]{1,0:T(8,128)} %get-tuple-element.246.dt_ref, ...), custom_call_target="tpu_custom_call" | custom-call | flops 19730006016 | bytes 144000000 | tf_op jit(solution)/shard_map/mix_backward/pallas_call | solution.py:690
  240.8 2.4 bitcast_add_fusion
  244.4 2.1 bitcast_add_fusion.1
  247.2 7.7 %fusion.88 = f32[768,1664]{1,0:T(8,128)S(1)} fusion(bf16[768,2048]{1,0:T(8,128)(2,1)} %get-tuple-element.261, bf16[2048,1664]{1,0:T(8,128)(2,1)S(1)} %copy-done.44), kind=kOutput, calls=%fused_computation.263 | convolution fusion | flops 5234491392 | bytes 15073280 | tf_op jit(solution)/shard_map/dot_general | solution.py:278
  254.9 1.2 fusion.2
  256.1 1.7 dynamic-slice_bitcast_fusion
  258.6 2.9 collective-permute-done.33
  262.5 12.3 %ema_back_ends.1 = (f32[2,1024,768]{2,1,0:T(8,128)}, f32[2,128,768]{2,1,0:T(8,128)}, f32[2,16,768]{2,1,0:T(8,128)}) custom-call(bf16[2,1024,768]{2,1,0:T(8,128)(2,1)} %bitcast.238, f32[2,1024,768]{2,1,0:T(8,128)} %get-tuple-element.273.p_ref, f32[16,768]{1,0:T(8,128)} %get-tuple-element.193.q_ref), custom_call_target="tpu_custom_call" | custom-call | bytes 54000000 | tf_op jit(solution)/shard_map/ema_back_ends/pallas_call | solution.py:231
  276.9 2.4 collective-permute-start.38
  279.4 7.5 %fusion.89 = f32[1536,768]{0,1:T(8,128)S(1)} fusion(bf16[2048,1536]{1,0:T(8,128)(2,1)} %get-tuple-element.284, bf16[2048,768]{1,0:T(8,128)(2,1)S(1)} %bitcast.223), kind=kOutput, calls=%fused_computation.264 | convolution fusion | flops 4831838208 | bytes 14155776 | tf_op jit(solution)/shard_map/ri,rj->ij/dot_general | solution.py:23
  287.7 1.5 convert_add_fusion
  289.4 2.2 collective-permute-done.37
  291.6 1.7 collective-permute-start.39
  293.4 1.2 collective-permute-start.42
  294.6 1.6 collective-permute-done.39
  296.3 1.4 collective-permute-start.41
  298.1 1.4 copy-done.7
  300.4 1.3 collective-permute-start.44
  302.6 9.0 %ema_backward.6 = (bf16[2,1024,768]{2,1,0:T(8,128)(2,1)}, f32[72,768]{1,0:T(8,128)}) custom-call(f32[2,1024,768]{2,1,0:T(8,128)} %get-tuple-element.280.d_ref, bf16[2,1024,768]{2,1,0:T(8,128)(2,1)} %bitcast.217, f32[16,768]{1,0:T(8,128)} %get-tuple-element.193.q_ref, f32[16,768]{1,0:T(8,128)} %get-tuple-element.281.qi_ref, f32[16,768]{1,0:T(8,128)} %copy-done.9, ...), custom_call_target="tpu_custom_call" | custom-call | bytes 28800000 | tf_op jit(solution)/shard_map/ema_backward/pallas_call | solution.py:253
  311.6 1.3 bitcast_add_fusion.4
  314.0 2.0 collective-permute-start.43
  316.1 8.8 %ema_backward.7 = (bf16[2,1024,768]{2,1,0:T(8,128)(2,1)}, f32[72,768]{1,0:T(8,128)}) custom-call(f32[2,1024,768]{2,1,0:T(8,128)} %get-tuple-element.280.d_ref, bf16[2,1024,768]{2,1,0:T(8,128)(2,1)} %bitcast.218, f32[16,768]{1,0:T(8,128)} %get-tuple-element.193.q_ref, ...), custom_call_target="tpu_custom_call", output_to_operand_aliasing={{0}: (11, {}), {1}: (12, {})} | custom-call | bytes 28800000 | tf_op jit(solution)/shard_map/ema_backward/pallas_call | solution.py:253
  324.9 3.6 collective-permute-done.45
  329.6 1.2 bitcast_add_fusion.5
  331.6 1.5 collective-permute-start.46
  333.1 8.8 %ema_backward.8 = (bf16[2,1024,768]{2,1,0:T(8,128)(2,1)}, f32[72,768]{1,0:T(8,128)}) custom-call(f32[2,1024,768]{2,1,0:T(8,128)} %get-tuple-element.280.d_ref, bf16[2,1024,768]{2,1,0:T(8,128)(2,1)} %bitcast.219, f32[16,768]{1,0:T(8,128)} %get-tuple-element.193.q_ref, ...), custom_call_target="tpu_custom_call", output_to_operand_aliasing={{0}: (11, {}), {1}: (12, {})} | custom-call | bytes 28800000 | tf_op jit(solution)/shard_map/ema_backward/pallas_call | solution.py:253
  348.0 8.8 %ema_backward.9 = (bf16[2,1024,768]{2,1,0:T(8,128)(2,1)}, f32[72,768]{1,0:T(8,128)}) custom-call(f32[2,1024,768]{2,1,0:T(8,128)} %get-tuple-element.280.d_ref, bf16[2,1024,768]{2,1,0:T(8,128)(2,1)} %bitcast.220, f32[16,768]{1,0:T(8,128)} %get-tuple-element.193.q_ref, ...), custom_call_target="tpu_custom_call", output_to_operand_aliasing={{0}: (11, {}), {1}: (12, {})} | custom-call | bytes 28800000 | tf_op jit(solution)/shard_map/ema_backward/pallas_call | solution.py:253
  357.9 3.4 collective-permute-start.49
  361.5 8.8 %ema_backward.10 = (bf16[2,1024,768]{2,1,0:T(8,128)(2,1)}, f32[72,768]{1,0:T(8,128)}) custom-call(f32[2,1024,768]{2,1,0:T(8,128)} %get-tuple-element.280.d_ref, bf16[2,1024,768]{2,1,0:T(8,128)(2,1)} %bitcast.221, f32[16,768]{1,0:T(8,128)} %get-tuple-element.193.q_ref, ...), custom_call_target="tpu_custom_call", output_to_operand_aliasing={{0}: (11, {}), {1}: (12, {})} | custom-call | bytes 28800000 | tf_op jit(solution)/shard_map/ema_backward/pallas_call | solution.py:253
  370.6 8.8 %ema_backward.11 = (bf16[2,1024,768]{2,1,0:T(8,128)(2,1)}, f32[72,768]{1,0:T(8,128)}) custom-call(f32[2,1024,768]{2,1,0:T(8,128)} %get-tuple-element.280.d_ref, bf16[2,1024,768]{2,1,0:T(8,128)(2,1)} %bitcast.222, f32[16,768]{1,0:T(8,128)} %get-tuple-element.193.q_ref, ...), custom_call_target="tpu_custom_call", output_to_operand_aliasing={{0}: (11, {}), {1}: (12, {})} | custom-call | bytes 28800000 | tf_op jit(solution)/shard_map/ema_backward/pallas_call | solution.py:253
  379.5 8.4 %collective-permute-done.51 = bf16[4,192,768]{2,1,0:T(8,128)(2,1)S(1)} collective-permute-done((bf16[4,192,768]{2,1,0:T(8,128)(2,1)S(1)}, bf16[4,192,768]{2,1,0:T(8,128)(2,1)S(1)}, u32[]{:S(2)}, u32[]{:S(2)}) %collective-permute-start.51) | collective-permute-done | bytes 1179680 | tf_op jit(solution)/shard_map/ppermute | solution.py:716
  394.6 1.2 fusion.73
  395.8 1.2 fusion.74
  397.0 1.2 collective-permute-done.53
  398.2 2.2 collective-permute-done.54
  401.3 9.0 %collective-permute-done.56 = f32[136,192]{1,0:T(8,128)S(1)} collective-permute-done((f32[136,192]{1,0:T(8,128)S(1)}, f32[136,192]{1,0:T(8,128)S(1)}, u32[]{:S(2)}, u32[]{:S(2)}) %collective-permute-start.56) | collective-permute-done | bytes 104480 | tf_op jit(solution)/shard_map/ppermute | solution.py:716
  410.6 5.0 %collective-permute-done.57 = f32[136,192]{1,0:T(8,128)S(1)} collective-permute-done((f32[136,192]{1,0:T(8,128)S(1)}, f32[136,192]{1,0:T(8,128)S(1)}, u32[]{:S(2)}, u32[]{:S(2)}) %collective-permute-start.57) | collective-permute-done | bytes 104480 | tf_op jit(solution)/shard_map/ppermute | solution.py:716
  415.5 1.7 collective-permute-start.58
  418.4 2.2 collective-permute-done.58
  429.8 1.6 pad_maximum_fusion.2
  (330 shorter events, 71.9 us)
Async XLA Ops:
  10.2 4.9 %collective-permute-start = (bf16[192,79]{0,1:T(8,128)(2,1)S(1)}, bf16[192,79]{0,1:T(8,128)(2,1)S(1)}, u32[]{:S(2)}, u32[]{:S(2)}) collective-permute-start(bf16[192,79]{0,1:T(8,128)(2,1)S(1)} %concatenate.80), channel_id=1, source_target_pairs={{0,1},{1,0},{2,3},{3,2},{4,5},{5,4},{6,7},{7,6},{8,9},{9,8},{10,11... | collective-permute-start | bytes 91016 | tf_op jit(solution)/shard_map/ppermute | solution.py:716
  10.7 6.2 %collective-permute-start.1 = (bf16[192,79]{0,1:T(8,128)(2,1)S(1)}, bf16[192,79]{0,1:T(8,128)(2,1)S(1)}, u32[]{:S(2)}, u32[]{:S(2)}) collective-permute-start(bf16[192,79]{0,1:T(8,128)(2,1)S(1)} %concatenate.80), channel_id=1, source_target_pairs={{0,2},{1,3},{2,0},{3,1},{4,6},{5,7},{6,4},{7,5},{8,10},{9,11},{10,... | collective-permute-start | bytes 91016 | tf_op jit(solution)/shard_map/ppermute | solution.py:716
  13.2 3.6 collective-permute-start.2
  13.3 15.2 %collective-permute-start.3 = (bf16[192,3200]{1,0:T(8,128)(2,1)}, bf16[192,3200]{1,0:T(8,128)(2,1)}, u32[]{:S(2)}, u32[]{:S(2)}) collective-permute-start(bf16[192,3200]{1,0:T(8,128)(2,1)} %refs_0_.2), channel_id=1, source_target_pairs={{0,1},{1,0},{2,3},{3,2},{4,5},{5,4},{6,7},{7,6},{8,9},{9,8},{10,11... | collective-permute-start | bytes 3686408 | tf_op jit(solution)/shard_map/ppermute | solution.py:716
  13.4 15.1 %collective-permute-start.4 = (bf16[192,1536]{1,0:T(8,128)(2,1)}, bf16[192,1536]{1,0:T(8,128)(2,1)S(1)}, u32[]{:S(2)}, u32[]{:S(2)}) collective-permute-start(bf16[192,1536]{1,0:T(8,128)(2,1)} %refs_6_.1), channel_id=1, source_target_pairs={{0,1},{1,0},{2,3},{3,2},{4,5},{5,4},{6,7},{7,6},{8,9},{9,8},{10,11... | collective-permute-start | bytes 1769480 | tf_op jit(solution)/shard_map/ppermute | solution.py:716
  15.1 18.9 %collective-permute-start.6 = (bf16[96,3200]{1,0:T(8,128)(2,1)S(1)}, bf16[96,3200]{1,0:T(8,128)(2,1)}, u32[]{:S(2)}, u32[]{:S(2)}) collective-permute-start(bf16[96,3200]{1,0:T(8,128)(2,1)S(1)} %constant_dynamic-slice_fusion.33), channel_id=1, source_target_pairs={{0,2},{1,3},{2,0},{3,1},{4,6},{5,7},{6,4},{7,5},{8,10},{9,11},{10,... | collective-permute-start | bytes 1843208 | tf_op jit(solution)/shard_map/ppermute | solution.py:716
  18.0 17.8 %copy-start.9 = (f32[16,768]{1,0:T(8,128)}, f32[16,768]{1,0:T(8,128)S(1)}, u32[]{:S(2)}) copy-start(f32[16,768]{1,0:T(8,128)S(1)} %get-tuple-element.194.w_ref) | copy-start | bytes 147460
  28.5 28.6 %copy-start.18 = (f32[16,768]{1,0:T(8,128)}, f32[16,768]{1,0:T(8,128)S(1)}, u32[]{:S(2)}) copy-start(f32[16,768]{1,0:T(8,128)S(1)} %get-tuple-element.447) | copy-start | bytes 147460
  28.5 28.6 %copy-start.20 = (f32[16,768]{1,0:T(8,128)}, f32[16,768]{1,0:T(8,128)S(1)}, u32[]{:S(2)}) copy-start(f32[16,768]{1,0:T(8,128)S(1)} %get-tuple-element.450) | copy-start | bytes 147460
  29.3 5.0 %collective-permute-start.5 = (f32[2,16,768]{2,1,0:T(8,128)}, f32[2,16,768]{2,1,0:T(8,128)S(1)}, u32[]{:S(2)}, u32[]{:S(2)}) collective-permute-start(f32[2,16,768]{2,1,0:T(8,128)} %get-tuple-element.187), channel_id=1, source_target_pairs={{0,4},{4,0},{8,12},{12,8},{16,20},{20,16},{24,28},{28,24},{1,5},{5... | collective-permute-start | bytes 294920 | tf_op jit(solution)/shard_map/ppermute | solution.py:716
  30.9 18.4 %collective-permute-start.9 = (bf16[96,1536]{1,0:T(8,128)(2,1)S(1)}, bf16[96,1536]{1,0:T(8,128)(2,1)}, u32[]{:S(2)}, u32[]{:S(2)}) collective-permute-start(bf16[96,1536]{1,0:T(8,128)(2,1)S(1)} %constant_dynamic-slice_fusion.32), channel_id=1, source_target_pairs={{0,2},{1,3},{2,0},{3,1},{4,6},{5,7},{6,4},{7,5},{8,10},{9,11},{10,... | collective-permute-start | bytes 884744 | tf_op jit(solution)/shard_map/ppermute | solution.py:716
  32.7 24.4 %collective-permute-start.12 = (bf16[192,768]{1,0:T(8,128)(2,1)S(1)}, bf16[192,768]{1,0:T(8,128)(2,1)}, u32[]{:S(2)}, u32[]{:S(2)}) collective-permute-start(bf16[192,768]{1,0:T(8,128)(2,1)S(1)} %constant_dynamic-slice_fusion.31), channel_id=1, source_target_pairs={{0,2},{1,3},{2,0},{3,1},{4,6},{5,7},{6,4},{7,5},{8,10},{9,11},{10,... | collective-permute-start | bytes 884744 | tf_op jit(solution)/shard_map/ppermute | solution.py:716
  34.3 15.0 %collective-permute-start.10 = (bf16[96,3200]{1,0:T(8,128)(2,1)}, bf16[96,3200]{1,0:T(8,128)(2,1)}, u32[]{:S(2)}, u32[]{:S(2)}) collective-permute-start(bf16[96,3200]{1,0:T(8,128)(2,1)} %collective-permute-done.6.refs_2_), channel_id=1, source_target_pairs={{0,1},{1,0},{2,3},{3,2},{4,5},{5,4},{6,7},{7,6},{8,9},{9,8},{10,11... | collective-permute-start | bytes 1843208 | tf_op jit(solution)/shard_map/ppermute | solution.py:716
  34.3 22.8 %collective-permute-start.11 = (bf16[96,3200]{1,0:T(8,128)(2,1)}, bf16[96,3200]{1,0:T(8,128)(2,1)}, u32[]{:S(2)}, u32[]{:S(2)}) collective-permute-start(bf16[96,3200]{1,0:T(8,128)(2,1)} %collective-permute-done.6.refs_2_), channel_id=1, source_target_pairs={{0,4},{4,0},{8,12},{12,8},{16,20},{20,16},{24,28},{28,24},{1,5},{5... | collective-permute-start | bytes 1843208 | tf_op jit(solution)/shard_map/ppermute | solution.py:716
  36.3 5.0 %collective-permute-start.7 = (f32[2,16,768]{2,1,0:T(8,128)S(1)}, f32[2,16,768]{2,1,0:T(8,128)S(1)}, u32[]{:S(2)}, u32[]{:S(2)}) collective-permute-start(f32[2,16,768]{2,1,0:T(8,128)S(1)} %add_select_fusion.7), channel_id=1, source_target_pairs={{0,8},{4,12},{8,0},{12,4},{16,24},{20,28},{24,16},{28,20},{1,9},{5... | collective-permute-start | bytes 294920 | tf_op jit(solution)/shard_map/ppermute | solution.py:716
  38.6 18.5 %copy-start.5 = (f32[80,768]{1,0:T(8,128)}, f32[80,768]{1,0:T(8,128)S(1)}, u32[]{:S(2)}) copy-start(f32[80,768]{1,0:T(8,128)S(1)} %get-tuple-element.290.k_ref) | copy-start | bytes 737284
  41.3 7.3 %collective-permute-start.8 = (f32[2,16,768]{2,1,0:T(8,128)S(1)}, f32[2,16,768]{2,1,0:T(8,128)S(1)}, u32[]{:S(2)}, u32[]{:S(2)}) collective-permute-start(f32[2,16,768]{2,1,0:T(8,128)S(1)} %add_select_fusion.6), channel_id=1, source_target_pairs={{0,16},{4,20},{8,24},{12,28},{16,0},{20,4},{24,8},{28,12},{1,17},{... | collective-permute-start | bytes 294920 | tf_op jit(solution)/shard_map/ppermute | solution.py:716
  49.3 7.8 %collective-permute-start.13 = (bf16[96,1536]{1,0:T(8,128)(2,1)}, bf16[96,1536]{1,0:T(8,128)(2,1)S(1)}, u32[]{:S(2)}, u32[]{:S(2)}) collective-permute-start(bf16[96,1536]{1,0:T(8,128)(2,1)} %collective-permute-done.9.refs_8_), channel_id=1, source_target_pairs={{0,1},{1,0},{2,3},{3,2},{4,5},{5,4},{6,7},{7,6},{8,9},{9,8},{10,11... | collective-permute-start | bytes 884744 | tf_op jit(solution)/shard_map/ppermute | solution.py:716
  57.1 16.6 %collective-permute-start.17 = (bf16[96,3200]{1,0:T(8,128)(2,1)}, bf16[96,3200]{1,0:T(8,128)(2,1)S(1)}, u32[]{:S(2)}, u32[]{:S(2)}) collective-permute-start(bf16[96,3200]{1,0:T(8,128)(2,1)} %collective-permute-done.11.refs_3_), channel_id=1, source_target_pairs={{0,1},{1,0},{2,3},{3,2},{4,5},{5,4},{6,7},{7,6},{8,9},{9,8},{10,11... | collective-permute-start | bytes 1843208 | tf_op jit(solution)/shard_map/ppermute | solution.py:716
  57.7 16.0 %collective-permute-start.18 = (bf16[384,768]{1,0:T(8,128)(2,1)S(1)}, bf16[384,768]{1,0:T(8,128)(2,1)S(1)}, u32[]{:S(2)}, u32[]{:S(2)}) collective-permute-start(bf16[384,768]{1,0:T(8,128)(2,1)S(1)} %copy-done.26), channel_id=1, source_target_pairs={{0,1},{1,0},{2,3},{3,2},{4,5},{5,4},{6,7},{7,6},{8,9},{9,8},{10,11... | collective-permute-start | bytes 1769480 | tf_op jit(solution)/shard_map/ppermute | solution.py:716
  57.8 14.6 %collective-permute-start.14 = (bf16[96,1536]{1,0:T(8,128)(2,1)}, bf16[96,1536]{1,0:T(8,128)(2,1)S(1)}, u32[]{:S(2)}, u32[]{:S(2)}) collective-permute-start(bf16[96,1536]{1,0:T(8,128)(2,1)} %collective-permute-done.9.refs_8_), channel_id=1, source_target_pairs={{0,4},{4,0},{8,12},{12,8},{16,20},{20,16},{24,28},{28,24},{1,5},{5... | collective-permute-start | bytes 884744 | tf_op jit(solution)/shard_map/ppermute | solution.py:716
  58.3 15.4 %collective-permute-start.15 = (bf16[192,768]{1,0:T(8,128)(2,1)}, bf16[192,768]{1,0:T(8,128)(2,1)S(1)}, u32[]{:S(2)}, u32[]{:S(2)}) collective-permute-start(bf16[192,768]{1,0:T(8,128)(2,1)} %collective-permute-done.12.refs_14_), channel_id=1, source_target_pairs={{0,4},{4,0},{8,12},{12,8},{16,20},{20,16},{24,28},{28,24},{1,5},{5... | collective-permute-start | bytes 884744 | tf_op jit(solution)/shard_map/ppermute | solution.py:716
  59.8 13.9 %collective-permute-start.16 = (bf16[192,768]{1,0:T(8,128)(2,1)}, bf16[192,768]{1,0:T(8,128)(2,1)S(1)}, u32[]{:S(2)}, u32[]{:S(2)}) collective-permute-start(bf16[192,768]{1,0:T(8,128)(2,1)} %collective-permute-done.12.refs_14_), channel_id=1, source_target_pairs={{0,1},{1,0},{2,3},{3,2},{4,5},{5,4},{6,7},{7,6},{8,9},{9,8},{10,11... | collective-permute-start | bytes 884744 | tf_op jit(solution)/shard_map/ppermute | solution.py:716
  73.7 3.4 collective-permute-start.19
  73.8 3.6 collective-permute-start.20
  75.0 36.2 %collective-permute-start.21 = (bf16[192,1536]{1,0:T(8,128)(2,1)}, bf16[192,1536]{1,0:T(8,128)(2,1)S(1)}, u32[]{:S(2)}, u32[]{:S(2)}) collective-permute-start(bf16[192,1536]{1,0:T(8,128)(2,1)} %refs_0_.1), channel_id=1, source_target_pairs={{0,2},{1,3},{2,0},{3,1},{4,6},{5,7},{6,4},{7,5},{8,10},{9,11},{10,... | collective-permute-start | bytes 1769480 | tf_op jit(solution)/shard_map/ppermute | solution.py:716
  76.0 35.2 %collective-permute-start.23 = (bf16[192,1536]{1,0:T(8,128)(2,1)}, bf16[192,1536]{1,0:T(8,128)(2,1)S(1)}, u32[]{:S(2)}, u32[]{:S(2)}) collective-permute-start(bf16[192,1536]{1,0:T(8,128)(2,1)} %refs_0_.1), channel_id=1, source_target_pairs={{0,1},{1,0},{2,3},{3,2},{4,5},{5,4},{6,7},{7,6},{8,9},{9,8},{10,11... | collective-permute-start | bytes 1769480 | tf_op jit(solution)/shard_map/ppermute | solution.py:716
  76.0 35.3 %collective-permute-start.22 = (bf16[384,768]{1,0:T(8,128)(2,1)}, bf16[384,768]{1,0:T(8,128)(2,1)}, u32[]{:S(2)}, u32[]{:S(2)}) collective-permute-start(bf16[384,768]{1,0:T(8,128)(2,1)} %refs_4_), channel_id=1, source_target_pairs={{0,2},{1,3},{2,0},{3,1},{4,6},{5,7},{6,4},{7,5},{8,10},{9,11},{10,... | collective-permute-start | bytes 1769480 | tf_op jit(solution)/shard_map/ppermute | solution.py:716
  77.1 34.2 %collective-permute-start.24 = (bf16[384,768]{1,0:T(8,128)(2,1)}, bf16[384,768]{1,0:T(8,128)(2,1)}, u32[]{:S(2)}, u32[]{:S(2)}) collective-permute-start(bf16[384,768]{1,0:T(8,128)(2,1)} %refs_4_), channel_id=1, source_target_pairs={{0,1},{1,0},{2,3},{3,2},{4,5},{5,4},{6,7},{7,6},{8,9},{9,8},{10,11... | collective-permute-start | bytes 1769480 | tf_op jit(solution)/shard_map/ppermute | solution.py:716
  111.3 2.1 collective-permute-start.25
  111.6 2.9 collective-permute-start.26
  166.8 22.8 %collective-permute-start.28 = (bf16[2,2,2,2,24,1536]{5,4,3,2,1,0:T(8,128)(2,1)S(1)}, bf16[2,2,2,2,24,1536]{5,4,3,2,1,0:T(8,128)(2,1)S(1)}, u32[]{:S(2)}, u32[]{:S(2)}) collective-permute-start(bf16[2,2,2,2,24,1536]{5,4,3,2,1,0:T(8,128)(2,1)S(1)} %fusion.9), channel_id=1, source_target_pairs={{0,1},{1,0},{2,3},{3,2},{4,5},{5,4},{6,7},{7,6},{8,9},{9,8},{10,11... | collective-permute-start | bytes 3538952 | tf_op jit(solution)/shard_map/ppermute | solution.py:716
  172.4 17.2 %collective-permute-start.27 = (bf16[2,2,2,2,48,768]{5,4,3,2,1,0:T(8,128)(2,1)S(1)}, bf16[2,2,2,2,48,768]{5,4,3,2,1,0:T(8,128)(2,1)S(1)}, u32[]{:S(2)}, u32[]{:S(2)}) collective-permute-start(bf16[2,2,2,2,48,768]{5,4,3,2,1,0:T(8,128)(2,1)S(1)} %fusion.3), channel_id=1, source_target_pairs={{0,1},{1,0},{2,3},{3,2},{4,5},{5,4},{6,7},{7,6},{8,9},{9,8},{10,11... | collective-permute-start | bytes 3538952 | tf_op jit(solution)/shard_map/ppermute | solution.py:716
  180.0 9.6 %collective-permute-start.31 = (bf16[2,2,2,2,24,1536]{5,4,2,1,0,3:T(8,128)(2,1)S(1)}, bf16[2,2,2,2,24,1536]{5,4,2,1,0,3:T(8,128)(2,1)S(1)}, u32[]{:S(2)}, u32[]{:S(2)}) collective-permute-start(bf16[2,2,2,2,24,1536]{5,4,2,1,0,3:T(8,128)(2,1)S(1)} %fusion.7), channel_id=1, source_target_pairs={{0,1},{1,0},{2,3},{3,2},{4,5},{5,4},{6,7},{7,6},{8,9},{9,8},{10,11... | collective-permute-start | bytes 3538952 | tf_op jit(solution)/shard_map/ppermute | solution.py:716
  188.8 2.9 collective-permute-start.30
  192.6 48.1 %collective-permute-start.32 = (bf16[2,2,2,96,768]{4,3,2,1,0:T(8,128)(2,1)S(1)}, bf16[2,2,2,96,768]{4,3,2,1,0:T(8,128)(2,1)}, u32[]{:S(2)}, u32[]{:S(2)}) collective-permute-start(bf16[2,2,2,96,768]{4,3,2,1,0:T(8,128)(2,1)S(1)} %fusion.5), channel_id=1, source_target_pairs={{0,4},{4,0},{8,12},{12,8},{16,20},{20,16},{24,28},{28,24},{1,5},{5... | collective-permute-start | bytes 3538952 | tf_op jit(solution)/shard_map/ppermute | solution.py:716
  199.1 41.6 %collective-permute-start.29 = (bf16[2,2,2,96,768]{4,3,2,1,0:T(8,128)(2,1)}, bf16[2,2,2,96,768]{4,3,2,1,0:T(8,128)(2,1)}, u32[]{:S(2)}, u32[]{:S(2)}) collective-permute-start(bf16[2,2,2,96,768]{4,3,2,1,0:T(8,128)(2,1)} %fusion.4), channel_id=1, source_target_pairs={{0,2},{1,3},{2,0},{3,1},{4,6},{5,7},{6,4},{7,5},{8,10},{9,11},{10,... | collective-permute-start | bytes 3538952 | tf_op jit(solution)/shard_map/ppermute | solution.py:716
  243.3 15.3 %collective-permute-start.34 = (bf16[2,2,96,768]{3,2,1,0:T(8,128)(2,1)S(1)}, bf16[2,2,96,768]{3,2,1,0:T(8,128)(2,1)S(1)}, u32[]{:S(2)}, u32[]{:S(2)}) collective-permute-start(bf16[2,2,96,768]{3,2,1,0:T(8,128)(2,1)S(1)} %fusion.22), channel_id=1, source_target_pairs={{0,2},{1,3},{2,0},{3,1},{4,6},{5,7},{6,4},{7,5},{8,10},{9,11},{10,... | collective-permute-start | bytes 1769480 | tf_op jit(solution)/shard_map/ppermute | solution.py:716
  246.5 14.9 %collective-permute-start.33 = (bf16[2,2,96,768]{3,2,1,0:T(8,128)(2,1)S(1)}, bf16[2,2,96,768]{3,2,1,0:T(8,128)(2,1)S(1)}, u32[]{:S(2)}, u32[]{:S(2)}) collective-permute-start(bf16[2,2,96,768]{3,2,1,0:T(8,128)(2,1)S(1)} %fusion.21), channel_id=1, source_target_pairs={{0,4},{4,0},{8,12},{12,8},{16,20},{20,16},{24,28},{28,24},{1,5},{5... | collective-permute-start | bytes 1769480 | tf_op jit(solution)/shard_map/ppermute | solution.py:716
  256.1 19.7 %collective-permute-start.36 = (bf16[2,2,2,2,24,1664]{5,4,3,2,1,0:T(8,128)(2,1)}, bf16[2,2,2,2,24,1664]{5,4,3,2,1,0:T(8,128)(2,1)}, u32[]{:S(2)}, u32[]{:S(2)}) collective-permute-start(bf16[2,2,2,2,24,1664]{5,4,3,2,1,0:T(8,128)(2,1)} %fusion.2), channel_id=1, source_target_pairs={{0,1},{1,0},{2,3},{3,2},{4,5},{5,4},{6,7},{7,6},{8,9},{9,8},{10,11... | collective-permute-start | bytes 3833864 | tf_op jit(solution)/shard_map/ppermute | solution.py:716
  261.8 14.0 %collective-permute-start.35 = (bf16[2,192,768]{2,1,0:T(8,128)(2,1)S(1)}, bf16[2,192,768]{2,1,0:T(8,128)(2,1)S(1)}, u32[]{:S(2)}, u32[]{:S(2)}) collective-permute-start(bf16[2,192,768]{2,1,0:T(8,128)(2,1)S(1)} %fusion.24), channel_id=1, source_target_pairs={{0,8},{4,12},{8,0},{12,4},{16,24},{20,28},{24,16},{28,20},{1,9},{5... | collective-permute-start | bytes 1769480 | tf_op jit(solution)/shard_map/ppermute | solution.py:716
  276.9 14.6 %collective-permute-start.38 = (bf16[192,768]{1,0:T(8,128)(2,1)S(1)}, bf16[192,768]{1,0:T(8,128)(2,1)S(1)}, u32[]{:S(2)}, u32[]{:S(2)}) collective-permute-start(bf16[192,768]{1,0:T(8,128)(2,1)S(1)} %fusion.29), channel_id=1, source_target_pairs={{0,16},{4,20},{8,24},{12,28},{16,0},{20,4},{24,8},{28,12},{1,17},{... | collective-permute-start | bytes 884744 | tf_op jit(solution)/shard_map/ppermute | solution.py:716
  286.9 4.7 %collective-permute-start.37 = (f32[2,16,768]{2,1,0:T(8,128)S(1)}, f32[2,16,768]{2,1,0:T(8,128)S(1)}, u32[]{:S(2)}, u32[]{:S(2)}) collective-permute-start(f32[2,16,768]{2,1,0:T(8,128)S(1)} %copy-done.28), channel_id=1, source_target_pairs={{0,4},{4,0},{8,12},{12,8},{16,20},{20,16},{24,28},{28,24},{1,5},{5... | collective-permute-start | bytes 294920 | tf_op jit(solution)/shard_map/ppermute | solution.py:716
  287.6 8.7 %collective-permute-start.40 = (bf16[2,2,2,2,24,1536]{5,4,2,1,3,0:T(8,128)(2,1)S(1)}, bf16[2,2,2,2,24,1536]{5,4,2,1,3,0:T(8,128)(2,1)S(1)}, u32[]{:S(2)}, u32[]{:S(2)}) collective-permute-start(bf16[2,2,2,2,24,1536]{5,4,2,1,3,0:T(8,128)(2,1)S(1)} %fusion.8), channel_id=1, source_target_pairs={{0,1},{1,0},{2,3},{3,2},{4,5},{5,4},{6,7},{7,6},{8,9},{9,8},{10,11... | collective-permute-start | bytes 3538952 | tf_op jit(solution)/shard_map/ppermute | solution.py:716
  291.6 4.7 %collective-permute-start.39 = (f32[2,16,768]{2,1,0:T(8,128)S(1)}, f32[2,16,768]{2,1,0:T(8,128)S(1)}, u32[]{:S(2)}, u32[]{:S(2)}) collective-permute-start(f32[2,16,768]{2,1,0:T(8,128)S(1)} %add_select_fusion.5), channel_id=1, source_target_pairs={{0,8},{4,12},{8,0},{12,4},{16,24},{20,28},{24,16},{28,20},{1,9},{5... | collective-permute-start | bytes 294920 | tf_op jit(solution)/shard_map/ppermute | solution.py:716
  293.4 18.2 %collective-permute-start.42 = (bf16[2,2,2,24,1664]{4,3,2,1,0:T(8,128)(2,1)S(1)}, bf16[2,2,2,24,1664]{4,3,2,1,0:T(8,128)(2,1)}, u32[]{:S(2)}, u32[]{:S(2)}) collective-permute-start(bf16[2,2,2,24,1664]{4,3,2,1,0:T(8,128)(2,1)S(1)} %fusion.15), channel_id=1, source_target_pairs={{0,2},{1,3},{2,0},{3,1},{4,6},{5,7},{6,4},{7,5},{8,10},{9,11},{10,... | collective-permute-start | bytes 1916936 | tf_op jit(solution)/shard_map/ppermute | solution.py:716
  296.3 5.6 %collective-permute-start.41 = (f32[2,16,768]{2,1,0:T(8,128)S(1)}, f32[2,16,768]{2,1,0:T(8,128)S(1)}, u32[]{:S(2)}, u32[]{:S(2)}) collective-permute-start(f32[2,16,768]{2,1,0:T(8,128)S(1)} %add_select_fusion.4), channel_id=1, source_target_pairs={{0,16},{4,20},{8,24},{12,28},{16,0},{20,4},{24,8},{28,12},{1,17},{... | collective-permute-start | bytes 294920 | tf_op jit(solution)/shard_map/ppermute | solution.py:716
  300.4 28.2 %collective-permute-start.44 = (bf16[2,2,2,24,1536]{4,3,1,0,2:T(8,128)(2,1)}, bf16[2,2,2,24,1536]{4,3,1,0,2:T(8,128)(2,1)}, u32[]{:S(2)}, u32[]{:S(2)}) collective-permute-start(bf16[2,2,2,24,1536]{4,3,1,0,2:T(8,128)(2,1)} %fusion.23), channel_id=1, source_target_pairs={{0,2},{1,3},{2,0},{3,1},{4,6},{5,7},{6,4},{7,5},{8,10},{9,11},{10,... | collective-permute-start | bytes 1769480 | tf_op jit(solution)/shard_map/ppermute | solution.py:716
  314.0 14.5 %collective-permute-start.43 = (bf16[2,2,24,1664]{3,2,1,0:T(8,128)(2,1)S(1)}, bf16[2,2,24,1664]{3,2,1,0:T(8,128)(2,1)S(1)}, u32[]{:S(2)}, u32[]{:S(2)}) collective-permute-start(bf16[2,2,24,1664]{3,2,1,0:T(8,128)(2,1)S(1)} %fusion.26), channel_id=1, source_target_pairs={{0,4},{4,0},{8,12},{12,8},{16,20},{20,16},{24,28},{28,24},{1,5},{5... | collective-permute-start | bytes 958472 | tf_op jit(solution)/shard_map/ppermute | solution.py:716
  316.0 12.5 %collective-permute-start.45 = (bf16[1,192,768]{2,1,0:T(8,128)(2,1)S(1)}, bf16[1,192,768]{2,1,0:T(8,128)(2,1)S(1)}, u32[]{:S(2)}, u32[]{:S(2)}) collective-permute-start(bf16[1,192,768]{2,1,0:T(8,128)(2,1)S(1)} %fusion.31), channel_id=1, source_target_pairs={{0,16},{4,20},{8,24},{12,28},{16,0},{20,4},{24,8},{28,12},{1,17},{... | collective-permute-start | bytes 884744 | tf_op jit(solution)/shard_map/ppermute | solution.py:716
  329.6 14.2 %collective-permute-start.47 = (bf16[2,192,768]{2,1,0:T(8,128)(2,1)}, bf16[2,192,768]{2,1,0:T(8,128)(2,1)}, u32[]{:S(2)}, u32[]{:S(2)}) collective-permute-start(bf16[2,192,768]{2,1,0:T(8,128)(2,1)} %pad_maximum_fusion.8), channel_id=1, source_target_pairs={{0,8},{4,12},{8,0},{12,4},{16,24},{20,28},{24,16},{28,20},{1,9},{5... | collective-permute-start | bytes 1769480 | tf_op jit(solution)/shard_map/ppermute | solution.py:716
  331.6 11.4 %collective-permute-start.46 = (bf16[2,2,24,1536]{3,2,1,0:T(8,128)(2,1)}, bf16[2,2,24,1536]{3,2,1,0:T(8,128)(2,1)}, u32[]{:S(2)}, u32[]{:S(2)}) collective-permute-start(bf16[2,2,24,1536]{3,2,1,0:T(8,128)(2,1)} %fusion.30), channel_id=1, source_target_pairs={{0,4},{4,0},{8,12},{12,8},{16,20},{20,16},{24,28},{28,24},{1,5},{5... | collective-permute-start | bytes 884744 | tf_op jit(solution)/shard_map/ppermute | solution.py:716
  345.6 11.2 %collective-permute-start.48 = (bf16[2,24,3200]{2,1,0:T(8,128)(2,1)}, bf16[2,24,3200]{2,1,0:T(8,128)(2,1)}, u32[]{:S(2)}, u32[]{:S(2)}) collective-permute-start(bf16[2,24,3200]{2,1,0:T(8,128)(2,1)} %fusion.27), channel_id=1, source_target_pairs={{0,8},{4,12},{8,0},{12,4},{16,24},{20,28},{24,16},{28,20},{1,9},{5... | collective-permute-start | bytes 921608 | tf_op jit(solution)/shard_map/ppermute | solution.py:716
  357.9 12.3 %collective-permute-start.49 = (bf16[24,3200]{1,0:T(8,128)(2,1)S(1)}, bf16[24,3200]{1,0:T(8,128)(2,1)S(1)}, u32[]{:S(2)}, u32[]{:S(2)}) collective-permute-start(bf16[24,3200]{1,0:T(8,128)(2,1)S(1)} %fusion.32), channel_id=1, source_target_pairs={{0,16},{4,20},{8,24},{12,28},{16,0},{20,4},{24,8},{28,12},{1,17},{... | collective-permute-start | bytes 460808 | tf_op jit(solution)/shard_map/ppermute | solution.py:716
  361.4 26.5 %collective-permute-start.51 = (bf16[4,192,768]{2,1,0:T(8,128)(2,1)S(1)}, bf16[4,192,768]{2,1,0:T(8,128)(2,1)S(1)}, u32[]{:S(2)}, u32[]{:S(2)}) collective-permute-start(bf16[4,192,768]{2,1,0:T(8,128)(2,1)S(1)} %pad_maximum_fusion.5), channel_id=1, source_target_pairs={{0,4},{4,0},{8,12},{12,8},{16,20},{20,16},{24,28},{28,24},{1,5},{5... | collective-permute-start | bytes 3538952 | tf_op jit(solution)/shard_map/ppermute | solution.py:716
  370.3 9.1 %collective-permute-start.50 = (bf16[1,24,3200]{2,1,0:T(8,128)(2,1)S(1)}, bf16[1,24,3200]{2,1,0:T(8,128)(2,1)S(1)}, u32[]{:S(2)}, u32[]{:S(2)}) collective-permute-start(bf16[1,24,3200]{2,1,0:T(8,128)(2,1)S(1)} %fusion.33), channel_id=1, source_target_pairs={{0,16},{4,20},{8,24},{12,28},{16,0},{20,4},{24,8},{28,12},{1,17},{... | collective-permute-start | bytes 460808 | tf_op jit(solution)/shard_map/ppermute | solution.py:716
  388.9 11.4 %collective-permute-start.55 = (bf16[2,24,3200]{2,1,0:T(8,128)(2,1)S(1)}, bf16[2,24,3200]{2,1,0:T(8,128)(2,1)S(1)}, u32[]{:S(2)}, u32[]{:S(2)}) collective-permute-start(bf16[2,24,3200]{2,1,0:T(8,128)(2,1)S(1)} %pad_maximum_fusion.9), channel_id=1, source_target_pairs={{0,8},{4,12},{8,0},{12,4},{16,24},{20,28},{24,16},{28,20},{1,9},{5... | collective-permute-start | bytes 921608 | tf_op jit(solution)/shard_map/ppermute | solution.py:716
  391.5 5.5 %collective-permute-start.52 = (f32[136,192]{1,0:T(8,128)S(1)}, f32[136,192]{1,0:T(8,128)S(1)}, u32[]{:S(2)}, u32[]{:S(2)}) collective-permute-start(f32[136,192]{1,0:T(8,128)S(1)} %bitcast.267), channel_id=1, source_target_pairs={{0,1},{1,0},{2,3},{3,2},{4,5},{5,4},{6,7},{7,6},{8,9},{9,8},{10,11... | collective-permute-start | bytes 313352 | tf_op jit(solution)/shard_map/ppermute | solution.py:716
  391.6 6.5 %collective-permute-start.53 = (f32[136,192]{1,0:T(8,128)S(1)}, f32[136,192]{1,0:T(8,128)S(1)}, u32[]{:S(2)}, u32[]{:S(2)}) collective-permute-start(f32[136,192]{1,0:T(8,128)S(1)} %bitcast.268), channel_id=1, source_target_pairs={{0,2},{1,3},{2,0},{3,1},{4,6},{5,7},{6,4},{7,5},{8,10},{9,11},{10,... | collective-permute-start | bytes 313352 | tf_op jit(solution)/shard_map/ppermute | solution.py:716
  392.6 7.8 %collective-permute-start.54 = (f32[136,192]{1,0:T(8,128)S(1)}, f32[136,192]{1,0:T(8,128)S(1)}, u32[]{:S(2)}, u32[]{:S(2)}) collective-permute-start(f32[136,192]{1,0:T(8,128)S(1)} %bitcast.269), channel_id=1, source_target_pairs={{0,3},{1,2},{2,1},{3,0},{4,7},{5,6},{6,5},{7,4},{8,11},{9,10},{10,... | collective-permute-start | bytes 313352 | tf_op jit(solution)/shard_map/ppermute | solution.py:716
  400.5 20.1 %collective-permute-start.59 = (bf16[4,24,3200]{2,1,0:T(8,128)(2,1)S(1)}, bf16[4,24,3200]{2,1,0:T(8,128)(2,1)S(1)}, u32[]{:S(2)}, u32[]{:S(2)}) collective-permute-start(bf16[4,24,3200]{2,1,0:T(8,128)(2,1)S(1)} %pad_maximum_fusion.7), channel_id=1, source_target_pairs={{0,4},{4,0},{8,12},{12,8},{16,20},{20,16},{24,28},{28,24},{1,5},{5... | collective-permute-start | bytes 1843208 | tf_op jit(solution)/shard_map/ppermute | solution.py:716
  400.9 9.5 %collective-permute-start.56 = (f32[136,192]{1,0:T(8,128)S(1)}, f32[136,192]{1,0:T(8,128)S(1)}, u32[]{:S(2)}, u32[]{:S(2)}) collective-permute-start(f32[136,192]{1,0:T(8,128)S(1)} %fusion.39), channel_id=1, source_target_pairs={{0,16},{4,20},{8,24},{12,28},{16,0},{20,4},{24,8},{28,12},{1,17},{... | collective-permute-start | bytes 313352 | tf_op jit(solution)/shard_map/ppermute | solution.py:716
  410.4 5.1 %collective-permute-start.57 = (f32[136,192]{1,0:T(8,128)S(1)}, f32[136,192]{1,0:T(8,128)S(1)}, u32[]{:S(2)}, u32[]{:S(2)}) collective-permute-start(f32[136,192]{1,0:T(8,128)S(1)} %add.295), channel_id=1, source_target_pairs={{0,8},{4,12},{8,0},{12,4},{16,24},{20,28},{24,16},{28,20},{1,9},{5... | collective-permute-start | bytes 313352 | tf_op jit(solution)/shard_map/ppermute | solution.py:716
  415.5 5.1 %collective-permute-start.58 = (f32[136,192]{1,0:T(8,128)S(1)}, f32[136,192]{1,0:T(8,128)S(1)}, u32[]{:S(2)}, u32[]{:S(2)}) collective-permute-start(f32[136,192]{1,0:T(8,128)S(1)} %add.296), channel_id=1, source_target_pairs={{0,4},{4,0},{8,12},{12,8},{16,20},{20,16},{24,28},{28,24},{1,5},{5... | collective-permute-start | bytes 313352 | tf_op jit(solution)/shard_map/ppermute | solution.py:716
  (42 other events, 204.4 us)
